TPU v7x, 32 devices: a whole 2x2x4 slice. The times are simulated.
32 devices in a mesh: dp: 8 (over z, x), tensor: 4 (over y, core).
Axes of the slice: x: 2, y: 2, z: 4, core: 2. Of those that a mesh axis runs over, the one named last changes fastest.
Arguments:
- stream: float32 [8192, 768], P(('dp', 'tensor')), may hold values from -6 to 6
- cotangent: float32 [8192, 768], P(('dp', 'tensor')), may hold values from -6 to 6
- segments: int32 [8, 1024], P('dp'), may hold values from 0 to 3, never falling along the last dimension, each value on 1 to 800 neighbouring positions
- expert_pick: int32 [2, 8192, 2], P(None, 'dp'), may hold values from 0 to 3, as said below
- slot_index: int32 [2, 8192, 2], P(None, 'dp'), may hold values from -1 to 639, as said below
- norm_gains: float32 [2, 2, 768], replicated, may hold values from 0.5 to 1.5
- attention: bfloat16 [2, 3, 768, 768], P(None, None, 'dp', 'tensor'), may hold values from -0.21875 to 0.21875
- projection: bfloat16 [2, 768, 768], P(None, 'tensor', 'dp'), may hold values from -0.875 to 0.875
- router: bfloat16 [2, 768, 4], replicated, may hold values from -0.14941406 to 0.14941406
- widening: bfloat16 [2, 2, 768, 2048], P(None, None, 'dp', 'tensor'), may hold values from -0.21875 to 0.21875
- narrowing: bfloat16 [2, 2048, 768], P(None, 'tensor', 'dp'), may hold values from -0.125 to 0.125
- expansion: bfloat16 [2, 4, 2, 768, 2048], P(None, None, None, 'dp', 'tensor'), may hold values from -0.21875 to 0.21875
- contraction: bfloat16 [2, 4, 2048, 768], P(None, None, 'tensor', 'dp'), may hold values from -0.125 to 0.125
Outputs:
- stream_out: float32 [8192, 768], P(('dp', 'tensor'))
- stream_grad: float32 [8192, 768], P(('dp', 'tensor'))
- gains_grad: float32 [2, 2, 768], replicated
- attention_grad: float32 [2, 3, 768, 768], P(None, None, 'dp', 'tensor')
- projection_grad: float32 [2, 768, 768], P(None, 'tensor', 'dp')
- router_grad: float32 [2, 768, 4], replicated
- widening_grad: float32 [2, 2, 768, 2048], P(None, None, 'dp', 'tensor')
- narrowing_grad: float32 [2, 2048, 768], P(None, 'tensor', 'dp')
- expansion_grad: float32 [2, 4, 2, 768, 2048], P(None, None, None, 'dp', 'tensor')
- contraction_grad: float32 [2, 4, 2048, 768], P(None, None, 'tensor', 'dp')
Inputs may be any that keep to these rules, and one draw needn't show every extreme that they name: `segments`: numbers never fall along a sequence; a document ends where its number changes. `expert_pick`: the two experts of a token are different. `slot_index`: within one sequence and one layer the pairs of one expert take distinct slots below 640, given in order of token and then of choice; a pair is dropped only when its expert's 640 slots are taken; in every sequence and layer some expert fills all 640 slots.
All inputs are finite; a program needn't handle non-finite values.
Results may differ from a plain program's by a relative error of at most 0.04.
Values may be sent and summed in bfloat16 or wider, within the bound.
A program may use at most 256 MiB of HBM per device.

v0:
```python
import math

import jax
import jax.numpy as jnp
from jax import lax
from jax.sharding import PartitionSpec as P

HEAD = 64
CAP = 640


def norm_rows(values, gain_row):
    factor = lax.rsqrt(jnp.mean(values * values, axis=-1, keepdims=True) + 1e-06)
    return (values * factor * gain_row, factor)


def norm_back(values, factor, gain_row, upstream):
    scaled = upstream * gain_row
    inward = factor * scaled - values * factor * factor * factor * jnp.mean(
        scaled * values, axis=-1, keepdims=True
    )
    gain_part = jnp.sum(upstream * values * factor, axis=0)
    return (inward, gain_part)


def angle_tables(length, head_size):
    halfway = head_size // 2
    inverse = jnp.exp(
        jnp.arange(halfway, dtype=jnp.float32) * (-2.0 * math.log(10000.0) / head_size)
    )
    phases = jnp.arange(length, dtype=jnp.float32)[:, None] * inverse[None, :]
    return (jnp.cos(phases), jnp.sin(phases))


def rotate_pairs(values, cosine_table, sine_table):
    halfway = values.shape[-1] // 2
    former = values[..., :halfway]
    latter = values[..., halfway:]
    cosine_part = cosine_table[:, None, :]
    sine_part = sine_table[:, None, :]
    return jnp.concatenate(
        [former * cosine_part - latter * sine_part, latter * cosine_part + former * sine_part],
        axis=-1,
    )


def rotate_back(grads, cosine_table, sine_table):
    halfway = grads.shape[-1] // 2
    former = grads[..., :halfway]
    latter = grads[..., halfway:]
    cosine_part = cosine_table[:, None, :]
    sine_part = sine_table[:, None, :]
    return jnp.concatenate(
        [former * cosine_part + latter * sine_part, latter * cosine_part - former * sine_part],
        axis=-1,
    )


def mask_block(offset, extent, segment):
    row_index = offset + jnp.arange(extent)
    column_index = jnp.arange(segment.shape[0])
    row_segment = segment[offset : offset + extent]
    return (column_index[None, :] <= row_index[:, None]) & (
        segment[None, :] == row_segment[:, None]
    )


def swiglu_back(upstream, inner_gate, inner_up):
    squashed = jax.nn.sigmoid(inner_gate)
    gate_grad = (upstream * inner_up * squashed * (1.0 + inner_gate * (1.0 - squashed))).astype(
        jnp.bfloat16
    )
    up_grad = (upstream * inner_gate * squashed).astype(jnp.bfloat16)
    return (gate_grad, up_grad)


def spread(piece):
    return lax.all_gather(piece, "tensor", axis=0, tiled=True)


def collect(partial_sum):
    return lax.psum_scatter(
        partial_sum.astype(jnp.bfloat16), "tensor", scatter_dimension=0, tiled=True
    ).astype(jnp.float32)


def spread_back(piece):
    return lax.all_gather(piece, "tensor", axis=0, tiled=True)


def collect_back(partial_sum):
    return lax.psum_scatter(
        partial_sum.astype(jnp.bfloat16), "tensor", scatter_dimension=0, tiled=True
    ).astype(jnp.float32)


def fetch(first, second, third, fourth, fifth, sixth):
    return (
        lax.all_gather(first, "dp", axis=1, tiled=True),
        lax.all_gather(second, "dp", axis=1, tiled=True),
        lax.all_gather(third, "dp", axis=1, tiled=True),
        lax.all_gather(fourth, "dp", axis=1, tiled=True),
        lax.all_gather(fifth, "dp", axis=2, tiled=True),
        lax.all_gather(sixth, "dp", axis=2, tiled=True),
    )


def refetch(first, second, third, fourth, fifth, sixth):
    return (
        lax.all_gather(first, "dp", axis=1, tiled=True),
        lax.all_gather(second, "dp", axis=1, tiled=True),
        lax.all_gather(third, "dp", axis=1, tiled=True),
        lax.all_gather(fourth, "dp", axis=1, tiled=True),
        lax.all_gather(fifth, "dp", axis=2, tiled=True),
        lax.all_gather(sixth, "dp", axis=2, tiled=True),
    )


def flatten_about(member, split_at):
    shape_all = member.shape
    leading = math.prod(shape_all[:split_at])
    trailing = math.prod(shape_all[split_at + 1 :])
    return member.reshape(1, leading, shape_all[split_at], trailing)


def restore_sum(received, shape_all, split_at):
    total = jnp.sum(received, axis=0)
    count = received.shape[0]
    return total.reshape(
        shape_all[:split_at] + (shape_all[split_at] // count,) + shape_all[split_at + 1 :]
    )


def sum_layer(members, splits):
    flats = [flatten_about(member, split_at) for member, split_at in zip(members, splits)]
    received = (
        lax.all_to_all(
            flats[0].astype(jnp.bfloat16), "dp", split_axis=2, concat_axis=0, tiled=True
        ).astype(jnp.float32),
        lax.all_to_all(
            flats[1].astype(jnp.bfloat16), "dp", split_axis=2, concat_axis=0, tiled=True
        ).astype(jnp.float32),
        lax.all_to_all(
            flats[2].astype(jnp.bfloat16), "dp", split_axis=2, concat_axis=0, tiled=True
        ).astype(jnp.float32),
        lax.all_to_all(
            flats[3].astype(jnp.bfloat16), "dp", split_axis=2, concat_axis=0, tiled=True
        ).astype(jnp.float32),
        lax.all_to_all(
            flats[4].astype(jnp.bfloat16), "dp", split_axis=2, concat_axis=0, tiled=True
        ).astype(jnp.float32),
        lax.all_to_all(
            flats[5].astype(jnp.bfloat16), "dp", split_axis=2, concat_axis=0, tiled=True
        ).astype(jnp.float32),
    )
    return tuple(
        (
            restore_sum(piece, member.shape, split_at)
            for piece, member, split_at in zip(received, members, splits)
        )
    )


def on_device(
    stream,
    cotangent,
    segments,
    expert_pick,
    slot_index,
    norm_gains,
    attention,
    projection,
    router,
    widening,
    narrowing,
    expansion,
    contraction,
):
    layers = attention.shape[0]
    segment = segments[0]
    length = segment.shape[0]
    experts = expansion.shape[1]
    capacity = CAP
    model_width = stream.shape[1]
    local_heads = attention.shape[3] // HEAD
    cosine_table, sine_table = angle_tables(length, HEAD)
    block_rows = min(512, length)
    positions = jnp.arange(length, dtype=jnp.int32)
    inverse_scale = 1.0 / math.sqrt(HEAD)
    saved = []
    kept_weights = []
    current = stream
    for layer_index in range(layers):
        weights = fetch(
            attention[layer_index],
            projection[layer_index],
            widening[layer_index],
            narrowing[layer_index],
            expansion[layer_index],
            contraction[layer_index],
        )
        kept_weights.append(None)
        (
            attention_full,
            projection_full,
            widening_full,
            narrowing_full,
            expansion_full,
            contraction_full,
        ) = weights
        normed_own, factor_one = norm_rows(current, norm_gains[layer_index, 0])
        normed = spread(normed_own.astype(jnp.bfloat16))
        projected = jnp.einsum(
            "td,cdf->ctf", normed, attention_full, preferred_element_type=jnp.float32
        )
        rotated_queries = rotate_pairs(
            projected[0].reshape(length, local_heads, HEAD), cosine_table, sine_table
        ).astype(jnp.bfloat16)
        rotated_keys = rotate_pairs(
            projected[1].reshape(length, local_heads, HEAD), cosine_table, sine_table
        ).astype(jnp.bfloat16)
        values = projected[2].astype(jnp.bfloat16).reshape(length, local_heads, HEAD)
        block_outs = []
        block_sums = []
        for offset in range(0, length, block_rows):
            scores = (
                jnp.einsum(
                    "qhd,khd->hqk",
                    rotated_queries[offset : offset + block_rows],
                    rotated_keys,
                    preferred_element_type=jnp.float32,
                )
                * inverse_scale
            )
            allowed = mask_block(offset, block_rows, segment)
            masked = jnp.where(allowed[None], scores, -1e30)
            highest = jnp.max(masked, axis=-1, keepdims=True)
            exponent = jnp.exp(masked - highest)
            normaliser = jnp.sum(exponent, axis=-1, keepdims=True)
            probability = (exponent / normaliser).astype(jnp.bfloat16)
            block_outs.append(
                jnp.einsum("hqk,khd->qhd", probability, values, preferred_element_type=jnp.float32)
            )
            block_sums.append(highest[..., 0] + jnp.log(normaliser[..., 0]))
        attended = (
            jnp.concatenate(block_outs, axis=0)
            .reshape(length, local_heads * HEAD)
            .astype(jnp.bfloat16)
        )
        log_sums = jnp.concatenate(block_sums, axis=1)
        mid = current + collect(
            jnp.dot(attended, projection_full, preferred_element_type=jnp.float32)
        )
        moe_own, factor_two = norm_rows(mid, norm_gains[layer_index, 1])
        moe_in = spread(moe_own.astype(jnp.bfloat16))
        logits = jnp.dot(moe_in, router[layer_index], preferred_element_type=jnp.float32)
        expert_of = expert_pick[layer_index]
        slot_of = slot_index[layer_index]
        chosen = (expert_of[..., None] == jnp.arange(experts, dtype=jnp.int32)).astype(jnp.float32)
        gate_values = jax.nn.softmax(jnp.sum(chosen * logits[:, None, :], axis=-1), axis=-1)
        flat_slot = jnp.where(slot_of >= 0, expert_of * capacity + slot_of, experts * capacity)
        token_table = jnp.broadcast_to(positions[:, None], flat_slot.shape)
        slot_token = (
            jnp.full((experts * capacity,), length, jnp.int32)
            .at[flat_slot.reshape(-1)]
            .set(token_table.reshape(-1), mode="drop")
        )
        slot_gate = (
            jnp.zeros((experts * capacity,), jnp.float32)
            .at[flat_slot.reshape(-1)]
            .set(gate_values.reshape(-1), mode="drop")
        )
        padded_in = jnp.concatenate([moe_in, jnp.zeros((1, model_width), jnp.bfloat16)], axis=0)
        routed = padded_in[slot_token].reshape(experts, capacity, model_width)
        inner_act = jnp.einsum(
            "ecd,ekdf->ekcf", routed, expansion_full, preferred_element_type=jnp.float32
        )
        hidden = (jax.nn.silu(inner_act[:, 0]) * inner_act[:, 1]).astype(jnp.bfloat16)
        expert_out = jnp.einsum(
            "ecf,efd->ecd", hidden, contraction_full, preferred_element_type=jnp.float32
        ).reshape(experts * capacity, model_width)
        padded_out = jnp.concatenate([expert_out, jnp.zeros((1, model_width), jnp.float32)], axis=0)
        shared_act = jnp.einsum(
            "td,kdf->ktf", moe_in, widening_full, preferred_element_type=jnp.float32
        )
        shared_hidden = (jax.nn.silu(shared_act[0]) * shared_act[1]).astype(jnp.bfloat16)
        branch = jnp.dot(
            shared_hidden, narrowing_full, preferred_element_type=jnp.float32
        ) + jnp.sum(gate_values[..., None] * padded_out[flat_slot], axis=1)
        following = mid + collect(branch)
        saved.append(
            (
                current,
                factor_one,
                normed,
                rotated_queries,
                rotated_keys,
                values,
                log_sums,
                attended,
                mid,
                factor_two,
                moe_in,
                chosen,
                gate_values,
                flat_slot,
                slot_token,
                slot_gate,
                routed,
                inner_act,
                hidden,
                padded_out,
                shared_act,
                shared_hidden,
            )
        )
        current = following
    grad_rows = cotangent
    gain_parts = [None] * layers
    router_parts = [None] * layers
    layer_results = [None] * layers
    splits = (1, 1, 1, 1, 2, 2)
    for layer_index in reversed(range(layers)):
        (
            layer_input,
            factor_one,
            normed,
            rotated_queries,
            rotated_keys,
            values,
            log_sums,
            attended,
            mid,
            factor_two,
            moe_in,
            chosen,
            gate_values,
            flat_slot,
            slot_token,
            slot_gate,
            routed,
            inner_act,
            hidden,
            padded_out,
            shared_act,
            shared_hidden,
        ) = saved[layer_index]
        weights = refetch(
            attention[layer_index],
            projection[layer_index],
            widening[layer_index],
            narrowing[layer_index],
            expansion[layer_index],
            contraction[layer_index],
        )
        (
            attention_full,
            projection_full,
            widening_full,
            narrowing_full,
            expansion_full,
            contraction_full,
        ) = weights
        branch_grad = spread_back(grad_rows.astype(jnp.bfloat16))
        shared_down = jnp.dot(branch_grad, narrowing_full.T, preferred_element_type=jnp.float32)
        shared_gate_grad, shared_up_grad = swiglu_back(shared_down, shared_act[0], shared_act[1])
        shared_grad = jnp.stack([shared_gate_grad, shared_up_grad], axis=0)
        narrowing_part = jnp.dot(shared_hidden.T, branch_grad, preferred_element_type=jnp.float32)
        widening_part = jnp.einsum(
            "td,ktf->kdf", moe_in, shared_grad, preferred_element_type=jnp.float32
        )
        moe_grad = jnp.einsum(
            "ktf,kdf->td", shared_grad, widening_full, preferred_element_type=jnp.float32
        )
        padded_grad = jnp.concatenate(
            [branch_grad, jnp.zeros((1, model_width), jnp.bfloat16)], axis=0
        )
        slot_grad = (
            (padded_grad[slot_token].astype(jnp.float32) * slot_gate[:, None])
            .astype(jnp.bfloat16)
            .reshape(experts, capacity, model_width)
        )
        expert_down = jnp.einsum(
            "ecd,efd->ecf", slot_grad, contraction_full, preferred_element_type=jnp.float32
        )
        expert_gate_grad, expert_up_grad = swiglu_back(
            expert_down, inner_act[:, 0], inner_act[:, 1]
        )
        expert_grad = jnp.stack([expert_gate_grad, expert_up_grad], axis=1)
        contraction_part = jnp.einsum(
            "ecf,ecd->efd", hidden, slot_grad, preferred_element_type=jnp.float32
        )
        expansion_part = jnp.einsum(
            "ecd,ekcf->ekdf", routed, expert_grad, preferred_element_type=jnp.float32
        )
        routed_grad = jnp.einsum(
            "ekcf,ekdf->ecd", expert_grad, expansion_full, preferred_element_type=jnp.float32
        ).reshape(experts * capacity, model_width)
        padded_routed = jnp.concatenate(
            [routed_grad, jnp.zeros((1, model_width), jnp.float32)], axis=0
        )
        moe_grad = moe_grad + jnp.sum(padded_routed[flat_slot], axis=1)
        gate_grad = jnp.sum(
            branch_grad.astype(jnp.float32)[:, None, :] * padded_out[flat_slot], axis=-1
        )
        logit_pair = gate_values[:, 0] * gate_values[:, 1] * (gate_grad[:, 0] - gate_grad[:, 1])
        signed_pair = jnp.stack([logit_pair, -logit_pair], axis=-1)
        logit_grad = jnp.sum(signed_pair[..., None] * chosen, axis=1)
        router_parts[layer_index] = jnp.dot(
            moe_in.astype(jnp.float32).T, logit_grad, precision=lax.Precision.HIGHEST
        )
        moe_grad = moe_grad + jnp.dot(
            logit_grad, router[layer_index].astype(jnp.float32).T, precision=lax.Precision.HIGHEST
        )
        moe_own_grad = collect_back(moe_grad)
        inward_two, gain_two = norm_back(mid, factor_two, norm_gains[layer_index, 1], moe_own_grad)
        mid_grad = grad_rows + inward_two
        residual_grad = spread_back(mid_grad.astype(jnp.bfloat16))
        projection_part = jnp.dot(attended.T, residual_grad, preferred_element_type=jnp.float32)
        attended_grad = (
            jnp.dot(residual_grad, projection_full.T, preferred_element_type=jnp.float32)
            .astype(jnp.bfloat16)
            .reshape(length, local_heads, HEAD)
        )
        query_parts = []
        keys_grad = jnp.zeros((length, local_heads, HEAD), jnp.float32)
        values_grad = jnp.zeros((length, local_heads, HEAD), jnp.float32)
        for offset in range(0, length, block_rows):
            query_block = rotated_queries[offset : offset + block_rows]
            upstream_block = attended_grad[offset : offset + block_rows]
            scores = (
                jnp.einsum(
                    "qhd,khd->hqk", query_block, rotated_keys, preferred_element_type=jnp.float32
                )
                * inverse_scale
            )
            allowed = mask_block(offset, block_rows, segment)
            probability = jnp.where(
                allowed[None],
                jnp.exp(scores - log_sums[:, offset : offset + block_rows, None]),
                0.0,
            )
            prob_grad = jnp.einsum(
                "qhd,khd->hqk", upstream_block, values, preferred_element_type=jnp.float32
            )
            inner_sum = jnp.sum(probability * prob_grad, axis=-1, keepdims=True)
            score_grad = (probability * (prob_grad - inner_sum)).astype(jnp.bfloat16)
            query_parts.append(
                jnp.einsum(
                    "hqk,khd->qhd", score_grad, rotated_keys, preferred_element_type=jnp.float32
                )
                * inverse_scale
            )
            keys_grad = (
                keys_grad
                + jnp.einsum(
                    "hqk,qhd->khd", score_grad, query_block, preferred_element_type=jnp.float32
                )
                * inverse_scale
            )
            values_grad = values_grad + jnp.einsum(
                "hqk,qhd->khd",
                probability.astype(jnp.bfloat16),
                upstream_block,
                preferred_element_type=jnp.float32,
            )
        queries_grad = rotate_back(
            jnp.concatenate(query_parts, axis=0), cosine_table, sine_table
        ).astype(jnp.bfloat16)
        keys_back = rotate_back(keys_grad, cosine_table, sine_table).astype(jnp.bfloat16)
        projected_grad = jnp.stack(
            [
                queries_grad.reshape(length, -1),
                keys_back.reshape(length, -1),
                values_grad.astype(jnp.bfloat16).reshape(length, -1),
            ],
            axis=0,
        )
        attention_part = jnp.einsum(
            "td,ctf->cdf", normed, projected_grad, preferred_element_type=jnp.float32
        )
        normed_grad = jnp.einsum(
            "ctf,cdf->td", projected_grad, attention_full, preferred_element_type=jnp.float32
        )
        normed_own_grad = collect_back(normed_grad)
        inward_one, gain_one = norm_back(
            layer_input, factor_one, norm_gains[layer_index, 0], normed_own_grad
        )
        grad_rows = mid_grad + inward_one
        gain_parts[layer_index] = jnp.stack([gain_one, gain_two], axis=0)
        members = (
            attention_part,
            projection_part,
            widening_part,
            narrowing_part,
            expansion_part,
            contraction_part,
        )
        layer_results[layer_index] = sum_layer(members, splits)
    stacked = [
        jnp.stack([layer_results[index_layer][member] for index_layer in range(layers)], axis=0)
        for member in range(6)
    ]
    gains_grad, router_grad = lax.psum(
        (jnp.stack(gain_parts, axis=0), jnp.stack(router_parts, axis=0)), ("dp", "tensor")
    )
    return (
        current,
        grad_rows,
        gains_grad,
        stacked[0],
        stacked[1],
        router_grad,
        stacked[2],
        stacked[3],
        stacked[4],
        stacked[5],
    )


def solution(mesh):
    placed = (
        P(("dp", "tensor"), None),
        P(("dp", "tensor"), None),
        P("dp", None),
        P(None, "dp", None),
        P(None, "dp", None),
        P(),
        P(None, None, "dp", "tensor"),
        P(None, "tensor", "dp"),
        P(),
        P(None, None, "dp", "tensor"),
        P(None, "tensor", "dp"),
        P(None, None, None, "dp", "tensor"),
        P(None, None, "tensor", "dp"),
    )
    return jax.shard_map(
        on_device,
        mesh=mesh,
        in_specs=placed,
        out_specs=(
            P(("dp", "tensor"), None),
            P(("dp", "tensor"), None),
            P(),
            P(None, None, "dp", "tensor"),
            P(None, "tensor", "dp"),
            P(),
            P(None, None, "dp", "tensor"),
            P(None, "tensor", "dp"),
            P(None, None, None, "dp", "tensor"),
            P(None, None, "tensor", "dp"),
        ),
        check_vma=False,
    )
```

profile of v0, /device:TPU:0, one launch (start us, length us, event | category | flops | bytes accessed | tf_op | source)
XLA Modules:
  0.0 1743.0 jit_solution(4782600358945931730)
XLA Ops:
  14.1 38.8 %all-gather = bf16[1,3,768,192]{3,1,0,2:T(4,128)(2,1)S(1)} all-gather(bf16[1,3,96,192]{3,1,0,2:T(4,128)(2,1)S(1)} %copy.387), channel_id=2, replica_groups=mesh['dp'=8,'tensor'=4] {'dp'}, dimensions={2}, use_global_device_ids=true | all-gather | bytes 995328 | tf_op jit(solution)/shard_map/all_gather | solution.py:99
  54.6 32.1 %all-gather.1 = bf16[1,192,768]{1,0,2:T(2,128)(2,1)S(1)} all-gather(bf16[1,192,96]{1,0,2:T(2,128)(2,1)S(1)} %copy.388), channel_id=3, replica_groups=mesh['dp'=8,'tensor'=4] {'dp'}, dimensions={2}, use_global_device_ids=true | all-gather | bytes 331776 | tf_op jit(solution)/shard_map/all_gather | solution.py:100
  110.0 24.4 %reduce-scatter.9.cloned.1.call-done = bf16[256,768]{1,0:T(8,128)(2,1)} async-done(((bf16[1024,768]{1,0:T(8,128)(2,1)}), bf16[256,768]{1,0:T(8,128)(2,1)}) %reduce-scatter.9.cloned.1.call-update) | async-done | bytes 393232 | tf_op jit(solution)/shard_map/reduce_scatter | solution.py:82
  142.2 8.1 scatter_custom_fusion
  150.4 35.5 %all-gather.3 = bf16[1,512,768]{1,2,0:T(8,128)(2,1)} all-gather(bf16[1,512,96]{1,2,0:T(8,128)(2,1)S(1)} %get-tuple-element.154), channel_id=5, replica_groups=mesh['dp'=8,'tensor'=4] {'dp'}, dimensions={2}, use_global_device_ids=true | all-gather | bytes 884736 | tf_op jit(solution)/shard_map/all_gather | solution.py:102
  203.0 8.6 gather_fusion
  211.6 34.5 %all-gather.43.cloned.1.call-done = bf16[1,2,768,512]{3,2,1,0:T(8,128)(2,1)} async-done(((bf16[1,2,96,512]{3,2,1,0:T(8,128)(2,1)}), bf16[1,2,768,512]{3,2,1,0:T(8,128)(2,1)}) %all-gather.43.cloned.1.call-update) | async-done | bytes 1572880 | tf_op jit(solution)/shard_map/all_gather | solution.py:101
  252.5 93.7 %all-gather.45.cloned.1.call-done = bf16[1,4,2,768,512]{4,3,2,1,0:T(8,128)(2,1)} async-done(((bf16[1,4,2,96,512]{4,3,2,1,0:T(8,128)(2,1)}), bf16[1,4,2,768,512]{4,3,2,1,0:T(8,128)(2,1)}) %all-gather.45.cloned.1.call-update) | async-done | bytes 6291472 | tf_op jit(solution)/shard_map/all_gather | solution.py:103
  346.2 7.8 convolution_bitcast_fusion
  365.7 13.9 gather_fusion.1
  379.6 8.2 reshape.878
  387.8 31.1 %multiply_reduce_fusion.7 = f32[1024,768]{1,0:T(8,128)S(1)} fusion(f32[1024,2,768]{2,1,0:T(2,128)} %reshape.878, f32[1024,2]{1,0:T(8,128)S(1)} %copy.318), kind=kLoop, calls=%fused_computation.41 | loop fusion | flops 2359296 | bytes 9445376 | tf_op jit(solution)/shard_map/reduce_sum | solution.py:289
  421.2 26.5 %reduce-scatter.11.cloned.1.call-done = bf16[256,768]{1,0:T(8,128)(2,1)} async-done(((bf16[1024,768]{1,0:T(8,128)(2,1)}), bf16[256,768]{1,0:T(8,128)(2,1)}) %reduce-scatter.11.cloned.1.call-update) | async-done | bytes 393232 | tf_op jit(solution)/shard_map/reduce_scatter | solution.py:82
  450.0 37.5 %all-gather.6 = bf16[1,3,768,192]{3,1,0,2:T(4,128)(2,1)S(1)} all-gather(bf16[1,3,96,192]{3,1,0,2:T(4,128)(2,1)S(1)} %copy.391), channel_id=8, replica_groups=mesh['dp'=8,'tensor'=4] {'dp'}, dimensions={2}, use_global_device_ids=true | all-gather | bytes 995328 | tf_op jit(solution)/shard_map/all_gather | solution.py:99
  490.4 32.1 %all-gather.7 = bf16[1,192,768]{1,0,2:T(2,128)(2,1)S(1)} all-gather(bf16[1,192,96]{1,0,2:T(2,128)(2,1)S(1)} %copy.392), channel_id=9, replica_groups=mesh['dp'=8,'tensor'=4] {'dp'}, dimensions={2}, use_global_device_ids=true | all-gather | bytes 331776 | tf_op jit(solution)/shard_map/all_gather | solution.py:100
  522.5 10.6 copy.327
  551.7 25.5 %reduce-scatter.13.cloned.1.call-done = bf16[256,768]{1,0:T(8,128)(2,1)} async-done(((bf16[1024,768]{1,0:T(8,128)(2,1)}), bf16[256,768]{1,0:T(8,128)(2,1)}) %reduce-scatter.13.cloned.1.call-update) | async-done | bytes 393232 | tf_op jit(solution)/shard_map/reduce_scatter | solution.py:82
  582.2 8.2 scatter_custom_fusion.1
  591.0 35.0 %all-gather.9 = bf16[1,512,768]{1,2,0:T(8,128)(2,1)} all-gather(bf16[1,512,96]{1,2,0:T(8,128)(2,1)S(1)} %get-tuple-element.153), channel_id=11, replica_groups=mesh['dp'=8,'tensor'=4] {'dp'}, dimensions={2}, use_global_device_ids=true | all-gather | bytes 884736 | tf_op jit(solution)/shard_map/all_gather | solution.py:102
  627.6 8.5 gather_fusion.4
  639.4 24.7 %all-gather.53.cloned.1.call-done = bf16[1,4,512,768]{2,1,0,3:T(4,128)(2,1)} async-done(((bf16[1,4,512,96]{2,1,0,3:T(4,128)(2,1)}), bf16[1,4,512,768]{2,1,0,3:T(4,128)(2,1)}) %all-gather.53.cloned.1.call-update) | async-done | bytes 3145744 | tf_op jit(solution)/shard_map/all_gather | solution.py:104
  670.2 14.5 all-gather.33.cloned.1.call-done
  687.2 8.1 scatter_custom_fusion.2
  696.9 9.0 gather_fusion.2
  705.9 80.8 %all-gather.51.cloned.1.call-done = bf16[1,4,2,768,512]{4,3,2,1,0:T(8,128)(2,1)} async-done(((bf16[1,4,2,96,512]{4,3,2,1,0:T(8,128)(2,1)}), bf16[1,4,2,768,512]{4,3,2,1,0:T(8,128)(2,1)}) %all-gather.51.cloned.1.call-update) | async-done | bytes 6291472 | tf_op jit(solution)/shard_map/all_gather | solution.py:103
  786.7 12.2 fusion.16
  799.0 8.6 fusion.65
  813.4 14.0 gather_fusion.3
  827.3 8.2 reshape.894
  835.5 17.4 multiply_reduce_fusion.5
  853.4 8.6 fusion.6
  865.7 13.9 gather_fusion.5
  879.6 8.2 reshape.914
  887.7 12.1 reduce_sum.410
  912.1 26.5 %reduce-scatter.17.cloned.1.call-done = bf16[256,768]{1,0:T(8,128)(2,1)} async-done(((bf16[1024,768]{1,0:T(8,128)(2,1)}), bf16[256,768]{1,0:T(8,128)(2,1)}) %reduce-scatter.17.cloned.1.call-update) | async-done | bytes 393232 | tf_op jit(solution)/shard_map/reduce_scatter | solution.py:92
  942.9 7.4 fusion.70
  950.3 15.8 copy.370
  966.7 20.4 %reduce.56 = bf16[768,2048]{1,0:T(8,128)(2,1)} reduce(bf16[768,1,1,2048]{3,2,1,0:T(2,128)(2,1)} %bitcast.486, bf16[]{:T(256)} %broadcast.621), dimensions={1,2}, to_apply=%bitcast.395.reduce_sub_computation | reduce | bytes 6291458
  1054.5 20.1 %all-to-all-done.5 = bf16[1,2,768,512]{3,1,0,2:T(2,128)(2,1)} async-done(((bf16[1,2,768,512]{3,1,0,2:T(2,128)(2,1)}), bf16[1,2,768,512]{3,1,0,2:T(2,128)(2,1)}, u32[]{:S(2)}, u32[]{:S(2)}) %all-to-all-start.5) | async-done | bytes 1572896 | tf_op jit(solution)/shard_map/all_to_all | solution.py:143
  1102.6 46.8 %all-to-all-done.11 = bf16[8,2,98304]{2,1,0:T(2,128)(2,1)} async-done(((bf16[8,2,98304]{2,1,0:T(2,128)(2,1)}), bf16[8,2,98304]{2,1,0:T(2,128)(2,1)}, u32[]{:S(2)}, u32[]{:S(2)}) %all-to-all-start.11) | async-done | bytes 3145760 | tf_op jit(solution)/shard_map/all_to_all | solution.py:152
  1167.0 9.9 fusion.22
  1176.9 9.1 copy.364
  1186.1 17.1 all-to-all-done.1
  1213.4 8.4 scatter_custom_fusion.3
  1221.8 11.3 all-gather.39.cloned.1.call-done
  1234.6 8.5 gather_fusion.6
  1243.4 17.6 %multiply_reduce_fusion.2 = f32[1024,2]{1,0:T(8,128)S(1)} fusion(f32[1024,2,768]{2,1,0:T(2,128)} %reshape.878, f32[1024,768]{1,0:T(8,128)S(1)} %convert_element_type.583), kind=kLoop, calls=%fused_computation.28 | loop fusion | flops 3143680 | bytes 9445376 | tf_op jit(solution)/shard_map/reduce_sum | solution.py:403
  1264.6 8.3 fusion.66
  1272.9 8.8 fusion.2
  1285.4 13.8 gather_fusion.7
  1299.2 8.4 reshape.930
  1307.6 10.3 reduce_sum.417
  1360.4 8.7 all-to-all-done.6
  1376.0 7.4 fusion.67
  1383.4 15.9 copy.367
  1399.2 20.5 %reduce.57 = bf16[768,2048]{1,0:T(8,128)(2,1)} reduce(bf16[768,1,1,2048]{3,2,1,0:T(2,128)(2,1)} %bitcast.487, bf16[]{:T(256)} %broadcast.621), dimensions={1,2}, to_apply=%bitcast.397.reduce_sub_computation | reduce | bytes 6291458
  1462.0 8.8 multiply_convert_fusion
  1482.5 22.9 %all-to-all-done.10 = bf16[8,2,98304]{2,1,0:T(2,128)(2,1)} async-done(((bf16[8,2,98304]{2,1,0:T(2,128)(2,1)}), bf16[8,2,98304]{2,1,0:T(2,128)(2,1)}, u32[]{:S(2)}, u32[]{:S(2)}) %all-to-all-start.10) | async-done | bytes 3145760 | tf_op jit(solution)/shard_map/all_to_all | solution.py:152
  1524.9 9.9 fusion.19
  1534.8 9.2 copy.361
  1544.0 17.7 %all-to-all-done = bf16[1,3,768,192]{3,1,0,2:T(4,128)(2,1)} async-done(((bf16[1,3,768,192]{3,1,0,2:T(4,128)(2,1)}), bf16[1,3,768,192]{3,1,0,2:T(4,128)(2,1)}, u32[]{:S(2)}, u32[]{:S(2)}) %all-to-all-start) | async-done | bytes 884768 | tf_op jit(solution)/shard_map/all_to_all | solution.py:137
  1584.7 7.9 reshape.1022
  1627.3 7.8 reshape.1024
  1653.7 70.7 %all-reduce.8 = (f32[2,2,768]{2,1,0:T(2,128)}, f32[2,768,4]{1,2,0:T(4,128)}) all-reduce(f32[2,2,768]{2,1,0:T(2,128)S(1)} %pad_maximum_fusion.37, f32[2,768,4]{1,2,0:T(4,128)S(1)} %pad_maximum_fusion.36), channel_id=1, replica_groups=mesh['dp'=8,'tensor'=4] {'dp','tensor'}, use_global_device_ids=true, to_apply=%region_50.51 | all-reduce | flops 9216 | bytes 73728 | tf_op jit(solution)/shard_map/psum | solution.py:504
  (667 shorter events, 487.6 us)
Async XLA Ops:
  8.0 45.8 %copy-start.112 = (bf16[2,192,96]{2,1,0:T(8,128)(2,1)S(1)}, bf16[2,192,96]{2,1,0:T(8,128)(2,1)}, u32[]{:S(2)}) copy-start(bf16[2,192,96]{2,1,0:T(8,128)(2,1)} %param.20) | copy-start | bytes 221188
  8.0 82.1 %all-gather.27.cloned.1.call-start = ((), (), s32[]{:S(2)}) async-start(), calls=%async_computation.20 | async-start | bytes 1966080 | tf_op jit(solution)/shard_map/all_gather | solution.py:78
  8.9 45.7 %copy-start.118 = (f32[768]{0:T(1024)}, f32[768]{0:T(1024)S(1)}, u32[]{:S(2)}) copy-start(f32[768]{0:T(1024)S(1)} %get-tuple-element.82) | copy-start | bytes 9220
  8.9 126.7 %copy-start.110 = (f32[768]{0:T(1024)}, f32[768]{0:T(1024)S(1)}, u32[]{:S(2)}) copy-start(f32[768]{0:T(1024)S(1)} %get-tuple-element.81) | copy-start | bytes 9220
  8.9 440.0 %copy-start.120 = (f32[768]{0:T(1024)}, f32[768]{0:T(1024)S(1)}, u32[]{:S(2)}) copy-start(f32[768]{0:T(1024)S(1)} %get-tuple-element.80) | copy-start | bytes 9220
  12.2 76.1 %copy-start.142 = (s32[1,1024]{1,0:T(1,128)S(1)}, s32[1,1024]{1,0:T(1,128)}, u32[]{:S(2)}) copy-start(s32[1,1024]{1,0:T(1,128)} %param.15) | copy-start | bytes 12292
  12.2 122.2 %reduce-scatter.9.cloned.1.call-start = ((), (), s32[]{:S(2)}) async-start(), calls=%async_computation.21 | async-start | bytes 1966080 | tf_op jit(solution)/shard_map/reduce_scatter | solution.py:82
  53.8 39.2 %copy-start.88 = (bf16[1,3,768,192]{2,3,1,0:T(8,128)(2,1)}, bf16[1,3,768,192]{2,3,1,0:T(8,128)(2,1)S(1)}, u32[]{:S(2)}) copy-start(bf16[1,3,768,192]{2,3,1,0:T(8,128)(2,1)S(1)} %copy.315) | copy-start | bytes 2654212
  88.9 447.4 %copy-start.50 = (f32[1024,32]{0,1:T(8,128)}, f32[1024,32]{0,1:T(8,128)S(1)}, u32[]{:S(2)}) copy-start(f32[1024,32]{0,1:T(8,128)S(1)} %get-tuple-element.165) | copy-start | bytes 393220
  88.9 447.4 %copy-start.53 = (f32[1024,32]{0,1:T(8,128)}, f32[1024,32]{0,1:T(8,128)S(1)}, u32[]{:S(2)}) copy-start(f32[1024,32]{0,1:T(8,128)S(1)} %get-tuple-element.166) | copy-start | bytes 393220
  104.2 30.2 %copy-start.2 = (f32[256,768]{1,0:T(8,128)S(1)}, f32[256,768]{1,0:T(8,128)}, u32[]{:S(2)}) copy-start(f32[256,768]{1,0:T(8,128)} %param.13) | copy-start | bytes 2359300
  106.8 31.1 %copy-start.96 = (bf16[2,2,96,512]{3,2,1,0:T(8,128)(2,1)S(1)}, bf16[2,2,96,512]{3,2,1,0:T(8,128)(2,1)}, u32[]{:S(2)}) copy-start(bf16[2,2,96,512]{3,2,1,0:T(8,128)(2,1)} %param.22) | copy-start | bytes 1179652
  106.8 32.0 %copy-start.76 = (bf16[2,4,2,96,512]{4,3,2,1,0:T(8,128)(2,1)S(1)}, bf16[2,4,2,96,512]{4,3,2,1,0:T(8,128)(2,1)}, u32[]{:S(2)}) copy-start(bf16[2,4,2,96,512]{4,3,2,1,0:T(8,128)(2,1)} %param.24) | copy-start | bytes 4718596
  106.8 79.1 %all-gather.47.cloned.1.call-start = ((), (), s32[]{:S(2)}) async-start(), calls=%async_computation.38 | async-start | bytes 3538944 | tf_op jit(solution)/shard_map/all_gather | solution.py:104
  110.0 30.2 %copy-start.117 = (s32[2,1024,2]{1,2,0:T(2,128)S(1)}, s32[2,1024,2]{1,2,0:T(2,128)}, u32[]{:S(2)}) copy-start(s32[2,1024,2]{1,2,0:T(2,128)} %param.16) | copy-start | bytes 49156
  110.0 89.0 %all-gather.29.cloned.1.call-start = ((), (), s32[]{:S(2)}) async-start(), calls=%async_computation.22 | async-start | bytes 1966080 | tf_op jit(solution)/shard_map/all_gather | solution.py:78
  137.6 108.6 %all-gather.43.cloned.1.call-start = ((), (), s32[]{:S(2)}) async-start(), calls=%async_computation.36 | async-start | bytes 1769472 | tf_op jit(solution)/shard_map/all_gather | solution.py:101
  138.7 207.5 %all-gather.45.cloned.1.call-start = ((), (), s32[]{:S(2)}) async-start(), calls=%async_computation.37 | async-start | bytes 7077888 | tf_op jit(solution)/shard_map/all_gather | solution.py:103
  140.1 307.5 %reduce-scatter.11.cloned.1.call-start = ((), (), s32[]{:S(2)}) async-start(), calls=%async_computation.23 | async-start | bytes 1966080 | tf_op jit(solution)/shard_map/reduce_scatter | solution.py:82
  142.1 56.9 %copy-start.122 = (bf16[2,768,4]{1,2,0:T(4,128)(2,1)S(1)}, bf16[2,768,4]{1,2,0:T(4,128)(2,1)}, u32[]{:S(2)}) copy-start(bf16[2,768,4]{1,2,0:T(4,128)(2,1)} %param.21) | copy-start | bytes 36868
  142.2 49.7 %copy-start.149 = (s32[2048,1]{0,1:T(1,128)}, s32[2048,1]{0,1:T(1,128)S(1)}, u32[]{:S(2)}) copy-start(s32[2048,1]{0,1:T(1,128)S(1)} %compare_select_fusion.1) | copy-start | bytes 24580
  150.3 52.7 %copy-start.108 = (s32[3072]{0:T(1024)}, s32[3072]{0:T(1024)S(1)}, u32[]{:S(2)}) copy-start(s32[3072]{0:T(1024)S(1)} %pad_clamp_fusion.1) | copy-start | bytes 36868
  150.3 215.4 %copy-start = (s32[2048]{0:T(1024)}, s32[2048]{0:T(1024)S(1)}, u32[]{:S(2)}) copy-start(s32[2048]{0:T(1024)S(1)} %broadcast_clamp_fusion.1) | copy-start | bytes 24580
  150.4 50.6 %copy-start.115 = (s32[1024,2]{0,1:T(2,128)}, s32[1024,2]{0,1:T(2,128)S(1)}, u32[]{:S(2)}) copy-start(s32[1024,2]{0,1:T(2,128)S(1)} %get-tuple-element.160) | copy-start | bytes 24580
  201.3 186.5 %copy-start.35 = (f32[1024,2]{1,0:T(8,128)}, f32[1024,2]{1,0:T(8,128)S(1)}, u32[]{:S(2)}) copy-start(f32[1024,2]{1,0:T(8,128)S(1)} %copy.318) | copy-start | bytes 24580
  252.5 166.3 %copy-start.37 = (bf16[1024,512]{1,0:T(8,128)(2,1)}, bf16[1024,512]{1,0:T(8,128)(2,1)S(1)}, u32[]{:S(2)}) copy-start(bf16[1024,512]{1,0:T(8,128)(2,1)S(1)} %multiply_convert_fusion.15) | copy-start | bytes 3145732
  387.8 31.1 %copy-start.56 = (bf16[1,512,768]{1,2,0:T(8,128)(2,1)S(1)}, bf16[1,512,768]{1,2,0:T(8,128)(2,1)}, u32[]{:S(2)}) copy-start(bf16[1,512,768]{1,2,0:T(8,128)(2,1)} %all-gather.3) | copy-start | bytes 2359300
  421.1 112.0 %all-gather.31.cloned.1.call-start = ((), (), s32[]{:S(2)}) async-start(), calls=%async_computation.24 | async-start | bytes 1966080 | tf_op jit(solution)/shard_map/all_gather | solution.py:78
  449.8 127.4 %reduce-scatter.13.cloned.1.call-start = ((), (), s32[]{:S(2)}) async-start(), calls=%async_computation.25 | async-start | bytes 1966080 | tf_op jit(solution)/shard_map/reduce_scatter | solution.py:82
  547.8 32.5 %copy-start.44 = (bf16[1024,3,64]{0,2,1:T(8,128)(2,1)}, bf16[1024,3,64]{0,2,1:T(8,128)(2,1)S(1)}, u32[]{:S(2)}) copy-start(bf16[1024,3,64]{0,2,1:T(8,128)(2,1)S(1)} %pad_maximum_fusion.23) | copy-start | bytes 1179652
  549.6 32.1 %copy-start.137 = (s32[1,1024,2]{1,2,0:T(2,128)S(1)}, s32[1,1024,2]{1,2,0:T(2,128)}, u32[]{:S(2)}) copy-start(s32[1,1024,2]{1,2,0:T(2,128)} %get-tuple-element.93) | copy-start | bytes 24580
  549.6 40.9 %copy-start.136 = (s32[1024,2,1]{0,1,2:T(2,128)S(1)}, s32[1024,2,1]{0,1,2:T(2,128)}, u32[]{:S(2)}) copy-start(s32[1024,2,1]{0,1,2:T(2,128)} %get-tuple-element.92) | copy-start | bytes 24580
  549.6 76.4 %all-gather.35.cloned.1.call-start = ((), (), s32[]{:S(2)}) async-start(), calls=%async_computation.28 | async-start | bytes 1966080 | tf_op jit(solution)/shard_map/all_gather | solution.py:88
  550.5 113.6 %all-gather.53.cloned.1.call-start = ((), (), s32[]{:S(2)}) async-start(), calls=%async_computation.41 | async-start | bytes 3538944 | tf_op jit(solution)/shard_map/all_gather | solution.py:104
  551.6 133.0 %all-gather.33.cloned.1.call-start = ((), (), s32[]{:S(2)}) async-start(), calls=%async_computation.26 | async-start | bytes 1966080 | tf_op jit(solution)/shard_map/all_gather | solution.py:78
  580.3 206.4 %all-gather.51.cloned.1.call-start = ((), (), s32[]{:S(2)}) async-start(), calls=%async_computation.40 | async-start | bytes 7077888 | tf_op jit(solution)/shard_map/all_gather | solution.py:103
  581.0 318.9 %all-gather.49.cloned.1.call-start = ((), (), s32[]{:S(2)}) async-start(), calls=%async_computation.39 | async-start | bytes 1769472 | tf_op jit(solution)/shard_map/all_gather | solution.py:101
  581.6 357.0 %reduce-scatter.17.cloned.1.call-start = ((), (), s32[]{:S(2)}) async-start(), calls=%async_computation.29 | async-start | bytes 1966080 | tf_op jit(solution)/shard_map/reduce_scatter | solution.py:92
  912.0 30.8 %copy-start.133 = (f32[3,512]{1,0:T(4,128)S(1)}, f32[3,512]{1,0:T(4,128)}, u32[]{:S(2)}) copy-start(f32[3,512]{1,0:T(4,128)} %copy-done.132) | copy-start | bytes 18436
  912.0 30.8 %copy-start.135 = (f32[3,512]{1,0:T(4,128)S(1)}, f32[3,512]{1,0:T(4,128)}, u32[]{:S(2)}) copy-start(f32[3,512]{1,0:T(4,128)} %copy-done.134) | copy-start | bytes 18436
  912.1 110.9 %all-gather.37.cloned.1.call-start = ((), (), s32[]{:S(2)}) async-start(), calls=%async_computation.30 | async-start | bytes 1966080 | tf_op jit(solution)/shard_map/all_gather | solution.py:88
  1007.6 25.9 %all-to-all-start.7 = ((bf16[8,2,24576]{2,1,0:T(2,128)(2,1)}), bf16[8,2,24576]{2,1,0:T(2,128)(2,1)}, u32[]{:S(2)}, u32[]{:S(2)}) async-start(bf16[8,2,24576]{2,1,0:T(2,128)(2,1)} %reshape.1017), calls=%async_computation.15 | async-start | bytes 1572864 | tf_op jit(solution)/shard_map/all_to_all | solution.py:146
  1033.6 41.0 %all-to-all-start.5 = ((bf16[1,2,768,512]{3,1,0,2:T(2,128)(2,1)}), bf16[1,2,768,512]{3,1,0,2:T(2,128)(2,1)}, u32[]{:S(2)}, u32[]{:S(2)}) async-start(bf16[1,2,768,512]{3,1,0,2:T(2,128)(2,1)} %copy.354), calls=%async_computation.13 | async-start | bytes 3145728 | tf_op jit(solution)/shard_map/all_to_all | solution.py:143
  1074.6 74.7 %all-to-all-start.11 = ((bf16[8,2,98304]{2,1,0:T(2,128)(2,1)}), bf16[8,2,98304]{2,1,0:T(2,128)(2,1)}, u32[]{:S(2)}, u32[]{:S(2)}) async-start(bf16[8,2,98304]{2,1,0:T(2,128)(2,1)} %reshape.1021), calls=%async_computation.19 | async-start | bytes 6291456 | tf_op jit(solution)/shard_map/all_to_all | solution.py:152
  1079.2 128.9 %reduce-scatter.19.cloned.1.call-start = ((), (), s32[]{:S(2)}) async-start(), calls=%async_computation.31 | async-start | bytes 1966080 | tf_op jit(solution)/shard_map/reduce_scatter | solution.py:92
  1091.4 118.6 %reduce-scatter.15.cloned.1.call-start = ((), (), s32[]{:S(2)}) async-start(), calls=%async_computation.27 | async-start | bytes 1966080 | tf_op jit(solution)/shard_map/reduce_scatter | solution.py:82
  1095.6 57.3 %copy-start.98 = (bf16[1024,3,64]{0,2,1:T(8,128)(2,1)S(1)}, bf16[1024,3,64]{0,2,1:T(8,128)(2,1)}, u32[]{:S(2)}) copy-start(bf16[1024,3,64]{0,2,1:T(8,128)(2,1)} %copy-done.97) | copy-start | bytes 1179652
  1095.6 57.3 %copy-start.100 = (bf16[1024,3,64]{0,2,1:T(8,128)(2,1)S(1)}, bf16[1024,3,64]{0,2,1:T(8,128)(2,1)}, u32[]{:S(2)}) copy-start(bf16[1024,3,64]{0,2,1:T(8,128)(2,1)} %copy-done.99) | copy-start | bytes 1179652
  1095.6 57.3 %copy-start.153 = (bf16[3,64,1024]{2,1,0:T(8,128)(2,1)S(1)}, bf16[3,64,1024]{2,1,0:T(8,128)(2,1)}, u32[]{:S(2)}) copy-start(bf16[3,64,1024]{2,1,0:T(8,128)(2,1)} %copy-done.152) | copy-start | bytes 1179652
  1149.3 13.4 all-to-all-start.3
  1162.7 40.5 %all-to-all-start.1 = ((bf16[1,3,768,192]{3,1,0,2:T(4,128)(2,1)}), bf16[1,3,768,192]{3,1,0,2:T(4,128)(2,1)}, u32[]{:S(2)}, u32[]{:S(2)}) async-start(bf16[1,3,768,192]{3,1,0,2:T(4,128)(2,1)} %copy.344), calls=%async_computation.9 | async-start | bytes 3145728 | tf_op jit(solution)/shard_map/all_to_all | solution.py:137
  1203.2 141.9 %all-to-all-start.9 = ((bf16[1,8,768,512]{3,1,0,2:T(8,128)(2,1)}), bf16[1,8,768,512]{3,1,0,2:T(8,128)(2,1)}, u32[]{:S(2)}, u32[]{:S(2)}) async-start(bf16[1,8,768,512]{3,1,0,2:T(8,128)(2,1)} %copy.364), calls=%async_computation.17 | async-start | bytes 12582912 | tf_op jit(solution)/shard_map/all_to_all | solution.py:149
  1208.0 25.1 %all-gather.39.cloned.1.call-start = ((), (), s32[]{:S(2)}) async-start(), calls=%async_computation.32 | async-start | bytes 1966080 | tf_op jit(solution)/shard_map/all_gather | solution.py:88
  1213.0 145.9 %reduce-scatter.21.cloned.1.call-start = ((), (), s32[]{:S(2)}) async-start(), calls=%async_computation.33 | async-start | bytes 1966080 | tf_op jit(solution)/shard_map/reduce_scatter | solution.py:92
  1345.1 24.1 %all-to-all-start.6 = ((bf16[8,2,24576]{2,1,0:T(2,128)(2,1)}), bf16[8,2,24576]{2,1,0:T(2,128)(2,1)}, u32[]{:S(2)}, u32[]{:S(2)}) async-start(bf16[8,2,24576]{2,1,0:T(2,128)(2,1)} %reshape.1019), calls=%async_computation.14 | async-start | bytes 1572864 | tf_op jit(solution)/shard_map/all_to_all | solution.py:146
  1369.1 60.5 %all-to-all-start.4 = ((bf16[1,2,768,512]{3,1,0,2:T(2,128)(2,1)}), bf16[1,2,768,512]{3,1,0,2:T(2,128)(2,1)}, u32[]{:S(2)}, u32[]{:S(2)}) async-start(bf16[1,2,768,512]{3,1,0,2:T(2,128)(2,1)} %copy.351), calls=%async_computation.12 | async-start | bytes 3145728 | tf_op jit(solution)/shard_map/all_to_all | solution.py:143
  1373.4 53.4 %all-gather.41.cloned.1.call-start = ((), (), s32[]{:S(2)}) async-start(), calls=%async_computation.34 | async-start | bytes 1966080 | tf_op jit(solution)/shard_map/all_gather | solution.py:88
  1429.6 75.8 %all-to-all-start.10 = ((bf16[8,2,98304]{2,1,0:T(2,128)(2,1)}), bf16[8,2,98304]{2,1,0:T(2,128)(2,1)}, u32[]{:S(2)}, u32[]{:S(2)}) async-start(bf16[8,2,98304]{2,1,0:T(2,128)(2,1)} %reshape.1023), calls=%async_computation.18 | async-start | bytes 6291456 | tf_op jit(solution)/shard_map/all_to_all | solution.py:152
  1505.4 13.5 all-to-all-start.2
  1518.9 42.7 %all-to-all-start = ((bf16[1,3,768,192]{3,1,0,2:T(4,128)(2,1)}), bf16[1,3,768,192]{3,1,0,2:T(4,128)(2,1)}, u32[]{:S(2)}, u32[]{:S(2)}) async-start(bf16[1,3,768,192]{3,1,0,2:T(4,128)(2,1)} %copy.342), calls=%async_computation.8 | async-start | bytes 3145728 | tf_op jit(solution)/shard_map/all_to_all | solution.py:137
  1561.7 165.2 %all-to-all-start.8 = ((bf16[1,8,768,512]{3,1,0,2:T(8,128)(2,1)}), bf16[1,8,768,512]{3,1,0,2:T(8,128)(2,1)}, u32[]{:S(2)}, u32[]{:S(2)}) async-start(bf16[1,8,768,512]{3,1,0,2:T(8,128)(2,1)} %copy.361), calls=%async_computation.16 | async-start | bytes 12582912 | tf_op jit(solution)/shard_map/all_to_all | solution.py:149
  1566.4 86.0 %reduce-scatter.23.cloned.1.call-start = ((), (), s32[]{:S(2)}) async-start(), calls=%async_computation.35 | async-start | bytes 1966080 | tf_op jit(solution)/shard_map/reduce_scatter | solution.py:92
  1646.9 77.6 %copy-start.31 = (f32[256,768]{1,0:T(8,128)S(1)}, f32[256,768]{1,0:T(8,128)}, u32[]{:S(2)}) copy-start(f32[256,768]{1,0:T(8,128)} %get-tuple-element.89) | copy-start | bytes 2359300
  1646.9 77.5 %copy-start.42 = (bf16[256,768]{1,0:T(8,128)(2,1)S(1)}, bf16[256,768]{1,0:T(8,128)(2,1)}, u32[]{:S(2)}) copy-start(bf16[256,768]{1,0:T(8,128)(2,1)} %reduce-scatter.21.cloned.1.call-done) | copy-start | bytes 1179652
  (137 other events, 1062.5 us)
Sparse Core Ops, SparseCore 0:
  12.4 22.3 all-gather.26
  106.9 27.4 reduce-scatter.8
  421.2 26.3 reduce-scatter.10
  449.9 19.6 all-gather.30
  549.7 27.3 reduce-scatter.12
  578.6 19.6 all-gather.34
  601.3 62.7 all-gather.52
  666.3 18.2 all-gather.32
  687.6 99.0 all-gather.50
  789.6 42.3 all-gather.48
  1376.5 20.0 all-gather.40
Sparse Core Ops, SparseCore 1:
  110.3 68.2 all-gather.46
  180.6 18.4 all-gather.28
  201.9 44.2 all-gather.42
  249.2 96.9 all-gather.44
  912.1 26.4 reduce-scatter.16
  942.9 19.5 all-gather.36
  1091.5 28.4 reduce-scatter.18
  1122.5 28.0 reduce-scatter.14
  1213.1 19.9 all-gather.38
  1327.9 28.1 reduce-scatter.20
  1580.9 28.5 reduce-scatter.22
where the time goes:
time: 1760 us; the launch traced here: 1740 us
  waiting for transfers between devices  514 us (29%)
  local copies, waits for them, and re-layouts  396 us (22%)
  blocking collectives  282 us (16%)
  other arithmetic  239 us (14%)
  matrix products  235 us (13%)
  starting transfers between devices  58.4 us (3%)
  between operations  19 us (1%)
    all_gather x2, waiting for transfers between devices, fetch(): lax.all_gather(fifth, 'dp', axis=2, tiled=True)  174 us
    reduce_scatter x4, waiting for transfers between devices, collect(): lax.psum_scatter(partial_sum.astype(jnp.bfloat16), 'tensor', scatter_dime...  76.3 us
    all_gather x2, blocking collectives, fetch(): lax.all_gather(first, 'dp', axis=1, tiled=True)  76.3 us
    psum x1, blocking collectives, on_device(): lax.psum((jnp.stack(gain_parts, axis=0), jnp.stack(router_parts, axis=0))...  70.7 us
    all_gather x2, blocking collectives, fetch(): lax.all_gather(fourth, 'dp', axis=1, tiled=True)  70.5 us
    all_to_all x2, waiting for transfers between devices, sum_layer(): lax.all_to_all(flats[5].astype(jnp.bfloat16), 'dp', split_axis=2, concat_...  69.7 us
    unnamed x361, local copies, waits for them, and re-layouts  69.2 us
    all_gather x2, blocking collectives, fetch(): lax.all_gather(second, 'dp', axis=1, tiled=True)  64.2 us
  transfers between devices with their start and end apart: 34, of which 20 were waited for; matrix products, arithmetic and copies ran while one was open for 42% of the time, Pallas kernels for 0%

commit v1 on v0

v1 whole, which is shorter than its diff:
```python
import math

import jax
import jax.numpy as jnp
from jax import lax
from jax.experimental import pallas as pl
from jax.experimental.pallas import tpu as pltpu
from jax.sharding import PartitionSpec as P

HEAD = 64
CAP = 640
LANES = 128
BF16 = jnp.bfloat16
F32 = jnp.float32
VMEM_LIMIT = 60 * 1024 * 1024


def nn(left, right):
    return lax.dot_general(left, right, (((1,), (0,)), ((), ())), preferred_element_type=F32)


def nt(left, right):
    return lax.dot_general(left, right, (((1,), (1,)), ((), ())), preferred_element_type=F32)


def tn(left, right):
    return lax.dot_general(left, right, (((0,), (0,)), ((), ())), preferred_element_type=F32)


class Place:
    def __init__(self):
        self.dp = lax.axis_index("dp")
        self.me = lax.axis_index("tensor")
        core = lax.rem(self.me, 2)
        self.core_peer = self.me + 1 - 2 * core
        self.y_peer = lax.rem(self.me + 2, 4)
        self.far_peer = lax.rem(self.core_peer + 2, 4)

    def tensor_id(self, member):
        return (self.dp, member)

    def greet(self):
        barrier = pltpu.get_barrier_semaphore()
        for member in (self.core_peer, self.y_peer):
            pl.semaphore_signal(
                barrier, inc=1, device_id=self.tensor_id(member), device_id_type=pl.DeviceIdType.MESH
            )
        pl.semaphore_wait(barrier, 2)


def send(source, target, send_sem, recv_sem, device):
    return pltpu.make_async_remote_copy(
        src_ref=source,
        dst_ref=target,
        send_sem=send_sem,
        recv_sem=recv_sem,
        device_id=device,
        device_id_type=pl.DeviceIdType.MESH,
    )


class TokenGather:
    def __init__(self, place, buf, send_sem, recv_sem):
        self.place, self.buf, self.sems = place, buf, (send_sem, recv_sem)
        self.quarter = buf.shape[0] // 4

    def rows(self, member):
        return pl.ds(pl.multiple_of(member * self.quarter, self.quarter), self.quarter)

    def pass_on(self, owner, target, slot):
        block = self.buf.at[self.rows(owner)]
        copy = send(
            block, block, self.sems[0].at[slot], self.sems[1].at[slot], self.place.tensor_id(target)
        )
        copy.start()
        return copy

    def start(self):
        place = self.place
        self.far = self.pass_on(place.me, place.y_peer, 1)
        self.near = self.pass_on(place.me, place.core_peer, 0)

    def arrivals(self):
        place = self.place
        yield place.me
        self.near.wait_recv()
        yield place.core_peer
        self.far.wait_recv()
        self.onward = self.pass_on(place.y_peer, place.core_peer, 2)
        yield place.y_peer
        self.onward.wait_recv()
        yield place.far_peer

    def close(self):
        self.near.wait_send()
        self.far.wait_send()
        self.onward.wait_send()


class TokenScatter:
    def __init__(self, place, part, landing, summed, crossed, send_sem, recv_sem):
        self.place, self.part = place, part
        self.landing, self.summed, self.crossed = landing, summed, crossed
        self.sems = (send_sem, recv_sem)
        self.quarter = part.shape[0] // 4

    def rows(self, member):
        return pl.ds(pl.multiple_of(member * self.quarter, self.quarter), self.quarter)

    def push(self, source, target, slot, member):
        copy = send(
            source, target, self.sems[0].at[slot], self.sems[1].at[slot], self.place.tensor_id(member)
        )
        copy.start()
        return copy

    def run(self, block_of):
        place, part = self.place, self.part
        part[self.rows(place.far_peer), :] = block_of(place.far_peer).astype(BF16)
        first = self.push(part.at[self.rows(place.far_peer)], self.landing.at[0], 0, place.core_peer)
        crossing = block_of(place.y_peer)
        first.wait_recv()
        self.summed[...] = (crossing + self.landing[0].astype(F32)).astype(BF16)
        across = self.push(self.summed, self.crossed, 1, place.y_peer)
        part[self.rows(place.core_peer), :] = block_of(place.core_peer).astype(BF16)
        second = self.push(part.at[self.rows(place.core_peer)], self.landing.at[1], 2, place.core_peer)
        own = block_of(place.me)
        second.wait_recv()
        own = own + self.landing[1].astype(F32)
        across.wait_recv()
        own = own + self.crossed[...].astype(F32)
        first.wait_send()
        second.wait_send()
        across.wait_send()
        return own


def scatter_scratch(length, width):
    quarter = length // 4
    return [
        pltpu.VMEM((length, width), BF16),
        pltpu.VMEM((2, quarter, width), BF16),
        pltpu.VMEM((quarter, width), BF16),
        pltpu.VMEM((quarter, width), BF16),
        pltpu.SemaphoreType.DMA((3,)),
        pltpu.SemaphoreType.DMA((3,)),
    ]


def gather_scratch(length, width):
    return [
        pltpu.VMEM((length, width), BF16),
        pltpu.SemaphoreType.DMA((3,)),
        pltpu.SemaphoreType.DMA((3,)),
    ]


class Local:
    def __init__(self, sems):
        self.sems, self.used, self.open = sems, 0, []

    def start(self, source, target, keep=False):
        copy = pltpu.make_async_copy(source, target, self.sems.at[self.used])
        self.used += 1
        copy.start()
        if keep:
            self.open.append(copy)
        return copy

    def close(self):
        for copy in self.open:
            copy.wait()


def normalise(values, gain):
    factor = lax.rsqrt(jnp.mean(values * values, axis=-1, keepdims=True) + 1e-06)
    return values * factor * gain


def normalise_back(values, gain, upstream):
    factor = lax.rsqrt(jnp.mean(values * values, axis=-1, keepdims=True) + 1e-06)
    scaled = upstream * gain
    inward = factor * scaled - values * factor * factor * factor * jnp.mean(
        scaled * values, axis=-1, keepdims=True
    )
    return inward, jnp.sum(upstream * values * factor, axis=0, keepdims=True)


def swap_halves(values):
    width = values.shape[1]
    lane = lax.broadcasted_iota(jnp.int32, values.shape, 1)
    return jnp.where(
        lax.rem(lane, HEAD) < HEAD // 2,
        pltpu.roll(values, width - HEAD // 2, 1),
        pltpu.roll(values, HEAD // 2, 1),
    )


def turn(values, cosine, sine):
    times = values.shape[1] // cosine.shape[1]
    return values * jnp.concatenate([cosine] * times, axis=1) + swap_halves(
        values
    ) * jnp.concatenate([sine] * times, axis=1)


def allowed_keys(seg_row, seg_col, offset, rows, extent):
    row_index = offset + lax.broadcasted_iota(jnp.int32, (rows, extent), 0)
    column_index = lax.broadcasted_iota(jnp.int32, (rows, extent), 1)
    return (column_index <= row_index) & (
        seg_row[:, :extent] == seg_col[offset : offset + rows, :]
    )


def softmax_rows(query, keys, allowed):
    masked = jnp.where(allowed, nt(query, keys), -1e30)
    exponent = jnp.exp(masked - jnp.max(masked, axis=-1, keepdims=True))
    return exponent * (1.0 / jnp.sum(exponent, axis=-1, keepdims=True))


def sigmoid(values):
    return 1.0 / (1.0 + jnp.exp(-values))


def attention_forward(
    x_ref, gain_ref, w_hbm, cos_ref, sin_ref, segr_ref, segc_ref,
    mid_ref, nrm_hbm, qk_hbm, v_hbm, att_hbm,
    w, qk, v, att, nrm, gsend, grecv, part, landing, summed, crossed, ssend, srecv, lsem,
):
    place, local = Place(), Local(lsem)
    load = local.start(w_hbm, w)
    place.greet()
    length = nrm.shape[0]
    heads = v.shape[1] // HEAD
    wide = heads * HEAD
    gather = TokenGather(place, nrm, gsend, grecv)
    nrm[gather.rows(place.me), :] = normalise(x_ref[...], gain_ref[...]).astype(BF16)
    gather.start()
    load.wait()
    for owner in gather.arrivals():
        rows = gather.rows(owner)
        projected = nn(nrm[rows, :], w[:, : 3 * wide])
        qk[rows, :] = turn(projected[:, : 2 * wide], cos_ref[rows, :], sin_ref[rows, :]).astype(BF16)
        v[rows, :] = projected[:, 2 * wide :].astype(BF16)
    gather.close()
    local.start(nrm, nrm_hbm, True)
    local.start(qk, qk_hbm, True)
    local.start(v, v_hbm, True)
    block = 256
    for offset in range(0, length, block):
        extent = offset + block
        allowed = allowed_keys(segr_ref, segc_ref, offset, block, extent)
        for head in range(heads):
            query = qk[offset:extent, head * HEAD : (head + 1) * HEAD] * BF16(HEAD**-0.5)
            keys = qk[:extent, wide + head * HEAD : wide + (head + 1) * HEAD]
            values = v[:extent, head * HEAD : (head + 1) * HEAD]
            probability = softmax_rows(query, keys, allowed).astype(BF16)
            att[offset:extent, head * HEAD : (head + 1) * HEAD] = nn(probability, values).astype(BF16)
    local.start(att, att_hbm, True)
    scatter = TokenScatter(place, part, landing, summed, crossed, ssend, srecv)
    outward = w[:, 3 * wide :]
    mid_ref[...] = x_ref[...] + scatter.run(lambda owner: nt(att[scatter.rows(owner), :], outward))
    local.close()


def attention_backward(
    up_ref, x_ref, gain_ref, w_hbm, nrm_hbm, qk_hbm, v_hbm, att_hbm, cos_ref, sin_ref, segr_ref, segc_ref,
    grad_ref, gain_grad_ref, dw_hbm,
    w, dw, nrm, qk, v, att, datt, dqk, dv, dqkv,
    up, gsend, grecv, part, landing, summed, crossed, ssend, srecv, lsem,
):
    place, local = Place(), Local(lsem)
    loads = [local.start(a, b) for a, b in ((w_hbm, w), (att_hbm, att), (qk_hbm, qk), (v_hbm, v), (nrm_hbm, nrm))]
    place.greet()
    length = nrm.shape[0]
    heads = v.shape[1] // HEAD
    wide = heads * HEAD
    gather = TokenGather(place, up, gsend, grecv)
    up[gather.rows(place.me), :] = up_ref[...].astype(BF16)
    gather.start()
    loads[0].wait()
    outward = w[:, 3 * wide :]
    for owner in gather.arrivals():
        rows = gather.rows(owner)
        datt[rows, :] = nn(up[rows, :], outward).astype(BF16)
    gather.close()
    for load in loads[1:]:
        load.wait()
    dqk[...] = jnp.zeros_like(dqk)
    dv[...] = jnp.zeros_like(dv)
    block = 256
    for offset in range(0, length, block):
        extent = offset + block
        allowed = allowed_keys(segr_ref, segc_ref, offset, block, extent)
        for head in range(heads):
            own = slice(head * HEAD, (head + 1) * HEAD)
            key_columns = slice(wide + head * HEAD, wide + (head + 1) * HEAD)
            query = qk[offset:extent, own] * BF16(HEAD**-0.5)
            keys = qk[:extent, key_columns]
            values = v[:extent, own]
            outer = datt[offset:extent, own]
            probability = softmax_rows(query, keys, allowed)
            inner = nt(outer, values)
            score = probability * (inner - jnp.sum(probability * inner, axis=-1, keepdims=True))
            score = score.astype(BF16)
            dqk[offset:extent, own] = nn(score, keys) * HEAD**-0.5
            dqk[:extent, key_columns] += tn(score, query)
            dv[:extent, own] += tn(probability.astype(BF16), outer)
    for offset in range(0, length, block):
        rows = slice(offset, offset + block)
        dqkv[rows, : 2 * wide] = turn(dqk[rows, :], cos_ref[rows, :], -sin_ref[rows, :]).astype(BF16)
        dqkv[rows, 2 * wide :] = dv[rows, :].astype(BF16)
    scatter = TokenScatter(place, part, landing, summed, crossed, ssend, srecv)
    inward = w[:, : 3 * wide]
    total = scatter.run(lambda owner: nt(dqkv[scatter.rows(owner), :], inward))
    dw[:, : 3 * wide] = tn(nrm[...], dqkv[...]).astype(BF16)
    dw[:, 3 * wide :] = tn(up[...], att[...]).astype(BF16)
    local.start(dw, dw_hbm, True)
    inward, gain_part = normalise_back(x_ref[...], gain_ref[...], total)
    grad_ref[...] = up_ref[...] + inward
    gain_grad_ref[...] = gain_part
    local.close()


def pick_softmax(logits, chosen, axis):
    highest = jnp.max(jnp.where(chosen > 0, logits, -1e30), axis=axis, keepdims=True)
    exponent = chosen * jnp.exp(jnp.where(chosen > 0, logits - highest, 0.0))
    return exponent / jnp.sum(exponent, axis=axis, keepdims=True)


def slots_by_token(slot_row):
    shape = (CAP, slot_row.shape[1])
    return lax.broadcasted_iota(jnp.int32, shape, 0) == slot_row


def tokens_by_slot(slot_column):
    shape = (slot_column.shape[0], CAP)
    return lax.broadcasted_iota(jnp.int32, shape, 1) == slot_column


def ffn_forward(
    mid_ref, gain_ref, w_hbm, router_ref, router_t_ref, slotr_ref, slotc_ref, chosenr_ref, chosenc_ref,
    next_ref, gates_ref, moe_hbm, routed_hbm, act_hbm, shared_hbm,
    w, routed, act, shared, branch, gates,
    moe, gsend, grecv, part, landing, summed, crossed, ssend, srecv, lsem,
):
    place, local = Place(), Local(lsem)
    experts = routed.shape[0]
    units = w.shape[2] // 3
    loads = {e: local.start(w_hbm.at[e], w.at[e]) for e in (experts, *range(experts))}
    place.greet()
    gather = TokenGather(place, moe, gsend, grecv)
    moe[gather.rows(place.me), :] = normalise(mid_ref[...], gain_ref[...]).astype(BF16)
    gather.start()
    loads[experts].wait()
    for owner in gather.arrivals():
        rows = gather.rows(owner)
        inner = nn(moe[rows, :], w[experts, :, : 2 * units])
        shared[rows, :] = inner.astype(BF16)
        gate = inner[:, :units]
        hidden = (gate * sigmoid(gate) * inner[:, units:]).astype(BF16)
        branch[rows, :] = nt(hidden, w[experts, :, 2 * units :])
        logits = nn(moe[rows, :], router_ref[...])
        gates[rows, :] = pick_softmax(logits, chosenc_ref[rows, :], 1)
    gather.close()
    local.start(moe, moe_hbm, True)
    local.start(shared, shared_hbm, True)
    gates_ref[...] = pick_softmax(nt(router_t_ref[...], moe[...]), chosenr_ref[...], 0)
    scatter = TokenScatter(place, part, landing, summed, crossed, ssend, srecv)
    outs = None
    for e in range(experts):
        loads[e].wait()
        dispatch = slots_by_token(slotr_ref[e : e + 1, :]).astype(F32).astype(BF16)
        picked = nn(dispatch, moe[...]).astype(BF16)
        routed[e] = picked
        local.start(routed.at[e], routed_hbm.at[e], True)
        inner = nn(picked, w[e, :, : 2 * units])
        act[e] = inner.astype(BF16)
        local.start(act.at[e], act_hbm.at[e], True)
        gate = inner[:, :units]
        hidden = (gate * sigmoid(gate) * inner[:, units:]).astype(BF16)
        outs = nt(hidden, w[e, :, 2 * units :]).astype(BF16)
        if e < experts - 1:
            combine = tokens_by_slot(slotc_ref[:, e : e + 1]).astype(F32).astype(BF16)
            branch[...] += gates[:, e : e + 1] * nn(combine, outs)

    def block_of(owner):
        rows = scatter.rows(owner)
        combine = tokens_by_slot(slotc_ref[rows, experts - 1 : experts]).astype(F32).astype(BF16)
        return branch[rows, :] + gates[rows, experts - 1 : experts] * nn(combine, outs)

    next_ref[...] = mid_ref[...] + scatter.run(block_of)
    local.close()


def swiglu_back(down, inner):
    units = inner.shape[1] // 2
    gate, raised = inner[:, :units], inner[:, units:]
    squashed = sigmoid(gate)
    gate_grad = down * raised * squashed * (1.0 + gate * (1.0 - squashed))
    up_grad = down * gate * squashed
    return jnp.concatenate([gate_grad.astype(BF16), up_grad.astype(BF16)], axis=1)


def hidden_of(inner):
    units = inner.shape[1] // 2
    gate = inner[:, :units]
    return (gate * sigmoid(gate) * inner[:, units:]).astype(BF16)


def ffn_backward(
    up_ref, mid_ref, gain_ref, w_hbm, moe_hbm, routed_hbm, act_hbm, shared_hbm,
    gates_ref, slotr_ref, slotc_ref, chosenr_ref, router_t_ref,
    grad_ref, gain_grad_ref, router_grad_ref, dw_hbm,
    w, dw, moe, routed, act, shared, hidden_all, moe_grad, slot_sums, logit_grad,
    up, gsend, grecv, part, landing, summed, crossed, ssend, srecv, lsem,
):
    place, local = Place(), Local(lsem)
    experts = routed.shape[0]
    units = w.shape[2] // 3
    load_w = {experts: local.start(w_hbm.at[experts], w.at[experts])}
    load_shared = local.start(shared_hbm, shared)
    load_moe = local.start(moe_hbm, moe)
    load_act, load_routed = {}, {}
    for e in range(experts):
        load_w[e] = local.start(w_hbm.at[e], w.at[e])
        load_act[e] = local.start(act_hbm.at[e], act.at[e])
        load_routed[e] = local.start(routed_hbm.at[e], routed.at[e])
    place.greet()
    gather = TokenGather(place, up, gsend, grecv)
    up[gather.rows(place.me), :] = up_ref[...].astype(BF16)
    gather.start()
    load_w[experts].wait()
    load_shared.wait()
    for owner in gather.arrivals():
        rows = gather.rows(owner)
        inner = shared[rows, :].astype(F32)
        hidden_all[rows, :] = hidden_of(inner)
        down = nn(up[rows, :], w[experts, :, 2 * units :])
        inner_grad = swiglu_back(down, inner)
        shared[rows, :] = inner_grad
        moe_grad[rows, :] = nt(inner_grad, w[experts, :, : 2 * units])
    gather.close()
    load_moe.wait()
    dw[experts, :, : 2 * units] = tn(moe[...], shared[...]).astype(BF16)
    dw[experts, :, 2 * units :] = tn(up[...], hidden_all[...]).astype(BF16)
    local.start(dw.at[experts], dw_hbm.at[experts], True)
    slot_sums[...] = jnp.zeros_like(slot_sums)
    back = None
    for e in range(experts):
        load_w[e].wait()
        load_act[e].wait()
        load_routed[e].wait()
        held = slots_by_token(slotr_ref[e : e + 1, :])
        dispatch = held.astype(F32).astype(BF16)
        gate_slot = jnp.sum(jnp.where(held, gates_ref[e : e + 1, :], 0.0), axis=1, keepdims=True)
        arrived = nn(dispatch, up[...]).astype(BF16)
        slot_grad = (arrived.astype(F32) * gate_slot).astype(BF16)
        inner = act[e].astype(F32)
        hidden = hidden_of(inner)
        down = nn(arrived, w[e, :, 2 * units :])
        slot_dot = jnp.sum(hidden.astype(F32) * down, axis=1, keepdims=True)
        slot_sums[e : e + 1, :] = jnp.sum(jnp.where(held, slot_dot, 0.0), axis=0, keepdims=True)
        inner_grad = swiglu_back(down * gate_slot, inner)
        dw[e, :, : 2 * units] = tn(routed[e], inner_grad).astype(BF16)
        dw[e, :, 2 * units :] = tn(slot_grad, hidden).astype(BF16)
        local.start(dw.at[e], dw_hbm.at[e], True)
        back = nt(inner_grad, w[e, :, : 2 * units]).astype(BF16)
        if e < experts - 1:
            combine = tokens_by_slot(slotc_ref[:, e : e + 1]).astype(F32).astype(BF16)
            moe_grad[...] += nn(combine, back)
    gates = gates_ref[...]
    chosen = chosenr_ref[...]
    pair = jnp.sum(gates, axis=0, keepdims=True)
    product = 0.5 * (pair * pair - jnp.sum(gates * gates, axis=0, keepdims=True))
    sums = slot_sums[...]
    logit_grad[...] = (
        chosen * product * (2.0 * sums - jnp.sum(sums, axis=0, keepdims=True))
    ).astype(BF16)
    router_grad_ref[...] = nn(logit_grad[...], moe[...])
    scatter = TokenScatter(place, part, landing, summed, crossed, ssend, srecv)

    def block_of(owner):
        rows = scatter.rows(owner)
        combine = tokens_by_slot(slotc_ref[rows, experts - 1 : experts]).astype(F32).astype(BF16)
        return moe_grad[rows, :] + nn(combine, back) + tn(logit_grad[:, rows], router_t_ref[...])

    total = scatter.run(block_of)
    inward, gain_part = normalise_back(mid_ref[...], gain_ref[...], total)
    grad_ref[...] = up_ref[...] + inward
    gain_grad_ref[...] = gain_part
    local.close()


def call(body, collective_id, arguments, in_hbm, outs, scratch):
    hbm, vmem = pl.BlockSpec(memory_space=pl.ANY), pl.BlockSpec(memory_space=pltpu.VMEM)
    return pl.pallas_call(
        body,
        out_shape=[jax.ShapeDtypeStruct(shape, kind) for shape, kind, _ in outs],
        in_specs=[hbm if index in in_hbm else vmem for index in range(len(arguments))],
        out_specs=[hbm if far else vmem for _, _, far in outs],
        scratch_shapes=scratch,
        compiler_params=pltpu.CompilerParams(
            collective_id=collective_id, has_side_effects=True, vmem_limit_bytes=VMEM_LIMIT
        ),
    )(*arguments)


def on_device(
    stream, cotangent, segments, expert_pick, slot_index, norm_gains,
    attention, projection, router, widening, narrowing, expansion, contraction,
):
    layers = attention.shape[0]
    segment = segments[0]
    length = segment.shape[0]
    experts = expansion.shape[1]
    width = stream.shape[1]
    quarter = stream.shape[0]
    wide = attention.shape[3]
    units = widening.shape[3]
    rows = attention.shape[2]

    halfway = HEAD // 2
    inverse = jnp.exp(
        jnp.arange(halfway, dtype=F32) * (-2.0 * math.log(10000.0) / HEAD)
    )
    phases = jnp.arange(length, dtype=F32)[:, None] * inverse[None, :]
    cosine, sine = jnp.cos(phases), jnp.sin(phases)
    cosine = jnp.concatenate([cosine] * 4, axis=1)
    sine = jnp.concatenate([-sine, sine] * 2, axis=1)
    seg_row, seg_col = segment[None, :], segment[:, None]

    expert_ids = jnp.arange(experts, dtype=jnp.int32)
    picked = expert_pick[..., None] == expert_ids
    slots = jnp.sum(jnp.where(picked, slot_index[..., None] + 1, 0), axis=2) - 1
    chosen = jnp.any(picked, axis=2).astype(F32)
    slot_cols = slots
    slot_rows = jnp.swapaxes(slots, 1, 2)
    chosen_cols = jnp.pad(chosen, ((0, 0), (0, 0), (0, LANES - experts)))
    chosen_rows = jnp.pad(jnp.swapaxes(chosen, 1, 2), ((0, 0), (0, 8 - experts), (0, 0)))
    router_wide = jnp.pad(router, ((0, 0), (0, 0), (0, LANES - experts)))
    router_t = jnp.pad(jnp.swapaxes(router, 1, 2), ((0, 0), (0, 8 - experts), (0, 0)))

    att_shards = jnp.concatenate(
        [attention[:, 0], attention[:, 1], attention[:, 2], jnp.swapaxes(projection, 1, 2)], axis=-1
    )
    shared_shards = jnp.concatenate(
        [widening[:, 0], widening[:, 1], jnp.swapaxes(narrowing, 1, 2)], axis=-1
    )
    expert_shards = jnp.concatenate(
        [expansion[:, :, 0], expansion[:, :, 1], jnp.swapaxes(contraction, 2, 3)], axis=-1
    )
    ffn_shards = jnp.concatenate([expert_shards, shared_shards[:, None]], axis=1)

    att_full, ffn_full = [], []
    for layer in range(layers):
        att_full.append(lax.all_gather(att_shards[layer], "dp", axis=0, tiled=True))
        ffn_full.append(lax.all_gather(ffn_shards[layer], "dp", axis=1, tiled=True))

    token_gather, token_scatter = gather_scratch(length, width), scatter_scratch(length, width)
    dma = pltpu.SemaphoreType.DMA
    saved = []
    current = stream
    for layer in range(layers):
        mid, normed, qk, values, attended = call(
            attention_forward,
            0,
            (current, norm_gains[layer, 0][None], att_full[layer], cosine, sine, seg_row, seg_col),
            (2,),
            [
                ((quarter, width), F32, False),
                ((length, width), BF16, True),
                ((length, 2 * wide), BF16, True),
                ((length, wide), BF16, True),
                ((length, wide), BF16, True),
            ],
            [
                pltpu.VMEM((width, 4 * wide), BF16),
                pltpu.VMEM((length, 2 * wide), BF16),
                pltpu.VMEM((length, wide), BF16),
                pltpu.VMEM((length, wide), BF16),
                *token_gather,
                *token_scatter,
                dma((5,)),
            ],
        )
        following, gates, moe_in, routed, act, shared = call(
            ffn_forward,
            1,
            (
                mid, norm_gains[layer, 1][None], ffn_full[layer], router_wide[layer], router_t[layer],
                slot_rows[layer], slot_cols[layer], chosen_rows[layer], chosen_cols[layer],
            ),
            (2,),
            [
                ((quarter, width), F32, False),
                ((8, length), F32, False),
                ((length, width), BF16, True),
                ((experts, CAP, width), BF16, True),
                ((experts, CAP, 2 * units), BF16, True),
                ((length, 2 * units), BF16, True),
            ],
            [
                pltpu.VMEM((experts + 1, width, 3 * units), BF16),
                pltpu.VMEM((experts, CAP, width), BF16),
                pltpu.VMEM((experts, CAP, 2 * units), BF16),
                pltpu.VMEM((length, 2 * units), BF16),
                pltpu.VMEM((length, width), F32),
                pltpu.VMEM((length, LANES), F32),
                *token_gather,
                *token_scatter,
                dma((3 * experts + 3,)),
            ],
        )
        saved.append((current, normed, qk, values, attended, mid, gates, moe_in, routed, act, shared))
        current = following

    upstream = cotangent
    gain_parts, router_parts = [None] * layers, [None] * layers
    att_grads, ffn_grads = [None] * layers, [None] * layers
    for layer in reversed(range(layers)):
        x_in, normed, qk, values, attended, mid, gates, moe_in, routed, act, shared = saved[layer]
        mid_grad, gain_two, router_parts[layer], ffn_part = call(
            ffn_backward,
            2,
            (
                upstream, mid, norm_gains[layer, 1][None], ffn_full[layer], moe_in, routed, act, shared,
                gates, slot_rows[layer], slot_cols[layer], chosen_rows[layer], router_t[layer],
            ),
            (3, 4, 5, 6, 7),
            [
                ((quarter, width), F32, False),
                ((1, width), F32, False),
                ((8, width), F32, False),
                ((experts + 1, width, 3 * units), BF16, True),
            ],
            [
                pltpu.VMEM((experts + 1, width, 3 * units), BF16),
                pltpu.VMEM((experts + 1, width, 3 * units), BF16),
                pltpu.VMEM((length, width), BF16),
                pltpu.VMEM((experts, CAP, width), BF16),
                pltpu.VMEM((experts, CAP, 2 * units), BF16),
                pltpu.VMEM((length, 2 * units), BF16),
                pltpu.VMEM((length, units), BF16),
                pltpu.VMEM((length, width), F32),
                pltpu.VMEM((8, length), F32),
                pltpu.VMEM((8, length), BF16),
                *token_gather,
                *token_scatter,
                dma((4 * experts + 4,)),
            ],
        )
        ffn_grads[layer] = lax.psum_scatter(ffn_part, "dp", scatter_dimension=1, tiled=True)
        upstream, gain_one, att_part = call(
            attention_backward,
            3,
            (
                mid_grad, x_in, norm_gains[layer, 0][None], att_full[layer], normed, qk, values, attended,
                cosine, sine, seg_row, seg_col,
            ),
            (3, 4, 5, 6, 7),
            [
                ((quarter, width), F32, False),
                ((1, width), F32, False),
                ((width, 4 * wide), BF16, True),
            ],
            [
                pltpu.VMEM((width, 4 * wide), BF16),
                pltpu.VMEM((width, 4 * wide), BF16),
                pltpu.VMEM((length, width), BF16),
                pltpu.VMEM((length, 2 * wide), BF16),
                pltpu.VMEM((length, wide), BF16),
                pltpu.VMEM((length, wide), BF16),
                pltpu.VMEM((length, wide), BF16),
                pltpu.VMEM((length, 2 * wide), F32),
                pltpu.VMEM((length, wide), F32),
                pltpu.VMEM((length, 3 * wide), BF16),
                *token_gather,
                *token_scatter,
                dma((6,)),
            ],
        )
        att_grads[layer] = lax.psum_scatter(att_part, "dp", scatter_dimension=0, tiled=True)
        gain_parts[layer] = jnp.concatenate([gain_one, gain_two], axis=0)

    gains_grad, router_grad = lax.psum(
        (jnp.stack(gain_parts), jnp.stack(router_parts)), ("dp", "tensor")
    )
    att_grad = jnp.stack(att_grads).astype(F32)
    ffn_grad = jnp.stack(ffn_grads).astype(F32)
    attention_grad = jnp.stack([att_grad[:, :, k * wide : (k + 1) * wide] for k in range(3)], axis=1)
    projection_grad = jnp.swapaxes(att_grad[:, :, 3 * wide :], 1, 2)
    pair = jnp.stack([ffn_grad[..., :units], ffn_grad[..., units : 2 * units]], axis=2)
    third = jnp.swapaxes(ffn_grad[..., 2 * units :], 2, 3)
    return (
        current,
        upstream,
        gains_grad,
        attention_grad,
        projection_grad,
        jnp.swapaxes(router_grad[:, :experts], 1, 2),
        pair[:, experts],
        third[:, experts],
        pair[:, :experts],
        third[:, :experts],
    )


def solution(mesh):
    placed = (
        P(("dp", "tensor"), None),
        P(("dp", "tensor"), None),
        P("dp", None),
        P(None, "dp", None),
        P(None, "dp", None),
        P(),
        P(None, None, "dp", "tensor"),
        P(None, "tensor", "dp"),
        P(),
        P(None, None, "dp", "tensor"),
        P(None, "tensor", "dp"),
        P(None, None, None, "dp", "tensor"),
        P(None, None, "tensor", "dp"),
    )
    return jax.shard_map(
        on_device,
        mesh=mesh,
        in_specs=placed,
        out_specs=(
            P(("dp", "tensor"), None),
            P(("dp", "tensor"), None),
            P(),
            P(None, None, "dp", "tensor"),
            P(None, "tensor", "dp"),
            P(),
            P(None, None, "dp", "tensor"),
            P(None, "tensor", "dp"),
            P(None, None, None, "dp", "tensor"),
            P(None, None, "tensor", "dp"),
        ),
        check_vma=False,
    )
```

time: 1760 us -> 1240 us (0.70)
  local copies, waits for them, and re-layouts: 396 us -> 25 us
  Pallas kernels: 0 us -> 370 us
  waiting for transfers between devices: 514 us -> 774 us
  blocking collectives: 282 us -> 39.8 us
  matrix products: 235 us -> 0 us
  other arithmetic: 239 us -> 8.34 us
  starting transfers between devices: 58.4 us -> 0.32 us
    reduce_scatter x8 -> x4, waiting for transfers between devices: 103 us -> 481 us  [the longest x2 395 us: on_device(): lax.psum_scatter(ffn_part, 'dp', scatter_dimension=1, tiled=True)]
    pallas_call x0 -> x8, Pallas kernels: none -> 370 us  [call(): pl.pallas_call(body, out_shape=[jax.ShapeDtypeStruct(shape, kind) for sha...]
    dot_general x64 -> x0, matrix products: 229 us -> none  [the longest x4 21.5 us: on_device(): jnp.einsum('qhd,khd->hqk', upstream_block, values, preferred_element_type...]
    all_gather x6 -> x0, blocking collectives: 211 us -> none  [the longest x2 76.3 us: fetch(): lax.all_gather(first, 'dp', axis=1, tiled=True)]
    all_to_all x12 -> x0, waiting for transfers between devices: 143 us -> none  [the longest x2 69.7 us: sum_layer(): lax.all_to_all(flats[5].astype(jnp.bfloat16), 'dp', split_axis=2, concat_...]
    gather x12 -> x0, local copies, waits for them, and re-layouts: 123 us -> none  [the longest x4 44.3 us: on_device(): moe_grad = moe_grad + jnp.sum(padded_routed[flat_slot], axis=1)]
    reduce_sum x35 -> x1, other arithmetic: 122 us -> 0.03 us  [on_device(): slots = jnp.sum(jnp.where(picked, slot_index[..., None] + 1, 0), axis=2) - 1]
    convert_element_type x14 -> x0, local copies, waits for them, and re-layouts: 76.4 us -> none  [the longest x2 31.7 us: sum_layer(): flats[5].astype(jnp.bfloat16)]
  transfers between devices with their start and end apart: 34 -> 8, of which waited for: 20 -> 7; matrix products, arithmetic and copies ran while one was open for 42% -> 2% of each run, Pallas kernels for 0% -> 9%
where the time goes in v1:
time: 1240 us; the launch traced here: 1230 us
  waiting for transfers between devices  774 us (62%)
  Pallas kernels  370 us (30%)
  blocking collectives  39.8 us (3%)
  local copies, waits for them, and re-layouts  25 us (2%)
  between operations  15 us (1%)
    reduce_scatter x2, waiting for transfers between devices, on_device(): lax.psum_scatter(ffn_part, 'dp', scatter_dimension=1, tiled=True)  395 us
    pallas_call x8, Pallas kernels, call(): pl.pallas_call(body, out_shape=[jax.ShapeDtypeStruct(shape, kind) for sha...  370 us
    all_gather x2, waiting for transfers between devices, on_device(): ffn_full.append(lax.all_gather(ffn_shards[layer], 'dp', axis=1, tiled=True))  263 us
    reduce_scatter x2, waiting for transfers between devices, on_device(): lax.psum_scatter(att_part, 'dp', scatter_dimension=0, tiled=True)  86 us
    psum x1, blocking collectives, on_device(): lax.psum((jnp.stack(gain_parts), jnp.stack(router_parts)), ('dp', 'tensor'))  39.8 us
    all_gather x2, waiting for transfers between devices, on_device(): att_full.append(lax.all_gather(att_shards[layer], 'dp', axis=0, tiled=True))  26.4 us
  transfers between devices with their start and end apart: 8, of which 7 were waited for; matrix products, arithmetic and copies ran while one was open for 2% of the time, Pallas kernels for 9%

profile of v1, /device:TPU:0, one launch (start us, length us, event | category | flops | bytes accessed | tf_op | source)
XLA Modules:
  0.0 1232.5 jit_solution(7062006645637577063)
XLA Ops:
  7.3 1.1 copy.72
  8.4 1.0 slice_bitcast_fusion.20
  9.4 0.1 pad_maximum_fusion.5
  9.5 0.7 fusion.10
  10.3 0.0 all-gather.11.cloned.1.call-start
  10.5 0.1 slice_bitcast_fusion.4
  10.6 0.9 copy-done.3
  11.5 0.3 pad_maximum_fusion.1
  11.8 1.8 fusion.9
  13.6 0.0 all-gather.13.cloned.1.call-start
  13.7 0.7 all-gather.13.cloned.1.call-update
  14.4 0.5 all-gather.15.cloned.1.call-update
  15.0 0.5 copy.80
  15.5 0.3 copy.78
  15.8 1.0 copy.73.segc_ref
  16.9 0.4 copy.79
  17.3 0.1 broadcast_add_fusion
  17.4 0.1 slice_bitcast_fusion.7
  17.5 0.8 copy.83.slotr_ref
  18.3 0.8 copy.81.slotr_ref
  19.1 0.6 fusion.7
  19.7 0.8 fusion.4
  20.5 0.1 pad_convert_fusion
  20.7 2.0 fusion.2
  22.6 1.8 pad_maximum_fusion.3
  24.5 0.6 slice_bitcast_fusion.24
  25.1 0.6 slice_bitcast_fusion.21
  25.7 1.0 slice_bitcast_fusion.5
  26.8 1.1 slice_bitcast_fusion.6
  27.8 26.4 %all-gather.9.cloned.1.call-done = bf16[1,768,768]{2,1,0:T(8,128)(2,1)} async-done(((bf16[1,96,768]{2,1,0:T(8,128)(2,1)}), bf16[1,768,768]{2,1,0:T(8,128)(2,1)}) %all-gather.9.cloned.1.call-update) | async-done | bytes 1179664 | tf_op jit(solution)/shard_map/all_gather | solution.py:556
  54.2 34.4 %shard_map.204 = (f32[256,768]{1,0:T(8,128)}, bf16[1024,768]{1,0:T(8,128)(2,1)}, bf16[1024,384]{1,0:T(8,128)(2,1)}, bf16[1024,192]{1,0:T(8,128)(2,1)}, bf16[1024,192]{1,0:T(8,128)(2,1)}) custom-call(f32[256,768]{1,0:T(8,128)} %x_ref.3, f32[1,768]{1,0:T(1,128)} %get-tuple-element.148.gain_ref, bf16[768,768]{1,0:T(8,128)(2,1)} %bitcast.108, ...), custom_call_target="tpu_custom_call" | custom-call | tf_op jit(solution)/shard_map/pallas_call | solution.py:496
  88.7 134.0 %all-gather.11.cloned.1.call-done = bf16[1,5,768,1536]{3,2,1,0:T(8,128)(2,1)} async-done(((bf16[1,5,96,1536]{3,2,1,0:T(8,128)(2,1)}), bf16[1,5,768,1536]{3,2,1,0:T(8,128)(2,1)}) %all-gather.11.cloned.1.call-update) | async-done | bytes 11796496 | tf_op jit(solution)/shard_map/all_gather | solution.py:557
  222.6 46.3 %shard_map.205 = (f32[256,768]{1,0:T(8,128)}, f32[8,1024]{1,0:T(8,128)}, bf16[1024,768]{1,0:T(8,128)(2,1)}, bf16[4,640,768]{2,1,0:T(8,128)(2,1)}, bf16[4,640,102...) custom-call(f32[256,768]{1,0:T(8,128)} %get-tuple-element.46.mid_ref, f32[1,768]{1,0:T(1,128)} %get-tuple-element.147.gain_ref, ...), custom_call_target="tpu_custom_call" | custom-call | tf_op jit(solution)/shard_map/pallas_call | solution.py:496
  268.9 34.4 %shard_map.206 = (f32[256,768]{1,0:T(8,128)}, bf16[1024,768]{1,0:T(8,128)(2,1)}, bf16[1024,384]{1,0:T(8,128)(2,1)}, bf16[1024,192]{1,0:T(8,128)(2,1)}, bf16[1024,192]{1,0:T(8,128)(2,1)}) custom-call(f32[256,768]{1,0:T(8,128)} %get-tuple-element.47.x_ref, f32[1,768]{1,0:T(1,128)} %get-tuple-element.149.gain_ref, bf16[768,768]{1,0:T(8,128)(2,1)} %bitcast.110, ...), custom_call_target="tpu_custom_call" | custom-call | tf_op jit(solution)/shard_map/pallas_call | solution.py:496
  303.3 129.1 %all-gather.15.cloned.1.call-done = bf16[1,5,768,1536]{3,2,1,0:T(8,128)(2,1)} async-done(((bf16[1,5,96,1536]{3,2,1,0:T(8,128)(2,1)}), bf16[1,5,768,1536]{3,2,1,0:T(8,128)(2,1)}) %all-gather.15.cloned.1.call-update) | async-done | bytes 11796496 | tf_op jit(solution)/shard_map/all_gather | solution.py:557
  432.3 46.7 %shard_map.207 = (f32[256,768]{1,0:T(8,128)}, f32[8,1024]{1,0:T(8,128)}, bf16[1024,768]{1,0:T(8,128)(2,1)}, bf16[4,640,768]{2,1,0:T(8,128)(2,1)}, bf16[4,640,102...) custom-call(f32[256,768]{1,0:T(8,128)} %get-tuple-element.48.mid_ref, f32[1,768]{1,0:T(1,128)} %get-tuple-element.146.gain_ref, ...), custom_call_target="tpu_custom_call" | custom-call | tf_op jit(solution)/shard_map/pallas_call | solution.py:496
  479.0 60.0 %shard_map.208 = (f32[256,768]{1,0:T(8,128)}, f32[1,768]{1,0:T(1,128)}, f32[8,768]{1,0:T(8,128)}, bf16[5,768,1536]{2,1,0:T(8,128)(2,1)}) custom-call(f32[256,768]{1,0:T(8,128)} %up_ref.1, f32[256,768]{1,0:T(8,128)} %get-tuple-element.48.mid_ref, f32[1,768]{1,0:T(1,128)} %get-tuple-element.146.gain_ref, bf16[5,768,1536]{2,1,0:T(8,128)(2,1)} %bitcast.107, ...), custom_call_target="tpu_custom_call" | custom-call | tf_op jit(solution)/shard_map/pallas_call | solution.py:496
  539.1 44.2 %shard_map.209 = (f32[256,768]{1,0:T(8,128)}, f32[1,768]{1,0:T(1,128)}, bf16[768,768]{1,0:T(8,128)(2,1)}) custom-call(f32[256,768]{1,0:T(8,128)} %get-tuple-element.55.up_ref, f32[256,768]{1,0:T(8,128)} %get-tuple-element.47.x_ref, f32[1,768]{1,0:T(1,128)} %get-tuple-element.149.gain_ref, bf16[768,768]{1,0:T(8,128)(2,1)} %bitcast.111, ...), custom_call_target="tpu_custom_call" | custom-call | tf_op jit(solution)/shard_map/pallas_call | solution.py:496
  583.2 60.0 %shard_map.210 = (f32[256,768]{1,0:T(8,128)}, f32[1,768]{1,0:T(1,128)}, f32[8,768]{1,0:T(8,128)}, bf16[5,768,1536]{2,1,0:T(8,128)(2,1)}) custom-call(f32[256,768]{1,0:T(8,128)} %get-tuple-element.60.up_ref, f32[256,768]{1,0:T(8,128)} %get-tuple-element.46.mid_ref, f32[1,768]{1,0:T(1,128)} %get-tuple-element.147.gain_ref, bf16[5,768,1536]{2,1,0:T(8,128)(2,1)} %bitcast.105, ...), custom_call_target="tpu_custom_call" | custom-call | tf_op jit(solution)/shard_map/pallas_call | solution.py:496
  643.2 44.2 %shard_map.211 = (f32[256,768]{1,0:T(8,128)}, f32[1,768]{1,0:T(1,128)}, bf16[768,768]{1,0:T(8,128)(2,1)}) custom-call(f32[256,768]{1,0:T(8,128)} %get-tuple-element.66.up_ref, f32[256,768]{1,0:T(8,128)} %x_ref.3, f32[1,768]{1,0:T(1,128)} %get-tuple-element.148.gain_ref, bf16[768,768]{1,0:T(8,128)(2,1)} %bitcast.109, ...), custom_call_target="tpu_custom_call" | custom-call | tf_op jit(solution)/shard_map/pallas_call | solution.py:496
  687.5 0.5 reduce-scatter.7.cloned.1.call-update
  688.0 0.7 reduce-scatter.9.cloned.1.call-update
  688.8 0.6 reduce-scatter.11.cloned.1.call-update
  689.6 39.8 %all-reduce.4 = (f32[2,2,768]{2,1,0:T(2,128)}, f32[2,8,768]{2,1,0:T(8,128)S(1)}) all-reduce(f32[2,2,768]{2,1,0:T(2,128)S(1)} %pad_maximum_fusion.7, f32[2,8,768]{2,1,0:T(8,128)S(1)} %pad_maximum_fusion.6), channel_id=1, replica_groups=mesh['dp'=8,'tensor'=4] {'dp','tensor'}, use_global_device_ids=true, to_apply=%region_2.3 | all-reduce | flops 15360 | bytes 122880 | tf_op jit(solution)/shard_map/psum | solution.py:685
  729.4 0.6 slice_bitcast_fusion.23
  730.0 19.8 %reduce-scatter.5.cloned.1.call-done = bf16[96,768]{1,0:T(8,128)(2,1)} async-done(((bf16[768,768]{1,0:T(8,128)(2,1)}), bf16[96,768]{1,0:T(8,128)(2,1)}) %reduce-scatter.5.cloned.1.call-update) | async-done | bytes 147472 | tf_op jit(solution)/shard_map/reduce_scatter | solution.py:682
  749.9 66.2 %reduce-scatter.7.cloned.1.call-done = bf16[96,768]{1,0:T(8,128)(2,1)} async-done(((bf16[768,768]{1,0:T(8,128)(2,1)}), bf16[96,768]{1,0:T(8,128)(2,1)}) %reduce-scatter.7.cloned.1.call-update) | async-done | bytes 147472 | tf_op jit(solution)/shard_map/reduce_scatter | solution.py:682
  816.1 1.0 maximum_convert_fusion.1
  817.1 0.2 slice_bitcast_fusion.12
  817.3 0.8 copy.89
  818.1 0.9 copy.88
  819.0 196.0 %reduce-scatter.9.cloned.1.call-done = bf16[5,96,1536]{2,1,0:T(8,128)(2,1)} async-done(((bf16[5,768,1536]{2,1,0:T(8,128)(2,1)}), bf16[5,96,1536]{2,1,0:T(8,128)(2,1)}) %reduce-scatter.9.cloned.1.call-update) | async-done | bytes 1474576 | tf_op jit(solution)/shard_map/reduce_scatter | solution.py:652
  1015.0 199.4 %reduce-scatter.11.cloned.1.call-done = bf16[5,96,1536]{2,1,0:T(8,128)(2,1)} async-done(((bf16[5,768,1536]{2,1,0:T(8,128)(2,1)}), bf16[5,96,1536]{2,1,0:T(8,128)(2,1)}) %reduce-scatter.11.cloned.1.call-update) | async-done | bytes 1474576 | tf_op jit(solution)/shard_map/reduce_scatter | solution.py:652
  1214.4 2.2 maximum_convert_fusion
  1216.6 1.0 slice_bitcast_fusion
  1217.6 0.8 slice_bitcast_fusion.11
  1218.4 1.3 slice.189
  1219.6 0.1 maximum_bitcast_fusion
  1219.7 0.4 pad_maximum_fusion
  1220.1 2.0 copy.91
  1222.1 0.9 copy.90
  1223.0 0.5 copy-done.1
  1223.5 0.9 copy.101
  1224.4 0.9 copy.102
  (54 shorter events, 0.6 us)
Async XLA Ops:
  7.2 3.2 copy-start.4
  7.2 3.2 copy-start.5
  7.2 3.3 copy-start
  7.2 47.0 %all-gather.9.cloned.1.call-start = ((), (), s32[]{:S(2)}) async-start(), calls=%async_computation.8 | async-start | bytes 1327104 | tf_op jit(solution)/shard_map/all_gather | solution.py:556
  10.3 212.3 %all-gather.11.cloned.1.call-start = ((), (), s32[]{:S(2)}) async-start(), calls=%async_computation.9 | async-start | bytes 13271040 | tf_op jit(solution)/shard_map/all_gather | solution.py:557
  10.4 1.1 copy-start.3
  13.6 1.4 copy-start.7
  13.6 1.9 copy-start.8
  13.6 2.2 copy-start.6
  13.6 3.3 copy-start.11
  13.6 255.3 %all-gather.13.cloned.1.call-start = ((), (), s32[]{:S(2)}) async-start(), calls=%async_computation.10 | async-start | bytes 1327104 | tf_op jit(solution)/shard_map/all_gather | solution.py:556
  14.4 418.0 %all-gather.15.cloned.1.call-start = ((), (), s32[]{:S(2)}) async-start(), calls=%async_computation.11 | async-start | bytes 13271040 | tf_op jit(solution)/shard_map/all_gather | solution.py:557
  15.0 734.9 %reduce-scatter.5.cloned.1.call-start = ((), (), s32[]{:S(2)}) async-start(), calls=%async_computation.4 | async-start | bytes 1327104 | tf_op jit(solution)/shard_map/reduce_scatter | solution.py:682
  20.6 3.8 copy-start.12
  687.4 128.7 %reduce-scatter.7.cloned.1.call-start = ((), (), s32[]{:S(2)}) async-start(), calls=%async_computation.5 | async-start | bytes 1327104 | tf_op jit(solution)/shard_map/reduce_scatter | solution.py:682
  688.0 327.0 %reduce-scatter.9.cloned.1.call-start = ((), (), s32[]{:S(2)}) async-start(), calls=%async_computation.6 | async-start | bytes 13271040 | tf_op jit(solution)/shard_map/reduce_scatter | solution.py:652
  688.7 525.7 %reduce-scatter.11.cloned.1.call-start = ((), (), s32[]{:S(2)}) async-start(), calls=%async_computation.7 | async-start | bytes 13271040 | tf_op jit(solution)/shard_map/reduce_scatter | solution.py:652
  688.8 0.7 copy-start.15
  688.8 0.7 copy-start.16
  688.8 0.7 copy-start.13
  688.8 0.7 copy-start.14
  688.8 0.8 copy-start.9
  688.8 0.8 copy-start.10
  1222.1 1.4 copy-start.1
  1222.1 2.3 copy-start.2
Sparse Core Ops, SparseCore 0:
  10.4 43.7 all-gather.8
  57.0 165.5 all-gather.10
  224.8 39.2 all-gather.12
  266.7 165.5 all-gather.14
  687.5 62.2 reduce-scatter.4
  753.1 62.9 reduce-scatter.6
  819.7 195.3 reduce-scatter.8
  1019.1 195.2 reduce-scatter.10

commit v2 on v1

v2 whole, which is shorter than its diff:
```python
import functools
import math
import types

import jax
import jax.numpy as jnp
from jax import lax
from jax.experimental import pallas as pl
from jax.experimental.pallas import tpu as pltpu
from jax.sharding import PartitionSpec as P

HEAD = 64
CAP = 640
LANES = 128
BF16 = jnp.bfloat16
F32 = jnp.float32
ATT, SH, EX = range(3)
NRM, QK, V, ATTENDED = range(4)
MOE, SHARED, ROUTED, ACT = range(4)
GET_Z, GET_X, SUM_X, SUM_Z = range(4)
VMEM_LIMIT = 60 * 1024 * 1024


def nn(left, right):
    return lax.dot_general(left, right, (((1,), (0,)), ((), ())), preferred_element_type=F32)


def nt(left, right):
    return lax.dot_general(left, right, (((1,), (1,)), ((), ())), preferred_element_type=F32)


def tn(left, right):
    return lax.dot_general(left, right, (((0,), (0,)), ((), ())), preferred_element_type=F32)


class Place:
    def __init__(self):
        self.dp = lax.axis_index("dp")
        self.me = lax.axis_index("tensor")
        core = lax.rem(self.me, 2)
        self.core_peer = self.me + 1 - 2 * core
        self.y_peer = lax.rem(self.me + 2, 4)
        self.far_peer = lax.rem(self.core_peer + 2, 4)
        self.z = lax.div(self.dp, 2)
        self.x = lax.rem(self.dp, 2)
        self.half = lax.rem(self.z, 2)

    def member(self, tensor):
        return (self.dp, tensor)

    def row(self, away, x):
        return lax.rem(self.z + away + 4, 4) * 2 + x

    def beyond(self, away):
        return (self.row(away, self.x), self.me)

    def beside(self):
        return (self.row(0, 1 - self.x), self.me)

    def partner(self):
        return ((self.z + 1 - 2 * self.half) * 2 + self.x, self.me)

    def greet(self, peers):
        barrier = pltpu.get_barrier_semaphore()
        for peer in peers:
            pl.semaphore_signal(barrier, inc=1, device_id=peer, device_id_type=pl.DeviceIdType.MESH)
        pl.semaphore_wait(barrier, len(peers))

    def greet_sequence(self):
        return [self.member(self.core_peer), self.member(self.y_peer)]

    def greet_all(self):
        return [self.beside(), self.beyond(1), self.beyond(2), self.beyond(3)]


def send(source, target, send_sem, recv_sem, device):
    copy = pltpu.make_async_remote_copy(
        src_ref=source,
        dst_ref=target,
        send_sem=send_sem,
        recv_sem=recv_sem,
        device_id=device,
        device_id_type=pl.DeviceIdType.MESH,
    )
    copy.start()
    return copy


class Local:
    def __init__(self, sems):
        self.sems, self.used, self.open = sems, 0, []

    def start(self, source, target, keep=False):
        copy = pltpu.make_async_copy(source, target, self.sems.at[self.used])
        self.used += 1
        copy.start()
        if keep:
            self.open.append(copy)
        return copy

    def close(self):
        for copy in self.open:
            copy.wait()


def quarter_rows(length, member):
    quarter = length // 4
    return pl.ds(pl.multiple_of(member * quarter, quarter), quarter)


class TokenGather:
    def __init__(self, place, buf, sems):
        self.place, self.buf = place, buf
        self.sems = (sems["send_sem"], sems["recv_sem"])

    def rows(self, member):
        return quarter_rows(self.buf.shape[0], member)

    def pass_on(self, owner, target, slot):
        block = self.buf.at[self.rows(owner)]
        return send(block, block, self.sems[0].at[slot], self.sems[1].at[slot], self.place.member(target))

    def start(self):
        place = self.place
        self.far = self.pass_on(place.me, place.y_peer, 1)
        self.near = self.pass_on(place.me, place.core_peer, 0)

    def arrivals(self):
        place = self.place
        yield place.me
        self.near.wait_recv()
        yield place.core_peer
        self.far.wait_recv()
        self.onward = self.pass_on(place.y_peer, place.core_peer, 2)
        yield place.y_peer
        self.onward.wait_recv()
        yield place.far_peer
        self.near.wait_send()
        self.far.wait_send()
        self.onward.wait_send()


class TokenScatter:
    def __init__(self, place, refs):
        self.place = place
        refs = types.SimpleNamespace(**refs)
        self.part, self.landing, self.summed, self.crossed = refs.part, refs.landing, refs.summed, refs.crossed
        self.sems = (refs.send_sem, refs.recv_sem)

    def push(self, source, target, slot, member):
        return send(source, target, self.sems[0].at[slot], self.sems[1].at[slot], self.place.member(member))

    def begin(self, block_of):
        place, part = self.place, self.part
        part[0] = block_of(place.far_peer).astype(BF16)
        self.first = self.push(part.at[0], self.landing.at[0], 0, place.core_peer)
        crossing = block_of(place.y_peer)
        self.first.wait_recv()
        self.summed[...] = (crossing + self.landing[0].astype(F32)).astype(BF16)
        self.across = self.push(self.summed, self.crossed, 1, place.y_peer)
        part[1] = block_of(place.core_peer).astype(BF16)
        self.second = self.push(part.at[1], self.landing.at[1], 2, place.core_peer)
        self.own = block_of(place.me)

    def total(self):
        self.second.wait_recv()
        own = self.own + self.landing[1].astype(F32)
        self.across.wait_recv()
        own = own + self.crossed[...].astype(F32)
        self.first.wait_send()
        self.second.wait_send()
        self.across.wait_send()
        return own


def scatter_scratch(length, width):
    quarter = length // 4
    return dict(
        part=pltpu.VMEM((2, quarter, width), BF16),
        landing=pltpu.VMEM((2, quarter, width), BF16),
        summed=pltpu.VMEM((quarter, width), BF16),
        crossed=pltpu.VMEM((quarter, width), BF16),
        send_sem=pltpu.SemaphoreType.DMA((3,)),
        recv_sem=pltpu.SemaphoreType.DMA((3,)),
    )


def gather_scratch():
    return dict(send_sem=pltpu.SemaphoreType.DMA((3,)), recv_sem=pltpu.SemaphoreType.DMA((3,)))


class Straight:
    def __init__(self, place, source, target, rows, sems):
        self.place, self.source, self.target, self.rows = place, source, target, rows
        self.send_sem, self.recv_sem, self.local_sem = sems

    def part_for(self, away):
        source = self.source
        if len(source.shape) == 3:
            source = source.at[lax.rem(self.place.z + away, 2)]
        return source.at[pl.ds(*self.rows)]

    def start(self):
        place, mine = self.place, self.target.at[self.place.z]
        self.own = pltpu.make_async_copy(self.part_for(0), mine, self.local_sem.at[0])
        self.own.start()
        self.copies = [
            send(self.part_for(away), mine, self.send_sem.at[away], self.recv_sem.at[away], place.beyond(away))
            for away in (2, 1, 3)
        ]

    def arrived(self):
        self.own.wait()
        for copy in self.copies:
            copy.wait_recv()

    def close(self):
        for copy in self.copies:
            copy.wait_send()


class Aside:
    def __init__(self, place, source, target, sems):
        self.place, self.source, self.target = place, source, target
        self.send_sem, self.recv_sem = sems

    def start(self):
        self.copy = send(
            self.source, self.target, self.send_sem.at[0], self.recv_sem.at[0], self.place.beside()
        )

    def arrived(self):
        self.copy.wait_recv()

    def close(self):
        self.copy.wait_send()


class AsideSum:
    def __init__(self, place, source, own, landing, summed, sems):
        self.place, self.source, self.own, self.landing, self.summed = place, source, own, landing, summed
        self.send_sem, self.recv_sem, self.local_sem = sems

    def start(self):
        place = self.place
        self.copy = send(
            self.source.at[:, 1 - place.x], self.landing, self.send_sem.at[0], self.recv_sem.at[0], place.beside()
        )
        if self.own is not None:
            self.load = pltpu.make_async_copy(self.source.at[:, place.x], self.own, self.local_sem.at[0])
            self.load.start()

    def arrived(self):
        self.copy.wait_recv()
        if self.own is not None:
            self.load.wait()
        for at in range(4):
            own = self.source[at, self.place.x] if self.own is None else self.own[at]
            self.summed[at] = (own.astype(F32) + self.landing[at].astype(F32)).astype(BF16)

    def close(self):
        self.copy.wait_send()


class StraightSum:
    def __init__(self, place, source, landing, totals, sems):
        self.place, self.source, self.landing, self.totals = place, source, landing, totals
        self.send_sem, self.recv_sem, self.local_sem = sems

    def start(self):
        place = self.place
        self.copies = [
            send(
                self.source.at[lax.rem(place.z + away, 4)],
                self.landing.at[away],
                self.send_sem.at[away],
                self.recv_sem.at[away],
                place.beyond(away),
            )
            for away in (2, 1, 3)
        ]
        self.own = pltpu.make_async_copy(self.source.at[place.z], self.landing.at[0], self.local_sem.at[0])
        self.own.start()

    def arrived(self):
        for copy in self.copies:
            copy.wait_recv()
        self.own.wait()
        blocks = [self.landing[away].astype(F32) for away in range(4)]
        if len(self.totals) == 1:
            self.totals[0][...] = (blocks[0] + blocks[2]) + (blocks[1] + blocks[3])
        else:
            self.totals[0][...] = blocks[0] + blocks[2]
            self.totals[1][...] = blocks[1] + blocks[3]

    def close(self):
        for copy in self.copies:
            copy.wait_send()


def normalise(values, gain):
    factor = lax.rsqrt(jnp.mean(values * values, axis=-1, keepdims=True) + 1e-06)
    return values * factor * gain


def normalise_back(values, gain, upstream):
    factor = lax.rsqrt(jnp.mean(values * values, axis=-1, keepdims=True) + 1e-06)
    scaled = upstream * gain
    inward = factor * scaled - values * factor * factor * factor * jnp.mean(
        scaled * values, axis=-1, keepdims=True
    )
    return inward, jnp.sum(upstream * values * factor, axis=0, keepdims=True)


def swap_halves(values):
    width = values.shape[1]
    lane = lax.broadcasted_iota(jnp.int32, values.shape, 1)
    return jnp.where(
        lax.rem(lane, HEAD) < HEAD // 2,
        pltpu.roll(values, width - HEAD // 2, 1),
        pltpu.roll(values, HEAD // 2, 1),
    )


def turn(values, cosine, sine):
    times = values.shape[1] // cosine.shape[1]
    return values * jnp.concatenate([cosine] * times, axis=1) + swap_halves(
        values
    ) * jnp.concatenate([sine] * times, axis=1)


def allowed_keys(seg_row, seg_col, offset, rows, extent):
    row_index = offset + lax.broadcasted_iota(jnp.int32, (rows, extent), 0)
    column_index = lax.broadcasted_iota(jnp.int32, (rows, extent), 1)
    return (column_index <= row_index) & (
        seg_row[:, :extent] == seg_col[offset : offset + rows, :]
    )


def softmax_rows(query, keys, allowed):
    masked = jnp.where(allowed, nt(query, keys), -1e30)
    exponent = jnp.exp(masked - jnp.max(masked, axis=-1, keepdims=True))
    return exponent * (1.0 / jnp.sum(exponent, axis=-1, keepdims=True))


def sigmoid(values):
    return 1.0 / (1.0 + jnp.exp(-values))


def attention_forward(k):
    length, wide = k.kept[V].shape
    heads = wide // HEAD
    place = k.place
    k.early(ATT)
    gather = TokenGather(place, k.kept[NRM], k.gather)
    k.kept[NRM][gather.rows(place.me), :] = normalise(k.x[...], k.gain[...]).astype(BF16)
    gather.start()
    k.at(1)
    k.weight(ATT)
    inward, outward = k.matrix(ATT, 0, 3 * wide), k.matrix(ATT, 3 * wide, 4 * wide)
    for owner in gather.arrivals():
        rows = gather.rows(owner)
        projected = nn(k.kept[NRM][rows, :], inward)
        k.kept[QK][rows, :] = turn(projected[:, : 2 * wide], k.cosine[rows, :], k.sine[rows, :]).astype(BF16)
        k.kept[V][rows, :] = projected[:, 2 * wide :].astype(BF16)
    for at in (NRM, QK, V):
        k.local.start(k.kept[at], k.kept_out[at], True)
    k.at(2)
    block = 256
    for offset in range(0, length, block):
        extent = offset + block
        allowed = allowed_keys(k.seg_row, k.seg_col, offset, block, extent)
        for head in range(heads):
            own = slice(head * HEAD, (head + 1) * HEAD)
            query = k.kept[QK][offset:extent, own] * BF16(HEAD**-0.5)
            keys = k.kept[QK][:extent, wide + head * HEAD : wide + (head + 1) * HEAD]
            probability = softmax_rows(query, keys, allowed).astype(BF16)
            k.kept[ATTENDED][offset:extent, own] = nn(probability, k.kept[V][:extent, own]).astype(BF16)
        k.at(3 + offset // block)
    k.local.start(k.kept[ATTENDED], k.kept_out[ATTENDED], True)
    scatter = TokenScatter(place, k.scatter)
    scatter.begin(lambda owner: nt(k.kept[ATTENDED][quarter_rows(length, owner), :], outward))
    k.mid[...] = k.x[...] + scatter.total()


def attention_backward(k):
    length, wide = k.kept[V].shape
    heads = wide // HEAD
    place = k.place
    k.early(ATT)
    loads = [k.local.start(k.kept_in[at], k.kept[at]) for at in (ATTENDED, QK, V, NRM)]
    gather = TokenGather(place, k.up, k.gather)
    k.up[gather.rows(place.me), :] = k.upstream[...].astype(BF16)
    gather.start()
    k.at(1)
    k.weight(ATT)
    inward, outward = k.matrix(ATT, 0, 3 * wide), k.matrix(ATT, 3 * wide, 4 * wide)
    for owner in gather.arrivals():
        rows = gather.rows(owner)
        k.outer[rows, :] = nn(k.up[rows, :], outward).astype(BF16)
    for load in loads:
        load.wait()
    k.dqk[...] = jnp.zeros_like(k.dqk)
    k.dv[...] = jnp.zeros_like(k.dv)
    block = 256
    for offset in range(0, length, block):
        k.at(2 + offset // block)
        extent = offset + block
        allowed = allowed_keys(k.seg_row, k.seg_col, offset, block, extent)
        for head in range(heads):
            own = slice(head * HEAD, (head + 1) * HEAD)
            key_columns = slice(wide + head * HEAD, wide + (head + 1) * HEAD)
            query = k.kept[QK][offset:extent, own] * BF16(HEAD**-0.5)
            keys = k.kept[QK][:extent, key_columns]
            outer = k.outer[offset:extent, own]
            probability = softmax_rows(query, keys, allowed)
            inner = nt(outer, k.kept[V][:extent, own])
            score = probability * (inner - jnp.sum(probability * inner, axis=-1, keepdims=True))
            score = score.astype(BF16)
            k.dqk[offset:extent, own] = nn(score, keys) * HEAD**-0.5
            k.dqk[:extent, key_columns] += tn(score, query)
            k.dv[:extent, own] += tn(probability.astype(BF16), outer)
    for offset in range(0, length, block):
        rows = slice(offset, offset + block)
        k.dqkv[rows, : 2 * wide] = turn(k.dqk[rows, :], k.cosine[rows, :], -k.sine[rows, :]).astype(BF16)
        k.dqkv[rows, 2 * wide :] = k.dv[rows, :].astype(BF16)
    scatter = TokenScatter(place, k.scatter)
    scatter.begin(lambda owner: nt(k.dqkv[quarter_rows(length, owner), :], inward))
    k.put(ATT, 0, tn(k.kept[NRM][...], k.dqkv[...]))
    k.put(ATT, 3 * wide, tn(k.up[...], k.kept[ATTENDED][...]))
    k.made(ATT)
    inward, k.gain_grad[...] = normalise_back(k.x[...], k.gain[...], scatter.total())
    k.grad[...] = k.upstream[...] + inward


def pick_softmax(logits, chosen, axis):
    highest = jnp.max(jnp.where(chosen > 0, logits, -1e30), axis=axis, keepdims=True)
    exponent = chosen * jnp.exp(jnp.where(chosen > 0, logits - highest, 0.0))
    return exponent / jnp.sum(exponent, axis=axis, keepdims=True)


def slots_by_token(slot_row):
    shape = (CAP, slot_row.shape[1])
    return lax.broadcasted_iota(jnp.int32, shape, 0) == slot_row


def tokens_by_slot(slot_column):
    shape = (slot_column.shape[0], CAP)
    return (lax.broadcasted_iota(jnp.int32, shape, 1) == slot_column).astype(F32).astype(BF16)


def hidden_of(inner):
    units = inner.shape[1] // 2
    gate = inner[:, :units]
    return (gate * sigmoid(gate) * inner[:, units:]).astype(BF16)


def swiglu_back(down, inner):
    units = inner.shape[1] // 2
    gate, raised = inner[:, :units], inner[:, units:]
    squashed = sigmoid(gate)
    gate_grad = down * raised * squashed * (1.0 + gate * (1.0 - squashed))
    up_grad = down * gate * squashed
    return jnp.concatenate([gate_grad.astype(BF16), up_grad.astype(BF16)], axis=1)


def expert_order(sequences, experts):
    if sequences == 1:
        return [(0, e) for e in range(experts)]
    return [(0, 0), (1, 0), (1, 1), (0, 1)]


def both_arrivals(k, buf, on_rows, between):
    place = k.place
    sequences = buf.shape[0]
    own = TokenGather(place, buf.at[0], k.gather)
    quarter = own.rows(place.me)
    own.start()
    if sequences > 1:
        crossing = send(
            buf.at[0, quarter], buf.at[1, quarter], k.pair_send.at[0], k.pair_recv.at[0], place.partner()
        )
    for owner in own.arrivals():
        on_rows(0, own.rows(owner))
    if sequences > 1:
        crossing.wait_recv()
        other = TokenGather(place, buf.at[1], k.other_gather)
        other.start()
        k.at(1)
        between()
        for owner in other.arrivals():
            on_rows(1, other.rows(owner))
        crossing.wait_send()
    else:
        between()


def give_back(k, total):
    k.pair_sum[...] = total.astype(BF16)
    return send(k.pair_sum, k.pair_land, k.pair_send.at[1], k.pair_recv.at[1], k.place.partner())


def ffn_forward(k):
    sequences, length = k.kept[MOE].shape[:2]
    experts = k.kept[ROUTED].shape[0]
    place = k.place
    moe, branch = k.kept[MOE], k.branch
    k.early(SH, *(EX + e for e in range(experts)))
    moe[0, quarter_rows(length, place.me), :] = normalise(k.mid[...], k.gain[...]).astype(BF16)
    units = k.w[SH].shape[-1] // 3
    wide = k.w[EX].shape[-1] // 3

    def on_rows(s, rows):
        k.weight(SH)
        inner = nn(moe[s, rows, :], k.matrix(SH, 0, 2 * units))
        k.kept[SHARED][s, rows, :] = inner.astype(BF16)
        branch[s, rows, :] = nt(hidden_of(inner), k.matrix(SH, 2 * units, 3 * units))
        logits = nn(moe[s, rows, :], k.router[...])
        k.gates[s, rows, :] = pick_softmax(logits, k.chosen_cols[s, rows, :], 1)

    scatters = [TokenScatter(place, refs) for refs in k.scatters]

    def dispatch(s, e):
        index = s * experts + e
        held = slots_by_token(k.slot_rows[index : index + 1, :]).astype(F32).astype(BF16)
        k.kept[ROUTED][e, s * CAP : (s + 1) * CAP, :] = nn(held, moe[s]).astype(BF16)

    def expert(s, e):
        k.weight(EX + e)
        index = s * experts + e
        slots = slice(s * CAP, (s + 1) * CAP)
        inner = nn(k.kept[ROUTED][e, slots, :], k.matrix(EX + e, 0, 2 * wide))
        k.kept[ACT][e, slots, :] = inner.astype(BF16)
        outs = nt(hidden_of(inner), k.matrix(EX + e, 2 * wide, 3 * wide)).astype(BF16)
        if e < experts - 1:
            combine = tokens_by_slot(k.slot_cols[:, index : index + 1])
            branch[s] += k.gates[s, :, e : e + 1] * nn(combine, outs)
            return

        def block_of(owner):
            rows = quarter_rows(length, owner)
            combine = tokens_by_slot(k.slot_cols[rows, index : index + 1])
            return branch[s, rows, :] + k.gates[s, rows, e : e + 1] * nn(combine, outs)

        scatters[s].begin(block_of)

    def between():
        for e in range(experts):
            dispatch(0, e)
        k.gate_rows[0] = pick_softmax(nt(k.router_t[...], moe[0]), k.chosen_rows[0], 0)

    both_arrivals(k, moe, on_rows, between)
    k.local.start(moe, k.kept_out[MOE], True)
    k.local.start(k.kept[SHARED], k.kept_out[SHARED], True)
    k.at(2)
    for step, (s, e) in enumerate(expert_order(sequences, experts)):
        if s > 0:
            dispatch(s, e)
        expert(s, e)
        k.at(3 + step)
    for s in range(1, sequences):
        k.gate_rows[s] = pick_softmax(nt(k.router_t[...], moe[s]), k.chosen_rows[s], 0)
    k.local.start(k.kept[ROUTED], k.kept_out[ROUTED], True)
    k.local.start(k.kept[ACT], k.kept_out[ACT], True)
    if sequences > 1:
        returned = give_back(k, scatters[1].total())
    following = k.mid[...] + scatters[0].total()
    if sequences > 1:
        returned.wait_recv()
        following = following + k.pair_land[...].astype(F32)
        returned.wait_send()
    k.following[...] = following


def ffn_backward(k):
    sequences, length = k.kept[MOE].shape[:2]
    experts = k.kept[ROUTED].shape[0]
    place = k.place
    moe, up, moe_grad = k.kept[MOE], k.up, k.moe_grad
    routed, act, shared = k.kept[ROUTED], k.kept[ACT], k.kept[SHARED]
    load_shared = k.local.start(k.kept_in[SHARED], shared)
    k.early(SH, *(EX + e for e in range(experts)))
    load_act = [k.local.start(k.kept_in[ACT].at[e], act.at[e]) for e in range(experts)]
    load_routed = [k.local.start(k.kept_in[ROUTED].at[e], routed.at[e]) for e in range(experts)]
    load_moe = k.local.start(k.kept_in[MOE], moe)
    up[0, quarter_rows(length, place.me), :] = k.upstream[...].astype(BF16)
    units = k.w[SH].shape[-1] // 3
    wide = k.w[EX].shape[-1] // 3
    fresh = {SH}

    def on_rows(s, rows):
        k.weight(SH)
        if SH in fresh:
            fresh.remove(SH)
            load_shared.wait()
        inner = shared[s, rows, :].astype(F32)
        k.hidden_all[s, rows, :] = hidden_of(inner)
        down = nn(up[s, rows, :], k.matrix(SH, 2 * units, 3 * units))
        inner_grad = swiglu_back(down, inner)
        shared[s, rows, :] = inner_grad
        moe_grad[s, rows, :] = nt(inner_grad, k.matrix(SH, 0, 2 * units))

    scatters = [TokenScatter(place, refs) for refs in k.scatters]
    for s in range(sequences):
        k.slot_sums[s] = jnp.zeros_like(k.slot_sums[s])
    done = [0] * experts

    def expert(s, e):
        k.weight(EX + e)
        if not done[e]:
            load_act[e].wait()
            load_routed[e].wait()
        index = s * experts + e
        slots = slice(s * CAP, (s + 1) * CAP)
        held = slots_by_token(k.slot_rows[index : index + 1, :])
        gate_slot = jnp.sum(jnp.where(held, k.gate_rows[s, e : e + 1, :], 0.0), axis=1, keepdims=True)
        arrived = nn(held.astype(F32).astype(BF16), up[s]).astype(BF16)
        k.slot_grad[slots, :] = (arrived.astype(F32) * gate_slot).astype(BF16)
        inner = act[e, slots, :].astype(F32)
        hidden = hidden_of(inner)
        k.hidden[slots, :] = hidden
        down = nn(arrived, k.matrix(EX + e, 2 * wide, 3 * wide))
        slot_dot = jnp.sum(hidden.astype(F32) * down, axis=1, keepdims=True)
        k.slot_sums[s, e : e + 1, :] = jnp.sum(jnp.where(held, slot_dot, 0.0), axis=0, keepdims=True)
        inner_grad = swiglu_back(down * gate_slot, inner)
        act[e, slots, :] = inner_grad
        back = nt(inner_grad, k.matrix(EX + e, 0, 2 * wide)).astype(BF16)
        if e < experts - 1:
            combine = tokens_by_slot(k.slot_cols[:, index : index + 1])
            moe_grad[s] += nn(combine, back)
        else:
            gates = k.gate_rows[s]
            pair = jnp.sum(gates, axis=0, keepdims=True)
            product = 0.5 * (pair * pair - jnp.sum(gates * gates, axis=0, keepdims=True))
            sums = k.slot_sums[s]
            logit_grad = k.chosen_rows[s] * product * (2.0 * sums - jnp.sum(sums, axis=0, keepdims=True))
            k.logit_grad[s] = logit_grad.astype(BF16)

            def block_of(owner):
                rows = quarter_rows(length, owner)
                combine = tokens_by_slot(k.slot_cols[rows, index : index + 1])
                turned = tn(k.logit_grad[s, :, rows], k.router_t[...])
                return moe_grad[s, rows, :] + nn(combine, back) + turned

            scatters[s].begin(block_of)
        done[e] += 1
        if done[e] == sequences:
            k.put(EX + e, 0, tn(routed[e], act[e]))
            k.put(EX + e, 2 * wide, tn(k.slot_grad[...], k.hidden[...]))
            k.made(EX + e)

    order = expert_order(sequences, experts)
    both_arrivals(k, up, on_rows, lambda: expert(*order[0]))
    load_moe.wait()
    whole = sequences * length
    k.put(SH, 0, tn(moe[...].reshape(whole, -1), shared[...].reshape(whole, -1)))
    k.put(SH, 2 * units, tn(up[...].reshape(whole, -1), k.hidden_all[...].reshape(whole, -1)))
    k.made(SH)
    k.at(2)
    for step, (s, e) in enumerate(order[1:]):
        expert(s, e)
        k.at(3 + step)
    k.router_grad[...] = sum(nn(k.logit_grad[s], moe[s]) for s in range(sequences))
    if sequences > 1:
        returned = give_back(k, scatters[1].total())
    total = scatters[0].total()
    if sequences > 1:
        returned.wait_recv()
        total = total + k.pair_land[...].astype(F32)
        returned.wait_send()
    inward, k.gain_grad[...] = normalise_back(k.mid[...], k.gain[...], total)
    k.grad[...] = k.upstream[...] + inward


def last_sums(k):
    place = k.place
    stage = k.stage
    stage[0] = k.small[...]
    partners = (place.member(place.core_peer), place.member(place.y_peer), place.beside())
    for step, partner in enumerate(partners):
        copy = send(stage.at[step], k.land.at[step], k.small_send.at[step], k.small_recv.at[step], partner)
        copy.wait_recv()
        stage[step + 1] = stage[step] + k.land[step]
        copy.wait_send()
    k.at(1)
    last = len(partners)
    copies = []
    for away in (1, 2, 3):
        copies.append(
            send(
                stage.at[last],
                k.rows_z.at[place.z],
                k.small_send.at[last + away - 1],
                k.small_recv.at[last + away - 1],
                place.beyond(away),
            )
        )
    k.rows_z[place.z] = stage[last]
    for copy in copies:
        copy.wait_recv()
    k.small_sum[...] = (k.rows_z[0] + k.rows_z[1]) + (k.rows_z[2] + k.rows_z[3])
    for copy in copies:
        copy.wait_send()


class Far:
    def __init__(self, array):
        self.array = array


class Out:
    def __init__(self, shape, kind=F32, far=False):
        self.shape, self.kind, self.far = shape, kind, far


class Store:
    def __init__(self, height, width, columns, parts, paired):
        self.height, self.width, self.columns, self.parts, self.paired = height, width, columns, parts, paired
        self.source, self.full = {}, {}
        self.z, self.x = {}, {}
        self.made, self.sums, self.totals = {}, {}, {}

    def keys(self, layer, matrix):
        return [(layer, matrix, part) for part in range(len(self.parts[matrix]))]

    def shape_of(self, matrix):
        if self.paired:
            return (4, 2, self.height, self.columns[matrix])
        return (1, 1, self.width, self.columns[matrix])


def is_leaf(value):
    return not isinstance(value, (dict, list))


def call(store, body, collective_id, ins, outs, scratch, layer, weights=(), made=(), plan=(), tokens=True):
    ins, outs, scratch = dict(ins), dict(outs), dict(scratch)
    dma, vmem = pltpu.SemaphoreType.DMA, pltpu.VMEM
    width = store.width
    starts = [(kind, key) for _, kind, key, *end in plan if not end]
    starts += [(SUM_X, (layer, matrix)) for matrix in made if (layer, matrix) in store.own_sums]
    keys = [[key for own, key in starts if own == kind] for kind in range(4)]
    keys_in = [key for matrix in weights for key in store.keys(layer, matrix)]
    ins["src"] = {key: Far(store.source[key[:2]]) for key in keys[GET_Z]}
    ins["full_in"] = {m: Far(store.full[layer, m]) for m in weights if not store.paired}
    ins["z_in"], ins["x_in"] = {}, {}
    if store.paired:
        wanted = set(keys_in) | set(keys[GET_X])
        ins["z_in"] = {key: Far(store.z[key]) for key in sorted(wanted - set(keys[GET_Z]))}
        ins["x_in"] = {key: Far(store.x[key]) for key in sorted(set(keys_in) - set(keys[GET_X]))}
    ins["made_in"] = {key: Far(store.made[key]) for key in keys[SUM_X] if key in store.made}
    ins["sums_in"] = {key: Far(store.sums[key]) for key in keys[SUM_Z] if key not in keys[SUM_X]}

    def part_shape(key):
        return (4, store.parts[key[1]][key[2]][1], store.columns[key[1]])

    def block_shape(key):
        return (4, store.height, store.columns[key[1]])

    outs["z_out"] = {key: Out(part_shape(key), BF16, True) for key in keys[GET_Z]}
    outs["x_out"] = {key: Out(part_shape(key), BF16, True) for key in keys[GET_X]}
    outs["sums_out"] = {key: Out(block_shape(key), BF16) for key in keys[SUM_X]}
    outs["totals"] = {key: [Out(block_shape(key)[1:])] * (1 if key[1] == ATT else 2) for key in keys[SUM_Z]}
    outs["made_out"] = {
        m: Out(store.shape_of(m), BF16, True) for m in made if (layer, m) not in store.own_sums
    }
    scratch["w"] = {m: vmem(store.shape_of(m), BF16) for m in weights}
    scratch["sems"] = {
        GET_Z: {key: [dma((4,)), dma((4,)), dma((1,))] for key in keys[GET_Z]},
        GET_X: {key: [dma((1,)), dma((1,))] for key in keys[GET_X]},
        SUM_X: {key: [dma((1,)), dma((1,)), dma((1,))] for key in keys[SUM_X]},
        SUM_Z: {key: [dma((4,)), dma((4,)), dma((1,))] for key in keys[SUM_Z]},
    }
    scratch["blocks"] = {key: vmem(block_shape(key), BF16) for key in keys[SUM_X]}
    scratch["own"] = {key: vmem(block_shape(key), BF16) for key in keys[SUM_X] if key in store.made}
    scratch["lands"] = {key: vmem(block_shape(key), BF16) for key in keys[SUM_Z]}
    scratch["lsem"] = dma((2 * len(keys_in) + 12,))
    trees = [jax.tree.flatten(tree, is_leaf=is_leaf) for tree in (ins, outs, scratch)]
    (ins_flat, _), (outs_flat, outs_tree), (scratch_flat, _) = trees
    around = bool(starts)

    def kernel(*refs):
        k = types.SimpleNamespace()
        at = 0
        for flat, tree in trees:
            for name, value in jax.tree.unflatten(tree, refs[at : at + len(flat)]).items():
                setattr(k, name, value)
            at += len(flat)
        place = k.place = Place()
        k.local = Local(k.lsem)
        peers = place.greet_sequence() if tokens else []
        if around:
            peers += place.greet_all()
        elif store.paired:
            peers += [place.partner()]
        place.greet(peers)

        def job(kind, key):
            sems = k.sems[kind][key]
            if kind == GET_Z:
                return Straight(place, k.src[key], k.z_out[key], store.parts[key[1]][key[2]], sems)
            if kind == GET_X:
                source = k.z_out[key] if key in k.z_out else k.z_in[key]
                return Aside(place, source, k.x_out[key], sems)
            if kind == SUM_X:
                source = k.made_in[key] if key in k.made_in else k.w[key[1]]
                return AsideSum(place, source, k.own.get(key), k.blocks[key], k.sums_out[key], sems)
            source = k.sums_out[key] if key in k.sums_out else k.sums_in[key]
            return StraightSum(place, source, k.lands[key], k.totals[key], sems)

        running, ended = {}, set()

        def start(kind, key):
            running[kind, key] = job(kind, key)
            running[kind, key].start()

        def end(kind, key):
            if (kind, key) not in ended:
                ended.add((kind, key))
                running[kind, key].arrived()

        def at_point(point):
            for own, kind, key, *is_end in plan:
                if own == point:
                    (end if is_end else start)(kind, key)

        loads, loaded = {}, set()

        def parts_of(matrix):
            return [(key, *store.parts[matrix][key[2]]) for key in store.keys(layer, matrix)]

        def load_part(key, first, rows):
            w = k.w[key[1]]
            span = pl.ds(first, rows)
            for got, landed, kind, x in (
                (k.z_in, k.z_out, GET_Z, place.x),
                (k.x_in, k.x_out, GET_X, 1 - place.x),
            ):
                if key in landed:
                    end(kind, key)
                source = landed[key] if key in landed else got[key]
                loads.setdefault(key, []).append(k.local.start(source, w.at[:, x, span]))

        def early(*matrices):
            for matrix in matrices:
                if not store.paired:
                    loads[matrix] = [k.local.start(k.full_in[matrix], k.w[matrix])]
                    continue
                for key, first, rows in parts_of(matrix):
                    if key in k.z_in and key in k.x_in:
                        load_part(key, first, rows)

        def weight(matrix):
            if matrix in loaded:
                return
            loaded.add(matrix)
            if not store.paired:
                for copy in loads[matrix]:
                    copy.wait()
                return
            for key, first, rows in parts_of(matrix):
                if key not in loads:
                    load_part(key, first, rows)
            for key, *_ in parts_of(matrix):
                for copy in loads[key]:
                    copy.wait()

        def matrix_of(matrix, first, last):
            value = k.w[matrix][:, :, :, first:last]
            return value.reshape(width, last - first)

        def put(matrix, first, value):
            ref = k.w[matrix]
            shape = (*ref.shape[:3], value.shape[1])
            ref[:, :, :, first : first + value.shape[1]] = value.astype(BF16).reshape(shape)

        def finished(matrix):
            if (layer, matrix) in k.sums_out:
                start(SUM_X, (layer, matrix))
            else:
                k.local.start(k.w[matrix], k.made_out[matrix], True)

        k.at, k.early, k.weight, k.matrix, k.put, k.made = at_point, early, weight, matrix_of, put, finished
        at_point(0)
        body(k)
        for kind, key in running:
            end(kind, key)
        for transfer in running.values():
            transfer.close()
        k.local.close()

    hbm, near = pl.BlockSpec(memory_space=pl.ANY), pl.BlockSpec(memory_space=pltpu.VMEM)
    results = pl.pallas_call(
        kernel,
        out_shape=[jax.ShapeDtypeStruct(out.shape, out.kind) for out in outs_flat],
        in_specs=[hbm if isinstance(value, Far) else near for value in ins_flat],
        out_specs=[hbm if out.far else near for out in outs_flat],
        scratch_shapes=scratch_flat,
        compiler_params=pltpu.CompilerParams(
            collective_id=collective_id, has_side_effects=True, vmem_limit_bytes=VMEM_LIMIT
        ),
    )(*[value.array if isinstance(value, Far) else value for value in ins_flat])
    result = types.SimpleNamespace(**jax.tree.unflatten(outs_tree, results))
    store.z |= result.z_out
    store.x |= result.x_out
    store.sums |= result.sums_out
    store.totals |= result.totals
    store.made |= {(layer, m): value for m, value in result.made_out.items()}
    return result


def on_device(
    ring, stream, cotangent, segments, expert_pick, slot_index, norm_gains,
    attention, projection, router, widening, narrowing, expansion, contraction,
):
    layers = attention.shape[0]
    segment = segments[0]
    length = segment.shape[0]
    all_experts = expansion.shape[1]
    width = stream.shape[1]
    quarter = stream.shape[0]
    wide = attention.shape[3]
    units = widening.shape[3]
    height = attention.shape[2]
    paired = ring == 8
    sequences = 2 if paired else 1
    experts = all_experts // sequences
    shared_units = units // sequences
    dp = lax.axis_index("dp")
    upper = (dp // 2) % 2 == 1

    halfway = HEAD // 2
    inverse = jnp.exp(jnp.arange(halfway, dtype=F32) * (-2.0 * math.log(10000.0) / HEAD))
    phases = jnp.arange(length, dtype=F32)[:, None] * inverse[None, :]
    cosine, sine = jnp.cos(phases), jnp.sin(phases)
    cosine = jnp.concatenate([cosine] * 4, axis=1)
    sine = jnp.concatenate([-sine, sine] * 2, axis=1)
    places = dict(cosine=cosine, sine=sine, seg_row=segment[None, :], seg_col=segment[:, None])

    def local_first(values, axis):
        if not paired:
            return values
        return jnp.where(upper, jnp.roll(values, -experts, axis), values)

    def known_first(values, axis):
        if not paired:
            return values
        return jnp.where(upper, jnp.roll(values, experts, axis), values)

    picks = jnp.concatenate([expert_pick, slot_index], axis=2)[:, None]
    if paired:
        swap = [(at, (at // 4) * 4 + (at % 4 + 2) % 4) for at in range(ring)]
        picks = jnp.concatenate([picks, lax.ppermute(picks, "dp", swap)], axis=1)
    expert_of, slot_of = picks[..., :2], picks[..., 2:]
    held = expert_of[..., None] == jnp.arange(all_experts, dtype=jnp.int32)
    slots = local_first(jnp.sum(jnp.where(held, slot_of[..., None] + 1, 0), axis=3) - 1, 3)
    chosen = local_first(jnp.any(held, axis=3).astype(F32), 3)
    slots = slots[..., :experts]
    slot_rows = jnp.swapaxes(slots, 2, 3).reshape(layers, sequences * experts, length)
    slot_cols = jnp.swapaxes(slots, 1, 2).reshape(layers, length, sequences * experts)
    chosen_cols = jnp.pad(chosen, ((0, 0), (0, 0), (0, 0), (0, LANES - all_experts)))
    chosen_rows = jnp.pad(jnp.swapaxes(chosen, 2, 3), ((0, 0), (0, 0), (0, 8 - all_experts), (0, 0)))
    router_own = local_first(router, 2)
    router_wide = jnp.pad(router_own, ((0, 0), (0, 0), (0, LANES - all_experts)))
    router_t = jnp.pad(jnp.swapaxes(router_own, 1, 2), ((0, 0), (0, 8 - all_experts), (0, 0)))

    projection_t = jnp.swapaxes(projection, 1, 2)
    narrowing_t = jnp.swapaxes(narrowing, 1, 2)
    contraction_t = jnp.swapaxes(contraction, 2, 3)
    columns = {ATT: 4 * wide, SH: 3 * shared_units} | {EX + e: 3 * units for e in range(experts)}
    parts = {matrix: [(0, height)] for matrix in columns}
    if paired:
        parts[EX + 1] = [(0, height // 3), (height // 3, height - height // 3)]
    store = Store(height, width, columns, parts, paired)
    for layer in range(layers):
        store.source[layer, ATT] = jnp.concatenate([*attention[layer], projection_t[layer]], axis=-1)
        thirds = (widening[layer, 0], widening[layer, 1], narrowing_t[layer])
        whole = [
            jnp.concatenate([expansion[layer, e, 0], expansion[layer, e, 1], contraction_t[layer, e]], axis=-1)
            for e in range(all_experts)
        ]
        if paired:
            store.source[layer, SH] = jnp.stack(
                [
                    jnp.concatenate([third[:, a * shared_units : (a + 1) * shared_units] for third in thirds], axis=-1)
                    for a in range(2)
                ]
            )
            for e in range(experts):
                store.source[layer, EX + e] = jnp.stack([whole[e], whole[experts + e]])
        else:
            store.source[layer, SH] = jnp.concatenate(thirds, axis=-1)
            for e in range(experts):
                store.source[layer, EX + e] = whole[e]
    if not paired:
        store.full = {
            key: lax.all_gather(source, "dp", axis=0, tiled=True)[None, None] for key, source in store.source.items()
        }

    vmem = pltpu.VMEM
    token_scatter = scatter_scratch(length, width)
    pair_scratch = dict(scatters=[token_scatter] * sequences)
    if paired:
        pair_scratch |= dict(
            other_gather=gather_scratch(),
            pair_send=pltpu.SemaphoreType.DMA((2,)),
            pair_recv=pltpu.SemaphoreType.DMA((2,)),
            pair_sum=vmem((quarter, width), BF16),
            pair_land=vmem((quarter, width), BF16),
        )
    attention_shapes = {
        NRM: (length, width), QK: (length, 2 * wide), V: (length, wide), ATTENDED: (length, wide)
    }
    ffn_shapes = {
        MOE: (sequences, length, width),
        SHARED: (sequences, length, 2 * shared_units),
        ROUTED: (experts, sequences * CAP, width),
        ACT: (experts, sequences * CAP, 2 * units),
    }
    ffn_matrices = [SH, *(EX + e for e in range(experts))]
    rows_out = Out((quarter, width))
    gain_out = Out((1, width))
    last = layers - 1

    def kept_scratch(shapes):
        return {name: vmem(shape, BF16) for name, shape in shapes.items()}

    def kept_outs(shapes):
        return {name: Out(shape, BF16, True) for name, shape in shapes.items()}

    def kept_ins(arrays):
        return {name: Far(array) for name, array in arrays.items()}

    store.own_sums = {(layer, matrix) for layer in range(layers) for matrix in (SH, EX)} if paired else set()
    saved = []
    current = stream
    next_id = 0
    for layer in range(layers):
        first, second = (layer, EX + 1, 0), (layer, EX + 1, 1)
        att, sh, ex = (layer, ATT, 0), (layer, SH, 0), (layer, EX, 0)
        if layer == 0:
            plan = [
                (0, GET_Z, att), (1, GET_Z, att, True), (1, GET_X, att), (1, GET_Z, sh), (2, GET_Z, ex),
                (3, GET_Z, first), (4, GET_Z, sh, True), (4, GET_X, sh),
            ]
        else:
            plan = [(0, GET_X, sh), (0, GET_Z, ex), (2, GET_Z, first)]
        result = call(
            store,
            attention_forward,
            next_id,
            dict(x=current, gain=norm_gains[layer, 0][None], **places),
            dict(mid=rows_out, kept_out=kept_outs(attention_shapes)),
            dict(kept=kept_scratch(attention_shapes), gather=gather_scratch(), scatter=token_scatter),
            layer,
            [ATT],
            plan=plan if paired else (),
        )
        mid, attention_kept = result.mid, result.kept_out
        plan = [
            (0, GET_X, ex), (0, GET_X, first), (1, GET_Z, second), (3, GET_Z, second, True), (3, GET_X, second)
        ]
        if layer < last:
            att, sh = (layer + 1, ATT, 0), (layer + 1, SH, 0)
            plan += [(1, GET_Z, att), (1, GET_Z, sh), (5, GET_Z, att, True), (5, GET_X, att)]
        result = call(
            store,
            ffn_forward,
            next_id + 1,
            dict(
                mid=mid,
                gain=norm_gains[layer, 1][None],
                router=router_wide[layer],
                router_t=router_t[layer],
                slot_rows=slot_rows[layer],
                slot_cols=slot_cols[layer],
                chosen_rows=chosen_rows[layer],
                chosen_cols=chosen_cols[layer],
            ),
            dict(following=rows_out, gate_rows=Out((sequences, 8, length)), kept_out=kept_outs(ffn_shapes)),
            dict(
                kept=kept_scratch(ffn_shapes),
                branch=vmem((sequences, length, width), F32),
                gates=vmem((sequences, length, LANES), F32),
                gather=gather_scratch(),
                **pair_scratch,
            ),
            layer,
            ffn_matrices,
            plan=plan if paired else (),
        )
        saved.append((current, mid, attention_kept, result.gate_rows, result.kept_out))
        current = result.following
        next_id += 2

    upstream = cotangent
    gain_parts, router_parts = [None] * layers, [None] * layers
    for layer in reversed(range(layers)):
        x_in, mid, attention_kept, gate_rows, ffn_kept = saved[layer]
        plan = []
        if layer < last:
            above = (layer + 1, ATT)
            plan = [(0, SUM_X, above), (1, SUM_Z, (layer + 1, EX + 1)), (2, SUM_X, above, True), (2, SUM_Z, above)]
        result = call(
            store,
            ffn_backward,
            next_id,
            dict(
                upstream=upstream,
                mid=mid,
                gain=norm_gains[layer, 1][None],
                router_t=router_t[layer],
                slot_rows=slot_rows[layer],
                slot_cols=slot_cols[layer],
                chosen_rows=chosen_rows[layer],
                gate_rows=gate_rows,
                kept_in=kept_ins(ffn_kept),
            ),
            dict(grad=rows_out, gain_grad=gain_out, router_grad=Out((8, width))),
            dict(
                kept=kept_scratch(ffn_shapes),
                hidden_all=vmem((sequences, length, shared_units), BF16),
                hidden=vmem((sequences * CAP, units), BF16),
                slot_grad=vmem((sequences * CAP, width), BF16),
                moe_grad=vmem((sequences, length, width), F32),
                slot_sums=vmem((sequences, 8, length), F32),
                logit_grad=vmem((sequences, 8, length), BF16),
                up=vmem((sequences, length, width), BF16),
                gather=gather_scratch(),
                **pair_scratch,
            ),
            layer,
            ffn_matrices,
            ffn_matrices,
            plan=plan if paired else (),
        )
        mid_grad, gain_two, router_parts[layer] = result.grad, result.gain_grad, result.router_grad
        plan = [(0, SUM_Z, (layer, SH)), (0, SUM_X, (layer, EX + 1)), (1, SUM_Z, (layer, EX))]
        result = call(
            store,
            attention_backward,
            next_id + 1,
            dict(
                upstream=mid_grad, x=x_in, gain=norm_gains[layer, 0][None], kept_in=kept_ins(attention_kept), **places
            ),
            dict(grad=rows_out, gain_grad=gain_out),
            dict(
                kept=kept_scratch(attention_shapes),
                outer=vmem((length, wide), BF16),
                dqk=vmem((length, 2 * wide), F32),
                dv=vmem((length, wide), F32),
                dqkv=vmem((length, 3 * wide), BF16),
                up=vmem((length, width), BF16),
                gather=gather_scratch(),
                scatter=token_scatter,
            ),
            layer,
            [ATT],
            [ATT],
            plan=plan if paired else (),
        )
        upstream = result.grad
        gain_parts[layer] = jnp.concatenate([result.gain_grad, gain_two], axis=0)
        next_id += 2

    router_parts = [known_first(part[:all_experts], 0) for part in router_parts]
    small = jnp.concatenate(gain_parts + router_parts, axis=0)
    if paired:
        count = small.shape[0]
        padded = -(-count // 8) * 8
        small = jnp.pad(small, ((0, padded - count), (0, 0)))
        small = call(
            store,
            last_sums,
            next_id,
            dict(small=small),
            dict(small_sum=Out((padded, width))),
            dict(
                stage=vmem((4, padded, width), F32),
                land=vmem((3, padded, width), F32),
                rows_z=vmem((4, padded, width), F32),
                small_send=pltpu.SemaphoreType.DMA((6,)),
                small_recv=pltpu.SemaphoreType.DMA((6,)),
            ),
            0,
            plan=[(0, SUM_Z, (0, EX + 1)), (0, SUM_X, (0, ATT)), (1, SUM_X, (0, ATT), True), (1, SUM_Z, (0, ATT))],
        ).small_sum
    else:
        small = lax.psum(small, ("dp", "tensor"))
        store.totals = {
            key: [lax.psum_scatter(part[0, 0], "dp", scatter_dimension=0, tiled=True).astype(F32)]
            for key, part in store.made.items()
        }
    gains_grad = small[: 2 * layers].reshape(layers, 2, width)
    router_grad = small[2 * layers : 2 * layers + layers * all_experts].reshape(layers, all_experts, width)

    def split(pieces):
        mine, theirs = pieces
        return jnp.where(upper, theirs, mine), jnp.where(upper, mine, theirs)

    attention_grad, projection_grad, widening_grad, narrowing_grad, expansion_grad, contraction_grad = (
        [] for _ in range(6)
    )
    for layer in range(layers):
        (whole,) = store.totals[layer, ATT]
        attention_grad.append(jnp.stack([whole[:, n * wide : (n + 1) * wide] for n in range(3)]))
        projection_grad.append(whole[:, 3 * wide :].T)
        if paired:
            halves = split(store.totals[layer, SH])
            shared = [
                jnp.concatenate([half[:, n * shared_units : (n + 1) * shared_units] for half in halves], axis=1)
                for n in range(3)
            ]
            by_expert = [split(store.totals[layer, EX + e]) for e in range(experts)]
            wholes = [by_expert[e][a] for a in range(2) for e in range(experts)]
        else:
            (whole,) = store.totals[layer, SH]
            shared = [whole[:, n * units : (n + 1) * units] for n in range(3)]
            wholes = [store.totals[layer, EX + e][0] for e in range(experts)]
        widening_grad.append(jnp.stack(shared[:2]))
        narrowing_grad.append(shared[2].T)
        expansion_grad.append(
            jnp.stack([jnp.stack([one[:, :units], one[:, units : 2 * units]]) for one in wholes])
        )
        contraction_grad.append(jnp.stack([one[:, 2 * units :].T for one in wholes]))
    return (
        current,
        upstream,
        gains_grad,
        jnp.stack(attention_grad),
        jnp.stack(projection_grad),
        jnp.swapaxes(router_grad, 1, 2),
        jnp.stack(widening_grad),
        jnp.stack(narrowing_grad),
        jnp.stack(expansion_grad),
        jnp.stack(contraction_grad),
    )


def solution(mesh):
    placed = (
        P(("dp", "tensor"), None),
        P(("dp", "tensor"), None),
        P("dp", None),
        P(None, "dp", None),
        P(None, "dp", None),
        P(),
        P(None, None, "dp", "tensor"),
        P(None, "tensor", "dp"),
        P(),
        P(None, None, "dp", "tensor"),
        P(None, "tensor", "dp"),
        P(None, None, None, "dp", "tensor"),
        P(None, None, "tensor", "dp"),
    )
    return jax.shard_map(
        functools.partial(on_device, mesh.shape["dp"]),
        mesh=mesh,
        in_specs=placed,
        out_specs=(
            P(("dp", "tensor"), None),
            P(("dp", "tensor"), None),
            P(),
            P(None, None, "dp", "tensor"),
            P(None, "tensor", "dp"),
            P(),
            P(None, None, "dp", "tensor"),
            P(None, "tensor", "dp"),
            P(None, None, None, "dp", "tensor"),
            P(None, None, "tensor", "dp"),
        ),
        check_vma=False,
    )
```

time: 1240 us -> 638 us (0.51)
  waiting for transfers between devices: 774 us -> 0.01 us
  Pallas kernels: 370 us -> 575 us
  blocking collectives: 39.8 us -> 0 us
  between operations: 15 us -> 1.76 us
    reduce_scatter x4 -> x0, waiting for transfers between devices: 481 us -> none  [the longest x2 395 us: on_device(): lax.psum_scatter(ffn_part, 'dp', scatter_dimension=1, tiled=True)]
    all_gather x4 -> x0, waiting for transfers between devices: 289 us -> none  [the longest x2 263 us: on_device(): ffn_full.append(lax.all_gather(ffn_shards[layer], 'dp', axis=1, tiled=True))]
    pallas_call x8 -> x9, Pallas kernels: 370 us -> 575 us  [call(): pl.pallas_call(kernel, out_shape=[jax.ShapeDtypeStruct(out.shape, out.kin...]
    psum x1 -> x0, blocking collectives: 39.8 us -> none  [on_device(): lax.psum((jnp.stack(gain_parts), jnp.stack(router_parts)), ('dp', 'tensor'))]
  transfers between devices with their start and end apart: 8 -> 1, of which waited for: 7 -> 0; matrix products, arithmetic and copies ran while one was open for 2% -> 3% of each run, Pallas kernels for 9% -> 11%
where the time goes in v2:
time: 638 us; the launch traced here: 628 us
  Pallas kernels  575 us (90%)
  local copies, waits for them, and re-layouts  28.3 us (4%)
  other arithmetic  20.2 us (3%)
    pallas_call x9, Pallas kernels, call(): pl.pallas_call(kernel, out_shape=[jax.ShapeDtypeStruct(out.shape, out.kin...  575 us
  transfers between devices with their start and end apart: 1, of which 0 were waited for; matrix products, arithmetic and copies ran while one was open for 3% of the time, Pallas kernels for 11%

profile of v2, /device:TPU:0, one launch (start us, length us, event | category | flops | bytes accessed | tf_op | source)
XLA Modules:
  0.0 628.2 jit_solution(9480842035313906511)
XLA Ops:
  0.7 0.8 add_bitcast_fusion
  1.5 3.1 collective-permute-start
  4.6 1.4 slice_bitcast_fusion.70
  5.9 0.8 fusion.33
  6.7 1.0 copy.51
  7.8 1.0 slice_bitcast_fusion.24
  8.8 1.0 slice_bitcast_fusion.66
  10.1 2.0 fusion.4
  12.0 1.3 pad_maximum_fusion.8.refs_0_
  13.5 0.7 pad_maximum_fusion.11.refs_6_
  14.3 0.7 pad_maximum_fusion.12.refs_10_
  15.0 1.2 pad_maximum_fusion.9.refs_4_.refs_9_
  16.3 0.9 pad_maximum_fusion.5.refs_7_
  17.2 0.9 pad_maximum_fusion.4.refs_6_.refs_8_
  18.2 0.9 pad_maximum_fusion.3.refs_5_
  19.1 0.9 pad_maximum_fusion.6.refs_8_
  20.0 0.7 pad_maximum_fusion.15.refs_9_
  20.7 0.8 pad_maximum_fusion.14.refs_5_
  21.5 0.6 fusion.14
  22.1 0.8 copy.59.refs_4_
  22.9 0.8 copy.55.refs_4_
  23.7 1.0 copy.57.refs_2_.refs_7_
  24.7 70.6 %shard_map.204 = (bf16[1024,768]{1,0:T(8,128)(2,1)}, bf16[1024,384]{1,0:T(8,128)(2,1)}, bf16[1024,192]{1,0:T(8,128)(2,1)}, bf16[1024,192]{1,0:T(8,128)(2,1)}, f3...) custom-call(f32[1024,128]{1,0:T(8,128)} %pad_maximum_fusion.8.refs_0, ...), custom_call_target="tpu_custom_call" | custom-call | tf_op jit(solution)/shard_map/pallas_call | solution.py:893
  95.6 0.6 squeeze.185.refs_7_.refs_10_
  96.3 0.6 squeeze.177.refs_7_.refs_11_
  97.0 0.2 fusion.1
  97.3 0.6 fusion.9
  97.9 1.0 copy.56.refs_6_.refs_10_
  99.0 1.0 copy.60.refs_6_.refs_9_
  100.0 1.3 copy.54.refs_0_
  101.3 1.3 copy.58.refs_0_
  102.6 97.3 %shard_map.205 = (f32[256,768]{1,0:T(8,128)}, f32[2,8,1024]{2,1,0:T(8,128)}, bf16[2,1024,768]{2,1,0:T(8,128)(2,1)}, bf16[2,1024,512]{2,1,0:T(8,128)(2,1)}, bf16[...) custom-call(f32[2,1024,128]{2,1,0:T(8,128)} %copy.54.refs_0_, ...), custom_call_target="tpu_custom_call" | custom-call | tf_op jit(solution)/shard_map/pallas_call | solution.py:893
  199.9 39.4 %shard_map.206 = (bf16[1024,768]{1,0:T(8,128)(2,1)}, bf16[1024,384]{1,0:T(8,128)(2,1)}, bf16[1024,192]{1,0:T(8,128)(2,1)}, bf16[1024,192]{1,0:T(8,128)(2,1)}, f3...) custom-call(f32[1024,128]{1,0:T(8,128)} %pad_maximum_fusion.8.refs_0, ...), custom_call_target="tpu_custom_call" | custom-call | tf_op jit(solution)/shard_map/pallas_call | solution.py:893
  239.3 83.1 %shard_map.207 = (f32[256,768]{1,0:T(8,128)}, f32[2,8,1024]{2,1,0:T(8,128)}, bf16[2,1024,768]{2,1,0:T(8,128)(2,1)}, bf16[2,1024,512]{2,1,0:T(8,128)(2,1)}, bf16[...) custom-call(f32[2,1024,128]{2,1,0:T(8,128)} %copy.58.refs_0_, ...), custom_call_target="tpu_custom_call" | custom-call | tf_op jit(solution)/shard_map/pallas_call | solution.py:893
  322.4 73.4 %shard_map.208 = (f32[1,768]{1,0:T(1,128)}, f32[256,768]{1,0:T(8,128)}, bf16[4,2,96,1536]{3,2,1,0:T(8,128)(2,1)}, f32[8,768]{1,0:T(8,128)}, bf16[4,96,768]{2,1,0:T(8,128)(2,1)}, /*index=5*/bf16[4,96,1536]{2,1,0:T(8,128)(2,1)}) custom-call(f32[2,8,1024]{2,1,0:T(8,128)} %get-tuple-element.307.refs_1_.refs_0_, f32[1,768]{1,0:T(1,128)} %get-tuple-element.328.refs_2_.refs_1_, ...), custom_call_target="tpu_custom_call" | custom-call | tf_op jit(solution)/shard_map/pallas_call | solution.py:893
  395.8 44.3 %shard_map.209 = (f32[1,768]{1,0:T(1,128)}, f32[256,768]{1,0:T(8,128)}, bf16[4,2,96,768]{3,2,1,0:T(8,128)(2,1)}, bf16[4,96,1536]{2,1,0:T(8,128)(2,1)}, f32[96,76...) custom-call(f32[1024,128]{1,0:T(8,128)} %pad_maximum_fusion.8.refs_0_, ...), custom_call_target="tpu_custom_call" | custom-call | tf_op jit(solution)/shard_map/pallas_call | solution.py:893
  440.1 74.5 %shard_map.210 = (f32[1,768]{1,0:T(1,128)}, f32[256,768]{1,0:T(8,128)}, bf16[4,2,96,1536]{3,2,1,0:T(8,128)(2,1)}, f32[8,768]{1,0:T(8,128)}, bf16[4,96,768]{2,1,0...) custom-call(f32[2,8,1024]{2,1,0:T(8,128)} %get-tuple-element.306.ref, ...), custom_call_target="tpu_custom_call" | custom-call | tf_op jit(solution)/shard_map/pallas_call | solution.py:893
  514.6 0.8 fusion.32
  515.4 0.8 maximum_select_fusion.2
  516.2 43.9 %shard_map.211 = (f32[1,768]{1,0:T(1,128)}, f32[256,768]{1,0:T(8,128)}, bf16[4,2,96,768]{3,2,1,0:T(8,128)(2,1)}, bf16[4,96,1536]{2,1,0:T(8,128)(2,1)}, f32[96,76...) custom-call(f32[1024,128]{1,0:T(8,128)} %pad_maximum_fusion.8.refs_0_, ...), custom_call_target="tpu_custom_call" | custom-call | tf_op jit(solution)/shard_map/pallas_call | solution.py:893
  560.1 0.7 concatenate.117
  560.8 0.6 pad.24.refs_1_
  561.4 48.4 %shard_map.212 = (f32[16,768]{1,0:T(8,128)}, bf16[4,96,768]{2,1,0:T(8,128)(2,1)}, f32[96,768]{1,0:T(8,128)}, f32[96,1536]{1,0:T(8,128)}, f32[96,1536]{1,0:T(8,128)}) custom-call(bf16[4,2,96,768]{3,2,1,0:T(8,128)(2,1)} %get-tuple-element.141.refs_0_, f32[16,768]{1,0:T(8,128)} %pad.24.refs_1_, bf16[4,96,1536]{2,1,0:T(8,128)(2,1)} %get-tuple-element.148.refs_2_), custom_call_target="tpu_custom_call" | custom-call | tf_op jit(solution)/shard_map/pallas_call | solution.py:893
  609.9 0.8 slice.480
  610.7 0.8 slice.489
  611.5 0.6 reshape.57
  612.2 0.6 reshape.56
  612.8 1.2 slice_bitcast_fusion.35
  614.1 0.8 copy.65
  615.2 0.9 copy-done.8
  616.3 0.2 copy-done.10
  616.5 0.2 copy-done.11
  616.7 0.2 broadcast_select_fusion.6
  616.9 0.8 copy-done.6
  617.9 0.2 copy-done.4
  618.3 0.2 broadcast_select_fusion.2
  618.9 0.9 pad_maximum_fusion.7
  619.9 0.8 pad_maximum_fusion.10
  620.7 0.9 pad_maximum_fusion.2
  622.0 1.3 pad_maximum_fusion.1
  623.7 2.0 pad_maximum_fusion
  625.7 0.9 copy.74
  626.5 0.5 copy-done.3
  627.1 0.9 copy.75
  (119 shorter events, 3.0 us)
Async XLA Ops:
  0.6 9.1 %copy-start.13 = (bf16[2,2,96,512]{3,2,1,0:T(8,128)(2,1)S(1)}, bf16[2,2,96,512]{3,2,1,0:T(8,128)(2,1)}, u32[]{:S(2)}) copy-start(bf16[2,2,96,512]{3,2,1,0:T(8,128)(2,1)} %param.22) | copy-start | bytes 1179652
  1.5 93.9 %collective-permute-start = (s32[2,1,1024,4]{2,3,0,1:T(4,128)S(1)}, s32[2,1,1024,4]{2,3,0,1:T(4,128)S(1)}, u32[]{:S(2)}, u32[]{:S(2)}) collective-permute-start(s32[2,1,1024,4]{2,3,0,1:T(4,128)S(1)} %add_bitcast_fusion), channel_id=1, source_target_pairs={{0,8},{4,12},{8,0},{12,4},{16,24},{20,28},{24,16},{28,20},{1,9},{5... | collective-permute-start | bytes 98312 | tf_op jit(solution)/shard_map/ppermute | solution.py:953
  7.7 2.2 copy-start.19
  8.7 1.3 copy-start.1
  10.0 3.3 copy-start
  19.1 4.7 copy-start.18
  440.1 75.3 %copy-start.20 = (f32[8,768]{1,0:T(8,128)S(1)}, f32[8,768]{1,0:T(8,128)}, u32[]{:S(2)}) copy-start(f32[8,768]{1,0:T(8,128)} %get-tuple-element.147) | copy-start | bytes 73732
  516.2 43.9 %copy-start.21 = (f32[1,768]{1,0:T(1,128)S(1)}, f32[1,768]{1,0:T(1,128)}, u32[]{:S(2)}) copy-start(f32[1,768]{1,0:T(1,128)} %get-tuple-element.145) | copy-start | bytes 9220
  516.2 43.9 %copy-start.22 = (f32[1,768]{1,0:T(1,128)S(1)}, f32[1,768]{1,0:T(1,128)}, u32[]{:S(2)}) copy-start(f32[1,768]{1,0:T(1,128)} %get-tuple-element.144) | copy-start | bytes 9220
  516.2 43.9 %copy-start.23 = (f32[1,768]{1,0:T(1,128)S(1)}, f32[1,768]{1,0:T(1,128)}, u32[]{:S(2)}) copy-start(f32[1,768]{1,0:T(1,128)} %get-tuple-element.143) | copy-start | bytes 9220
  561.4 52.5 %copy-start.12 = (f32[96,768]{1,0:T(8,128)S(1)}, f32[96,768]{1,0:T(8,128)}, u32[]{:S(2)}) copy-start(f32[96,768]{1,0:T(8,128)} %get-tuple-element.151) | copy-start | bytes 884740
  609.9 5.1 copy-start.14
  609.9 5.0 copy-start.15
  609.9 5.0 copy-start.16
  609.9 5.0 copy-start.17
  615.0 1.1 copy-start.8
  615.1 1.2 copy-start.9
  615.1 1.4 copy-start.10
  615.1 1.6 copy-start.11
  616.6 1.1 copy-start.6
  616.7 1.2 copy-start.7
  616.9 1.2 copy-start.4
  616.9 1.4 copy-start.5
  623.7 2.0 copy-start.2
  625.7 1.4 copy-start.3

commit v3 on v2

--- a/solution.py
+++ b/solution.py
@@ -14,11 +14,10 @@
 LANES = 128
 BF16 = jnp.bfloat16
 F32 = jnp.float32
-ATT, SH, EX = range(3)
-NRM, QK, V, ATTENDED = range(4)
-MOE, SHARED, ROUTED, ACT = range(4)
+QKV, PRJ, SH, EX = range(4)
+NRM, TURNED, MOE, SHARED, ROUTED, ACT = range(6)
 GET_Z, GET_X, SUM_X, SUM_Z = range(4)
-VMEM_LIMIT = 60 * 1024 * 1024
+VMEM_LIMIT = 63 * 1024 * 1024
 
 
 def nn(left, right):
@@ -237,8 +236,8 @@
 
 
 class AsideSum:
-    def __init__(self, place, source, own, landing, summed, sems):
-        self.place, self.source, self.own, self.landing, self.summed = place, source, own, landing, summed
+    def __init__(self, place, source, own, landing, out, sems):
+        self.place, self.source, self.own, self.landing, self.out = place, source, own, landing, out
         self.send_sem, self.recv_sem, self.local_sem = sems
 
     def start(self):
@@ -256,10 +255,15 @@
             self.load.wait()
         for at in range(4):
             own = self.source[at, self.place.x] if self.own is None else self.own[at]
-            self.summed[at] = (own.astype(F32) + self.landing[at].astype(F32)).astype(BF16)
+            self.landing[at] = (own.astype(F32) + self.landing[at].astype(F32)).astype(BF16)
+        if self.out is not None:
+            self.store = pltpu.make_async_copy(self.landing, self.out, self.local_sem.at[1])
+            self.store.start()
 
     def close(self):
         self.copy.wait_send()
+        if self.out is not None:
+            self.store.wait()
 
 
 class StraightSum:
@@ -288,10 +292,10 @@
         self.own.wait()
         blocks = [self.landing[away].astype(F32) for away in range(4)]
         if len(self.totals) == 1:
-            self.totals[0][...] = (blocks[0] + blocks[2]) + (blocks[1] + blocks[3])
+            self.totals[0][...] = ((blocks[0] + blocks[2]) + (blocks[1] + blocks[3])).astype(BF16)
         else:
-            self.totals[0][...] = blocks[0] + blocks[2]
-            self.totals[1][...] = blocks[1] + blocks[3]
+            self.totals[0][...] = (blocks[0] + blocks[2]).astype(BF16)
+            self.totals[1][...] = (blocks[1] + blocks[3]).astype(BF16)
 
     def close(self):
         for copy in self.copies:
@@ -348,89 +352,102 @@
 
 
 def attention_forward(k):
-    length, wide = k.kept[V].shape
+    length = k.kept[TURNED].shape[0]
+    wide = k.kept[TURNED].shape[1] // 4
     heads = wide // HEAD
     place = k.place
-    k.early(ATT)
-    gather = TokenGather(place, k.kept[NRM], k.gather)
-    k.kept[NRM][gather.rows(place.me), :] = normalise(k.x[...], k.gain[...]).astype(BF16)
+    normed, turned = k.kept[NRM], k.kept[TURNED]
+    k.early(QKV, PRJ)
+    gather = TokenGather(place, normed, k.gather)
+    normed[gather.rows(place.me), :] = normalise(k.x[...], k.gains[0:1, :]).astype(BF16)
     gather.start()
     k.at(1)
-    k.weight(ATT)
-    inward, outward = k.matrix(ATT, 0, 3 * wide), k.matrix(ATT, 3 * wide, 4 * wide)
+    k.weight(QKV)
     for owner in gather.arrivals():
         rows = gather.rows(owner)
-        projected = nn(k.kept[NRM][rows, :], inward)
-        k.kept[QK][rows, :] = turn(projected[:, : 2 * wide], k.cosine[rows, :], k.sine[rows, :]).astype(BF16)
-        k.kept[V][rows, :] = projected[:, 2 * wide :].astype(BF16)
-    for at in (NRM, QK, V):
-        k.local.start(k.kept[at], k.kept_out[at], True)
+        projected = nn(normed[rows, :], k.matrix(QKV, 0, 3 * wide))
+        turned[rows, : 2 * wide] = turn(projected[:, : 2 * wide], k.cosine[rows, :], k.sine[rows, :]).astype(BF16)
+        turned[rows, 2 * wide : 3 * wide] = projected[:, 2 * wide :].astype(BF16)
+    k.local.start(normed, k.kept_out[NRM], True)
     k.at(2)
-    block = 256
+    block = 128
     for offset in range(0, length, block):
         extent = offset + block
         allowed = allowed_keys(k.seg_row, k.seg_col, offset, block, extent)
         for head in range(heads):
-            own = slice(head * HEAD, (head + 1) * HEAD)
-            query = k.kept[QK][offset:extent, own] * BF16(HEAD**-0.5)
-            keys = k.kept[QK][:extent, wide + head * HEAD : wide + (head + 1) * HEAD]
+            first = head * HEAD
+            query = turned[offset:extent, first : first + HEAD] * BF16(HEAD**-0.5)
+            keys = turned[:extent, wide + first : wide + first + HEAD]
+            values = turned[:extent, 2 * wide + first : 2 * wide + first + HEAD]
             probability = softmax_rows(query, keys, allowed).astype(BF16)
-            k.kept[ATTENDED][offset:extent, own] = nn(probability, k.kept[V][:extent, own]).astype(BF16)
-        k.at(3 + offset // block)
-    k.local.start(k.kept[ATTENDED], k.kept_out[ATTENDED], True)
+            turned[offset:extent, 3 * wide + first : 3 * wide + first + HEAD] = nn(probability, values).astype(BF16)
+        if extent % 256 == 0:
+            k.at(2 + extent // 256)
+    k.local.start(turned, k.kept_out[TURNED], True)
     scatter = TokenScatter(place, k.scatter)
-    scatter.begin(lambda owner: nt(k.kept[ATTENDED][quarter_rows(length, owner), :], outward))
+    k.weight(PRJ)
+    scatter.begin(lambda owner: nt(turned[quarter_rows(length, owner), 3 * wide :], k.matrix(PRJ, 0, wide)))
+    k.at(7)
     k.mid[...] = k.x[...] + scatter.total()
 
 
 def attention_backward(k):
-    length, wide = k.kept[V].shape
+    sequences, length, width = k.up.shape
+    wide = width // 4
     heads = wide // HEAD
     place = k.place
-    k.early(ATT)
-    loads = [k.local.start(k.kept_in[at], k.kept[at]) for at in (ATTENDED, QK, V, NRM)]
-    gather = TokenGather(place, k.up, k.gather)
-    k.up[gather.rows(place.me), :] = k.upstream[...].astype(BF16)
+    up, normed = k.up.at[0], k.kept[MOE].at[0]
+    turned, grads = (k.kept[MOE].at[1], k.up.at[1]) if sequences > 1 else (k.spare.at[0], k.spare.at[1])
+    sums = k.moe_grad.at[0]
+    load_turned = k.local.start(k.kept_in[TURNED], turned)
+    load_normed = k.local.start(k.kept_in[NRM], normed)
+    gather = TokenGather(place, up, k.own_gather)
+    up[gather.rows(place.me), :] = k.grad[...].astype(BF16)
+    load_rows = k.local.start(k.x, k.rows)
     gather.start()
-    k.at(1)
-    k.weight(ATT)
-    inward, outward = k.matrix(ATT, 0, 3 * wide), k.matrix(ATT, 3 * wide, 4 * wide)
+    k.at(10)
+    k.weight(QKV)
+    k.weight(PRJ)
+    sums[...] = jnp.zeros((length, width), F32)
     for owner in gather.arrivals():
         rows = gather.rows(owner)
-        k.outer[rows, :] = nn(k.up[rows, :], outward).astype(BF16)
-    for load in loads:
-        load.wait()
-    k.dqk[...] = jnp.zeros_like(k.dqk)
-    k.dv[...] = jnp.zeros_like(k.dv)
-    block = 256
+        grads[rows, 3 * wide :] = nn(up[rows, :], k.matrix(PRJ, 0, wide)).astype(BF16)
+    load_turned.wait()
+    block = 128
     for offset in range(0, length, block):
-        k.at(2 + offset // block)
+        if offset % 256 == 0:
+            k.at(11 + offset // 256)
         extent = offset + block
         allowed = allowed_keys(k.seg_row, k.seg_col, offset, block, extent)
         for head in range(heads):
-            own = slice(head * HEAD, (head + 1) * HEAD)
-            key_columns = slice(wide + head * HEAD, wide + (head + 1) * HEAD)
-            query = k.kept[QK][offset:extent, own] * BF16(HEAD**-0.5)
-            keys = k.kept[QK][:extent, key_columns]
-            outer = k.outer[offset:extent, own]
+            own, key, value, out = (slice(n * wide + head * HEAD, n * wide + (head + 1) * HEAD) for n in range(4))
+            query = turned[offset:extent, own] * BF16(HEAD**-0.5)
+            keys = turned[:extent, key]
+            outer = grads[offset:extent, out]
             probability = softmax_rows(query, keys, allowed)
-            inner = nt(outer, k.kept[V][:extent, own])
+            inner = nt(outer, turned[:extent, value])
             score = probability * (inner - jnp.sum(probability * inner, axis=-1, keepdims=True))
             score = score.astype(BF16)
-            k.dqk[offset:extent, own] = nn(score, keys) * HEAD**-0.5
-            k.dqk[:extent, key_columns] += tn(score, query)
-            k.dv[:extent, own] += tn(probability.astype(BF16), outer)
+            sums[offset:extent, own] = nn(score, keys) * HEAD**-0.5
+            sums[:extent, key] += tn(score, query)
+            sums[:extent, value] += tn(probability.astype(BF16), outer)
+    load_normed.wait()
+    k.put_product(PRJ, 0, (up, turned, slice(3 * wide, 4 * wide)))
+    k.made(PRJ)
     for offset in range(0, length, block):
         rows = slice(offset, offset + block)
-        k.dqkv[rows, : 2 * wide] = turn(k.dqk[rows, :], k.cosine[rows, :], -k.sine[rows, :]).astype(BF16)
-        k.dqkv[rows, 2 * wide :] = k.dv[rows, :].astype(BF16)
-    scatter = TokenScatter(place, k.scatter)
-    scatter.begin(lambda owner: nt(k.dqkv[quarter_rows(length, owner), :], inward))
-    k.put(ATT, 0, tn(k.kept[NRM][...], k.dqkv[...]))
-    k.put(ATT, 3 * wide, tn(k.up[...], k.kept[ATTENDED][...]))
-    k.made(ATT)
-    inward, k.gain_grad[...] = normalise_back(k.x[...], k.gain[...], scatter.total())
-    k.grad[...] = k.upstream[...] + inward
+        both = turn(sums[rows, : 2 * wide], k.cosine[rows, :], -k.sine[rows, :])
+        grads[rows, : 2 * wide] = both.astype(BF16)
+        grads[rows, 2 * wide : 3 * wide] = sums[rows, 2 * wide : 3 * wide].astype(BF16)
+    scatter = TokenScatter(place, k.scatters[0])
+    scatter.begin(lambda owner: nt(grads[quarter_rows(length, owner), : 3 * wide], k.matrix(QKV, 0, 3 * wide)))
+    k.at(15)
+    k.put_product(QKV, 0, (normed, grads, slice(0, 3 * wide)))
+    k.made(QKV)
+    k.at(16)
+    load_rows.wait()
+    inward, k.gain_att[...] = normalise_back(k.rows[...], k.gains[0:1, :], scatter.total())
+    k.grad[...] += inward
 
 
 def pick_softmax(logits, chosen, axis):
@@ -439,9 +456,13 @@
     return exponent / jnp.sum(exponent, axis=axis, keepdims=True)
 
 
-def slots_by_token(slot_row):
-    shape = (CAP, slot_row.shape[1])
-    return lax.broadcasted_iota(jnp.int32, shape, 0) == slot_row
+def slot_halves():
+    return [(0, CAP // 2), (CAP // 2, CAP)]
+
+
+def slots_by_token(slot_row, first, last):
+    shape = (last - first, slot_row.shape[1])
+    return lax.broadcasted_iota(jnp.int32, shape, 0) == slot_row - first
 
 
 def tokens_by_slot(slot_column):
@@ -470,29 +491,34 @@
     return [(0, 0), (1, 0), (1, 1), (0, 1)]
 
 
-def both_arrivals(k, buf, on_rows, between):
+def both_arrivals(k, buf, on_rows, between, point):
     place = k.place
     sequences = buf.shape[0]
-    own = TokenGather(place, buf.at[0], k.gather)
+    own = TokenGather(place, buf.at[0], k.own_gather)
     quarter = own.rows(place.me)
-    own.start()
     if sequences > 1:
         crossing = send(
             buf.at[0, quarter], buf.at[1, quarter], k.pair_send.at[0], k.pair_recv.at[0], place.partner()
         )
-    for owner in own.arrivals():
+    own.start()
+    k.at(point)
+    for count, owner in enumerate(own.arrivals()):
         on_rows(0, own.rows(owner))
+        if count == 1:
+            k.at(point + 1)
+    k.at(point + 2)
     if sequences > 1:
         crossing.wait_recv()
         other = TokenGather(place, buf.at[1], k.other_gather)
         other.start()
-        k.at(1)
         between()
+        k.at(point + 3)
         for owner in other.arrivals():
             on_rows(1, other.rows(owner))
         crossing.wait_send()
     else:
         between()
+    k.at(point + 4)
 
 
 def give_back(k, total):
@@ -506,7 +532,7 @@
     place = k.place
     moe, branch = k.kept[MOE], k.branch
     k.early(SH, *(EX + e for e in range(experts)))
-    moe[0, quarter_rows(length, place.me), :] = normalise(k.mid[...], k.gain[...]).astype(BF16)
+    moe[0, quarter_rows(length, place.me), :] = normalise(k.mid[...], k.gains[1:2, :]).astype(BF16)
     units = k.w[SH].shape[-1] // 3
     wide = k.w[EX].shape[-1] // 3
 
@@ -522,42 +548,48 @@
 
     def dispatch(s, e):
         index = s * experts + e
-        held = slots_by_token(k.slot_rows[index : index + 1, :]).astype(F32).astype(BF16)
-        k.kept[ROUTED][e, s * CAP : (s + 1) * CAP, :] = nn(held, moe[s]).astype(BF16)
+        for first, last in slot_halves():
+            held = slots_by_token(k.slot_rows[index : index + 1, :], first, last).astype(F32).astype(BF16)
+            k.kept[ROUTED][e, s * CAP + first : s * CAP + last, :] = nn(held, moe[s]).astype(BF16)
 
     def expert(s, e):
         k.weight(EX + e)
         index = s * experts + e
-        slots = slice(s * CAP, (s + 1) * CAP)
-        inner = nn(k.kept[ROUTED][e, slots, :], k.matrix(EX + e, 0, 2 * wide))
-        k.kept[ACT][e, slots, :] = inner.astype(BF16)
-        outs = nt(hidden_of(inner), k.matrix(EX + e, 2 * wide, 3 * wide)).astype(BF16)
+        for first, last in slot_halves():
+            slots = slice(s * CAP + first, s * CAP + last)
+            inner = nn(k.kept[ROUTED][e, slots, :], k.matrix(EX + e, 0, 2 * wide))
+            k.kept[ACT][e, slots, :] = inner.astype(BF16)
+            k.outs[first:last, :] = nt(hidden_of(inner), k.matrix(EX + e, 2 * wide, 3 * wide)).astype(BF16)
         if e < experts - 1:
-            combine = tokens_by_slot(k.slot_cols[:, index : index + 1])
-            branch[s] += k.gates[s, :, e : e + 1] * nn(combine, outs)
+            for first in range(0, length, length // 2):
+                rows = slice(first, first + length // 2)
+                combine = tokens_by_slot(k.slot_cols[rows, index : index + 1])
+                branch[s, rows, :] += k.gates[s, rows, e : e + 1] * nn(combine, k.outs[...])
             return
 
         def block_of(owner):
             rows = quarter_rows(length, owner)
             combine = tokens_by_slot(k.slot_cols[rows, index : index + 1])
-            return branch[s, rows, :] + k.gates[s, rows, e : e + 1] * nn(combine, outs)
+            return branch[s, rows, :] + k.gates[s, rows, e : e + 1] * nn(combine, k.outs[...])
 
         scatters[s].begin(block_of)
+
+    order = expert_order(sequences, experts)
 
     def between():
         for e in range(experts):
             dispatch(0, e)
         k.gate_rows[0] = pick_softmax(nt(k.router_t[...], moe[0]), k.chosen_rows[0], 0)
-
-    both_arrivals(k, moe, on_rows, between)
+        expert(*order[0])
+
+    both_arrivals(k, moe, on_rows, between, 8)
     k.local.start(moe, k.kept_out[MOE], True)
     k.local.start(k.kept[SHARED], k.kept_out[SHARED], True)
-    k.at(2)
-    for step, (s, e) in enumerate(expert_order(sequences, experts)):
+    for step, (s, e) in enumerate(order[1:]):
         if s > 0:
             dispatch(s, e)
         expert(s, e)
-        k.at(3 + step)
+        k.at(13 + step)
     for s in range(1, sequences):
         k.gate_rows[s] = pick_softmax(nt(k.router_t[...], moe[s]), k.chosen_rows[s], 0)
     k.local.start(k.kept[ROUTED], k.kept_out[ROUTED], True)
@@ -574,16 +606,23 @@
 
 def ffn_backward(k):
     sequences, length = k.kept[MOE].shape[:2]
-    experts = k.kept[ROUTED].shape[0]
+    experts = k.kept_in[ROUTED].shape[0]
     place = k.place
     moe, up, moe_grad = k.kept[MOE], k.up, k.moe_grad
     routed, act, shared = k.kept[ROUTED], k.kept[ACT], k.kept[SHARED]
     load_shared = k.local.start(k.kept_in[SHARED], shared)
+    load_upstream = k.local.start(k.upstream, k.grad)
+    load_rows = k.local.start(k.mid, k.rows)
     k.early(SH, *(EX + e for e in range(experts)))
-    load_act = [k.local.start(k.kept_in[ACT].at[e], act.at[e]) for e in range(experts)]
-    load_routed = [k.local.start(k.kept_in[ROUTED].at[e], routed.at[e]) for e in range(experts)]
+
+    def load_expert(e):
+        return [k.local.start(k.kept_in[name].at[e], k.kept[name]) for name in (ACT, ROUTED)]
+
+    loads = {0: load_expert(0)}
     load_moe = k.local.start(k.kept_in[MOE], moe)
-    up[0, quarter_rows(length, place.me), :] = k.upstream[...].astype(BF16)
+    k.early(QKV, PRJ)
+    load_upstream.wait()
+    up[0, quarter_rows(length, place.me), :] = k.grad[...].astype(BF16)
     units = k.w[SH].shape[-1] // 3
     wide = k.w[EX].shape[-1] // 3
     fresh = {SH}
@@ -607,27 +646,33 @@
 
     def expert(s, e):
         k.weight(EX + e)
-        if not done[e]:
-            load_act[e].wait()
-            load_routed[e].wait()
         index = s * experts + e
-        slots = slice(s * CAP, (s + 1) * CAP)
-        held = slots_by_token(k.slot_rows[index : index + 1, :])
-        gate_slot = jnp.sum(jnp.where(held, k.gate_rows[s, e : e + 1, :], 0.0), axis=1, keepdims=True)
-        arrived = nn(held.astype(F32).astype(BF16), up[s]).astype(BF16)
-        k.slot_grad[slots, :] = (arrived.astype(F32) * gate_slot).astype(BF16)
-        inner = act[e, slots, :].astype(F32)
-        hidden = hidden_of(inner)
-        k.hidden[slots, :] = hidden
-        down = nn(arrived, k.matrix(EX + e, 2 * wide, 3 * wide))
-        slot_dot = jnp.sum(hidden.astype(F32) * down, axis=1, keepdims=True)
-        k.slot_sums[s, e : e + 1, :] = jnp.sum(jnp.where(held, slot_dot, 0.0), axis=0, keepdims=True)
-        inner_grad = swiglu_back(down * gate_slot, inner)
-        act[e, slots, :] = inner_grad
-        back = nt(inner_grad, k.matrix(EX + e, 0, 2 * wide)).astype(BF16)
+        holding = k.slot_rows[index : index + 1, :]
+        gate_row = k.gate_rows[s, e : e + 1, :]
+        token_dots = jnp.zeros((1, length), F32)
+        for first, last in slot_halves():
+            slots = slice(s * CAP + first, s * CAP + last)
+            held = slots_by_token(holding, first, last)
+            gate_slot = jnp.sum(jnp.where(held, gate_row, 0.0), axis=1, keepdims=True)
+            arrived = nn(held.astype(F32).astype(BF16), up[s]).astype(BF16)
+            k.slot_grad[slots, :] = (arrived.astype(F32) * gate_slot).astype(BF16)
+            down = nn(arrived, k.matrix(EX + e, 2 * wide, 3 * wide))
+            for copy in loads.pop(e, ()):
+                copy.wait()
+            inner = act[slots, :].astype(F32)
+            hidden = hidden_of(inner)
+            k.hidden[slots, :] = hidden
+            slot_dot = jnp.sum(hidden.astype(F32) * down, axis=1, keepdims=True)
+            token_dots += jnp.sum(jnp.where(held, slot_dot, 0.0), axis=0, keepdims=True)
+            inner_grad = swiglu_back(down * gate_slot, inner)
+            act[slots, :] = inner_grad
+            k.outs[first:last, :] = nt(inner_grad, k.matrix(EX + e, 0, 2 * wide)).astype(BF16)
+        k.slot_sums[s, e : e + 1, :] = token_dots
         if e < experts - 1:
-            combine = tokens_by_slot(k.slot_cols[:, index : index + 1])
-            moe_grad[s] += nn(combine, back)
+            for first in range(0, length, length // 2):
+                rows = slice(first, first + length // 2)
+                combine = tokens_by_slot(k.slot_cols[rows, index : index + 1])
+                moe_grad[s, rows, :] += nn(combine, k.outs[...])
         else:
             gates = k.gate_rows[s]
             pair = jnp.sum(gates, axis=0, keepdims=True)
@@ -640,26 +685,28 @@
                 rows = quarter_rows(length, owner)
                 combine = tokens_by_slot(k.slot_cols[rows, index : index + 1])
                 turned = tn(k.logit_grad[s, :, rows], k.router_t[...])
-                return moe_grad[s, rows, :] + nn(combine, back) + turned
+                return moe_grad[s, rows, :] + nn(combine, k.outs[...]) + turned
 
             scatters[s].begin(block_of)
         done[e] += 1
         if done[e] == sequences:
-            k.put(EX + e, 0, tn(routed[e], act[e]))
-            k.put(EX + e, 2 * wide, tn(k.slot_grad[...], k.hidden[...]))
+            k.put_product(EX + e, 0, (routed, act, slice(None)))
+            k.put_product(EX + e, 2 * wide, (k.slot_grad, k.hidden, slice(None)))
             k.made(EX + e)
+            if e + 1 < experts:
+                loads[e + 1] = load_expert(e + 1)
 
     order = expert_order(sequences, experts)
-    both_arrivals(k, up, on_rows, lambda: expert(*order[0]))
+    both_arrivals(k, up, on_rows, lambda: expert(*order[0]), 1)
     load_moe.wait()
-    whole = sequences * length
-    k.put(SH, 0, tn(moe[...].reshape(whole, -1), shared[...].reshape(whole, -1)))
-    k.put(SH, 2 * units, tn(up[...].reshape(whole, -1), k.hidden_all[...].reshape(whole, -1)))
+    every = range(sequences)
+    k.put_product(SH, 0, *((moe.at[s], shared.at[s], slice(None)) for s in every))
+    k.put_product(SH, 2 * units, *((up.at[s], k.hidden_all.at[s], slice(None)) for s in every))
     k.made(SH)
-    k.at(2)
+    k.at(6)
     for step, (s, e) in enumerate(order[1:]):
         expert(s, e)
-        k.at(3 + step)
+        k.at(7 + step)
     k.router_grad[...] = sum(nn(k.logit_grad[s], moe[s]) for s in range(sequences))
     if sequences > 1:
         returned = give_back(k, scatters[1].total())
@@ -668,21 +715,40 @@
         returned.wait_recv()
         total = total + k.pair_land[...].astype(F32)
         returned.wait_send()
-    inward, k.gain_grad[...] = normalise_back(k.mid[...], k.gain[...], total)
-    k.grad[...] = k.upstream[...] + inward
-
-
-def last_sums(k):
-    place = k.place
-    stage = k.stage
-    stage[0] = k.small[...]
+    load_rows.wait()
+    inward, k.gain_ffn[...] = normalise_back(k.rows[...], k.gains[1:2, :], total)
+    k.grad[...] += inward
+
+
+def layer_forward(k):
+    attention_forward(k)
+    ffn_forward(k)
+
+
+def layer_backward(k):
+    ffn_backward(k)
+    attention_backward(k)
+
+
+def last_backward(k):
+    layer_backward(k)
+    place, stage = k.place, k.stage
+    half = k.slot_rows.shape[0] // 2
+    stage[0] = jnp.zeros_like(stage[0])
+    for at, row in enumerate((k.gain_att, k.gain_ffn, *k.later[:2])):
+        stage[0, at : at + 1, :] = row[...]
+    for at, part in enumerate((k.router_grad, k.later[2])):
+        first, second = part[:half, :], part[half : 2 * half, :]
+        upper = place.half == 1
+        stage[0, 8 * (at + 1) : 8 * (at + 1) + half, :] = jnp.where(upper, second, first)
+        stage[0, 8 * (at + 1) + half : 8 * (at + 1) + 2 * half, :] = jnp.where(upper, first, second)
     partners = (place.member(place.core_peer), place.member(place.y_peer), place.beside())
     for step, partner in enumerate(partners):
         copy = send(stage.at[step], k.land.at[step], k.small_send.at[step], k.small_recv.at[step], partner)
         copy.wait_recv()
         stage[step + 1] = stage[step] + k.land[step]
         copy.wait_send()
-    k.at(1)
+    k.at(17)
     last = len(partners)
     copies = []
     for away in (1, 2, 3):
@@ -759,8 +825,8 @@
 
     outs["z_out"] = {key: Out(part_shape(key), BF16, True) for key in keys[GET_Z]}
     outs["x_out"] = {key: Out(part_shape(key), BF16, True) for key in keys[GET_X]}
-    outs["sums_out"] = {key: Out(block_shape(key), BF16) for key in keys[SUM_X]}
-    outs["totals"] = {key: [Out(block_shape(key)[1:])] * (1 if key[1] == ATT else 2) for key in keys[SUM_Z]}
+    outs["sums_out"] = {key: Out(block_shape(key), BF16, True) for key in keys[SUM_X] if key not in keys[SUM_Z]}
+    outs["totals"] = {key: [Out(block_shape(key)[1:], BF16)] * (1 if key[1] in (QKV, PRJ) else 2) for key in keys[SUM_Z]}
     outs["made_out"] = {
         m: Out(store.shape_of(m), BF16, True) for m in made if (layer, m) not in store.own_sums
     }
@@ -768,13 +834,13 @@
     scratch["sems"] = {
         GET_Z: {key: [dma((4,)), dma((4,)), dma((1,))] for key in keys[GET_Z]},
         GET_X: {key: [dma((1,)), dma((1,))] for key in keys[GET_X]},
-        SUM_X: {key: [dma((1,)), dma((1,)), dma((1,))] for key in keys[SUM_X]},
+        SUM_X: {key: [dma((1,)), dma((1,)), dma((2,))] for key in keys[SUM_X]},
         SUM_Z: {key: [dma((4,)), dma((4,)), dma((1,))] for key in keys[SUM_Z]},
     }
     scratch["blocks"] = {key: vmem(block_shape(key), BF16) for key in keys[SUM_X]}
     scratch["own"] = {key: vmem(block_shape(key), BF16) for key in keys[SUM_X] if key in store.made}
     scratch["lands"] = {key: vmem(block_shape(key), BF16) for key in keys[SUM_Z]}
-    scratch["lsem"] = dma((2 * len(keys_in) + 12,))
+    scratch["lsem"] = dma((2 * len(keys_in) + 20,))
     trees = [jax.tree.flatten(tree, is_leaf=is_leaf) for tree in (ins, outs, scratch)]
     (ins_flat, _), (outs_flat, outs_tree), (scratch_flat, _) = trees
     around = bool(starts)
@@ -804,8 +870,8 @@
                 return Aside(place, source, k.x_out[key], sems)
             if kind == SUM_X:
                 source = k.made_in[key] if key in k.made_in else k.w[key[1]]
-                return AsideSum(place, source, k.own.get(key), k.blocks[key], k.sums_out[key], sems)
-            source = k.sums_out[key] if key in k.sums_out else k.sums_in[key]
+                return AsideSum(place, source, k.own.get(key), k.blocks[key], k.sums_out.get(key), sems)
+            source = k.blocks[key] if key in k.blocks else k.sums_in[key]
             return StraightSum(place, source, k.lands[key], k.totals[key], sems)
 
         running, ended = {}, set()
@@ -869,18 +935,27 @@
             value = k.w[matrix][:, :, :, first:last]
             return value.reshape(width, last - first)
 
-        def put(matrix, first, value):
-            ref = k.w[matrix]
-            shape = (*ref.shape[:3], value.shape[1])
-            ref[:, :, :, first : first + value.shape[1]] = value.astype(BF16).reshape(shape)
+        def put_product(matrix, first, *pairs):
+            ref, half = k.w[matrix], width // 2
+            blocks = ref.shape[0] // 2
+            for part in range(2):
+                cut = slice(part * half, (part + 1) * half)
+                value = sum(tn(left[:, cut], right[:, taken]) for left, right, taken in pairs).astype(BF16)
+                count, columns = value.shape[1], slice(first, first + value.shape[1])
+                if blocks:
+                    shape = (blocks, *ref.shape[1:3], count)
+                    ref[part * blocks : (part + 1) * blocks, :, :, columns] = value.reshape(shape)
+                else:
+                    ref[0, 0, part * half : (part + 1) * half, columns] = value
 
         def finished(matrix):
-            if (layer, matrix) in k.sums_out:
+            if (layer, matrix) in k.blocks:
                 start(SUM_X, (layer, matrix))
             else:
                 k.local.start(k.w[matrix], k.made_out[matrix], True)
 
-        k.at, k.early, k.weight, k.matrix, k.put, k.made = at_point, early, weight, matrix_of, put, finished
+        k.at, k.early, k.weight, k.matrix, k.made = at_point, early, weight, matrix_of, finished
+        k.put_product = put_product
         at_point(0)
         body(k)
         for kind, key in running:
@@ -907,6 +982,31 @@
     store.totals |= result.totals
     store.made |= {(layer, m): value for m, value in result.made_out.items()}
     return result
+
+
+def forward_plan(store, layer, last):
+    qkv, (prj,), (sh,) = (store.keys(layer, matrix) for matrix in (QKV, PRJ, SH))
+    low, high = store.keys(layer, EX), store.keys(layer, EX + 1)
+
+    def pass_on(point, *keys):
+        return [step for key in keys for step in ((point, GET_Z, key, True), (point, GET_X, key))]
+
+    if layer == 0:
+        plan = [(0, GET_Z, key) for key in (*qkv, prj, sh, *low)]
+        plan += pass_on(1, *qkv) + pass_on(2, prj) + pass_on(6, sh) + pass_on(7, low[0]) + pass_on(8, low[1])
+        plan += [(8, GET_Z, key) for key in high] + pass_on(9, low[2])
+    else:
+        plan = [(0, GET_X, sh)] + [(0, GET_Z, key) for key in (*low, high[0])]
+        plan += pass_on(3, low[0]) + pass_on(4, low[1]) + pass_on(7, low[2]) + pass_on(8, high[0])
+        plan += [(8, GET_Z, key) for key in high[1:]]
+    if layer < last:
+        qkv, (prj,), (sh,) = (store.keys(layer + 1, matrix) for matrix in (QKV, PRJ, SH))
+        plan += [(8, GET_Z, key) for key in (*qkv, prj, sh)] + pass_on(15, *qkv, prj)
+    if layer == 0:
+        plan += pass_on(11, high[0]) + pass_on(12, high[1]) + pass_on(13, high[2])
+    else:
+        plan += pass_on(11, high[1]) + pass_on(12, high[2])
+    return plan
 
 
 def on_device(
@@ -942,11 +1042,6 @@
             return values
         return jnp.where(upper, jnp.roll(values, -experts, axis), values)
 
-    def known_first(values, axis):
-        if not paired:
-            return values
-        return jnp.where(upper, jnp.roll(values, experts, axis), values)
-
     picks = jnp.concatenate([expert_pick, slot_index], axis=2)[:, None]
     if paired:
         swap = [(at, (at // 4) * 4 + (at % 4 + 2) % 4) for at in range(ring)]
@@ -967,13 +1062,16 @@
     projection_t = jnp.swapaxes(projection, 1, 2)
     narrowing_t = jnp.swapaxes(narrowing, 1, 2)
     contraction_t = jnp.swapaxes(contraction, 2, 3)
-    columns = {ATT: 4 * wide, SH: 3 * shared_units} | {EX + e: 3 * units for e in range(experts)}
+    columns = {QKV: 3 * wide, PRJ: wide, SH: 3 * shared_units} | {EX + e: 3 * units for e in range(experts)}
     parts = {matrix: [(0, height)] for matrix in columns}
     if paired:
-        parts[EX + 1] = [(0, height // 3), (height // 3, height - height // 3)]
+        third = height // 3
+        parts[QKV] = parts[EX] = [(at, third) for at in (0, third, 2 * third)]
+        parts[EX + 1] = [(0, height // 2), (height // 2, third), (height // 2 + third, height - height // 2 - third)]
     store = Store(height, width, columns, parts, paired)
     for layer in range(layers):
-        store.source[layer, ATT] = jnp.concatenate([*attention[layer], projection_t[layer]], axis=-1)
+        store.source[layer, QKV] = jnp.concatenate([*attention[layer]], axis=-1)
+        store.source[layer, PRJ] = projection_t[layer]
         thirds = (widening[layer, 0], widening[layer, 1], narrowing_t[layer])
         whole = [
             jnp.concatenate([expansion[layer, e, 0], expansion[layer, e, 1], contraction_t[layer, e]], axis=-1)
@@ -999,7 +1097,7 @@
 
     vmem = pltpu.VMEM
     token_scatter = scatter_scratch(length, width)
-    pair_scratch = dict(scatters=[token_scatter] * sequences)
+    pair_scratch = dict(scatters=[token_scatter] * sequences, own_gather=gather_scratch())
     if paired:
         pair_scratch |= dict(
             other_gather=gather_scratch(),
@@ -1008,9 +1106,7 @@
             pair_sum=vmem((quarter, width), BF16),
             pair_land=vmem((quarter, width), BF16),
         )
-    attention_shapes = {
-        NRM: (length, width), QK: (length, 2 * wide), V: (length, wide), ATTENDED: (length, wide)
-    }
+    attention_shapes = {NRM: (length, width), TURNED: (length, 4 * wide)}
     ffn_shapes = {
         MOE: (sequences, length, width),
         SHARED: (sequences, length, 2 * shared_units),
@@ -1028,171 +1124,143 @@
     def kept_outs(shapes):
         return {name: Out(shape, BF16, True) for name, shape in shapes.items()}
 
-    def kept_ins(arrays):
-        return {name: Far(array) for name, array in arrays.items()}
-
-    store.own_sums = {(layer, matrix) for layer in range(layers) for matrix in (SH, EX)} if paired else set()
+    store.own_sums = set()
     saved = []
     current = stream
     next_id = 0
     for layer in range(layers):
-        first, second = (layer, EX + 1, 0), (layer, EX + 1, 1)
-        att, sh, ex = (layer, ATT, 0), (layer, SH, 0), (layer, EX, 0)
-        if layer == 0:
-            plan = [
-                (0, GET_Z, att), (1, GET_Z, att, True), (1, GET_X, att), (1, GET_Z, sh), (2, GET_Z, ex),
-                (3, GET_Z, first), (4, GET_Z, sh, True), (4, GET_X, sh),
-            ]
-        else:
-            plan = [(0, GET_X, sh), (0, GET_Z, ex), (2, GET_Z, first)]
         result = call(
             store,
-            attention_forward,
+            layer_forward,
             next_id,
-            dict(x=current, gain=norm_gains[layer, 0][None], **places),
-            dict(mid=rows_out, kept_out=kept_outs(attention_shapes)),
-            dict(kept=kept_scratch(attention_shapes), gather=gather_scratch(), scatter=token_scatter),
-            layer,
-            [ATT],
-            plan=plan if paired else (),
-        )
-        mid, attention_kept = result.mid, result.kept_out
-        plan = [
-            (0, GET_X, ex), (0, GET_X, first), (1, GET_Z, second), (3, GET_Z, second, True), (3, GET_X, second)
-        ]
-        if layer < last:
-            att, sh = (layer + 1, ATT, 0), (layer + 1, SH, 0)
-            plan += [(1, GET_Z, att), (1, GET_Z, sh), (5, GET_Z, att, True), (5, GET_X, att)]
-        result = call(
-            store,
-            ffn_forward,
-            next_id + 1,
             dict(
-                mid=mid,
-                gain=norm_gains[layer, 1][None],
+                x=current,
+                gains=norm_gains[layer],
                 router=router_wide[layer],
                 router_t=router_t[layer],
                 slot_rows=slot_rows[layer],
                 slot_cols=slot_cols[layer],
                 chosen_rows=chosen_rows[layer],
                 chosen_cols=chosen_cols[layer],
+                **places,
             ),
-            dict(following=rows_out, gate_rows=Out((sequences, 8, length)), kept_out=kept_outs(ffn_shapes)),
             dict(
-                kept=kept_scratch(ffn_shapes),
+                mid=rows_out,
+                following=rows_out,
+                gate_rows=Out((sequences, 8, length)),
+                kept_out=kept_outs(attention_shapes | ffn_shapes),
+            ),
+            dict(
+                kept=kept_scratch(attention_shapes | ffn_shapes),
                 branch=vmem((sequences, length, width), F32),
+                outs=vmem((CAP, width), BF16),
                 gates=vmem((sequences, length, LANES), F32),
                 gather=gather_scratch(),
+                scatter=token_scatter,
                 **pair_scratch,
             ),
             layer,
-            ffn_matrices,
-            plan=plan if paired else (),
+            [QKV, PRJ, *ffn_matrices],
+            plan=forward_plan(store, layer, last) if paired else (),
         )
-        saved.append((current, mid, attention_kept, result.gate_rows, result.kept_out))
+        saved.append((current, result.mid, result.kept_out, result.gate_rows))
         current = result.following
-        next_id += 2
+        next_id += 1
 
     upstream = cotangent
-    gain_parts, router_parts = [None] * layers, [None] * layers
+    parts_small = [None] * layers
     for layer in reversed(range(layers)):
-        x_in, mid, attention_kept, gate_rows, ffn_kept = saved[layer]
-        plan = []
+        x_in, mid, kept, gate_rows = saved[layer]
+        plan = [
+            (8, SUM_X, (layer, SH), True), (8, SUM_Z, (layer, SH)), (11, SUM_X, (layer, EX), True), (11, SUM_Z, (layer, EX))
+        ]
+        made = [SH, EX, EX + 1]
         if layer < last:
-            above = (layer + 1, ATT)
-            plan = [(0, SUM_X, above), (1, SUM_Z, (layer + 1, EX + 1)), (2, SUM_X, above, True), (2, SUM_Z, above)]
+            above = [(layer + 1, PRJ), (layer + 1, QKV)]
+            plan += [(0, SUM_X, key) for key in above] + [(1, SUM_Z, (layer + 1, EX + 1))]
+            plan += [step for key in above for step in ((6, SUM_X, key, True), (6, SUM_Z, key))]
+        finish = paired and layer == 0
+        if finish:
+            made += [PRJ, QKV]
+            plan += [(15, SUM_X, (0, EX + 1), True), (15, SUM_Z, (0, EX + 1))]
+            plan += [step for m in (PRJ, QKV) for step in ((17, SUM_X, (0, m), True), (17, SUM_Z, (0, m)))]
+        store.own_sums = {(layer, matrix) for matrix in made} if paired else set()
+        ins = dict(
+            upstream=Far(upstream),
+            x=Far(x_in),
+            mid=Far(mid),
+            gains=norm_gains[layer],
+            router_t=router_t[layer],
+            slot_rows=slot_rows[layer],
+            slot_cols=slot_cols[layer],
+            chosen_rows=chosen_rows[layer],
+            gate_rows=gate_rows,
+            kept_in={name: Far(array) for name, array in kept.items()},
+            **places,
+        )
+        outs = dict(grad=rows_out, gain_att=gain_out, gain_ffn=gain_out, router_grad=Out((8, width)))
+        work = dict(
+            kept={
+                MOE: vmem((sequences, length, width), BF16),
+                SHARED: vmem((sequences, length, 2 * shared_units), BF16),
+                ROUTED: vmem((sequences * CAP, width), BF16),
+                ACT: vmem((sequences * CAP, 2 * units), BF16),
+            },
+            hidden_all=vmem((sequences, length, shared_units), BF16),
+            hidden=vmem((sequences * CAP, units), BF16),
+            slot_grad=vmem((sequences * CAP, width), BF16),
+            moe_grad=vmem((sequences, length, width), F32),
+            slot_sums=vmem((sequences, 8, length), F32),
+            logit_grad=vmem((sequences, 8, length), BF16),
+            up=vmem((sequences, length, width), BF16),
+            rows=vmem((quarter, width), F32),
+            outs=vmem((CAP, width), BF16),
+            **pair_scratch,
+        )
+        if not paired:
+            work |= dict(spare=vmem((2, length, width), BF16))
+        if finish:
+            rows = 8 * (1 + layers)
+            ins |= dict(later=list(parts_small[last]))
+            outs |= dict(small_sum=Out((rows, width)))
+            work |= dict(
+                stage=vmem((4, rows, width), F32),
+                land=vmem((3, rows, width), F32),
+                rows_z=vmem((4, rows, width), F32),
+                small_send=pltpu.SemaphoreType.DMA((6,)),
+                small_recv=pltpu.SemaphoreType.DMA((6,)),
+            )
         result = call(
             store,
-            ffn_backward,
+            last_backward if finish else layer_backward,
             next_id,
-            dict(
-                upstream=upstream,
-                mid=mid,
-                gain=norm_gains[layer, 1][None],
-                router_t=router_t[layer],
-                slot_rows=slot_rows[layer],
-                slot_cols=slot_cols[layer],
-                chosen_rows=chosen_rows[layer],
-                gate_rows=gate_rows,
-                kept_in=kept_ins(ffn_kept),
-            ),
-            dict(grad=rows_out, gain_grad=gain_out, router_grad=Out((8, width))),
-            dict(
-                kept=kept_scratch(ffn_shapes),
-                hidden_all=vmem((sequences, length, shared_units), BF16),
-                hidden=vmem((sequences * CAP, units), BF16),
-                slot_grad=vmem((sequences * CAP, width), BF16),
-                moe_grad=vmem((sequences, length, width), F32),
-                slot_sums=vmem((sequences, 8, length), F32),
-                logit_grad=vmem((sequences, 8, length), BF16),
-                up=vmem((sequences, length, width), BF16),
-                gather=gather_scratch(),
-                **pair_scratch,
-            ),
+            ins,
+            outs,
+            work,
             layer,
-            ffn_matrices,
-            ffn_matrices,
-            plan=plan if paired else (),
-        )
-        mid_grad, gain_two, router_parts[layer] = result.grad, result.gain_grad, result.router_grad
-        plan = [(0, SUM_Z, (layer, SH)), (0, SUM_X, (layer, EX + 1)), (1, SUM_Z, (layer, EX))]
-        result = call(
-            store,
-            attention_backward,
-            next_id + 1,
-            dict(
-                upstream=mid_grad, x=x_in, gain=norm_gains[layer, 0][None], kept_in=kept_ins(attention_kept), **places
-            ),
-            dict(grad=rows_out, gain_grad=gain_out),
-            dict(
-                kept=kept_scratch(attention_shapes),
-                outer=vmem((length, wide), BF16),
-                dqk=vmem((length, 2 * wide), F32),
-                dv=vmem((length, wide), F32),
-                dqkv=vmem((length, 3 * wide), BF16),
-                up=vmem((length, width), BF16),
-                gather=gather_scratch(),
-                scatter=token_scatter,
-            ),
-            layer,
-            [ATT],
-            [ATT],
+            [QKV, PRJ, *ffn_matrices],
+            [QKV, PRJ, *ffn_matrices],
             plan=plan if paired else (),
         )
         upstream = result.grad
-        gain_parts[layer] = jnp.concatenate([result.gain_grad, gain_two], axis=0)
-        next_id += 2
-
-    router_parts = [known_first(part[:all_experts], 0) for part in router_parts]
-    small = jnp.concatenate(gain_parts + router_parts, axis=0)
+        parts_small[layer] = (result.gain_att, result.gain_ffn, result.router_grad)
+        next_id += 1
+
     if paired:
-        count = small.shape[0]
-        padded = -(-count // 8) * 8
-        small = jnp.pad(small, ((0, padded - count), (0, 0)))
-        small = call(
-            store,
-            last_sums,
-            next_id,
-            dict(small=small),
-            dict(small_sum=Out((padded, width))),
-            dict(
-                stage=vmem((4, padded, width), F32),
-                land=vmem((3, padded, width), F32),
-                rows_z=vmem((4, padded, width), F32),
-                small_send=pltpu.SemaphoreType.DMA((6,)),
-                small_recv=pltpu.SemaphoreType.DMA((6,)),
+        gains_grad = result.small_sum[: 2 * layers].reshape(layers, 2, width)
+        router_grad = result.small_sum[8:].reshape(layers, 8, width)[:, :all_experts]
+    else:
+        gains_grad, router_grad = lax.psum(
+            (
+                jnp.stack([jnp.concatenate(part[:2], axis=0) for part in parts_small]),
+                jnp.stack([part[2][:all_experts] for part in parts_small]),
             ),
-            0,
-            plan=[(0, SUM_Z, (0, EX + 1)), (0, SUM_X, (0, ATT)), (1, SUM_X, (0, ATT), True), (1, SUM_Z, (0, ATT))],
-        ).small_sum
-    else:
-        small = lax.psum(small, ("dp", "tensor"))
+            ("dp", "tensor"),
+        )
         store.totals = {
             key: [lax.psum_scatter(part[0, 0], "dp", scatter_dimension=0, tiled=True).astype(F32)]
             for key, part in store.made.items()
         }
-    gains_grad = small[: 2 * layers].reshape(layers, 2, width)
-    router_grad = small[2 * layers : 2 * layers + layers * all_experts].reshape(layers, all_experts, width)
 
     def split(pieces):
         mine, theirs = pieces
@@ -1202,21 +1270,22 @@
         [] for _ in range(6)
     )
     for layer in range(layers):
-        (whole,) = store.totals[layer, ATT]
+        totals = {matrix: [part.astype(F32) for part in store.totals[layer, matrix]] for matrix in columns}
+        (whole,) = totals[QKV]
         attention_grad.append(jnp.stack([whole[:, n * wide : (n + 1) * wide] for n in range(3)]))
-        projection_grad.append(whole[:, 3 * wide :].T)
+        projection_grad.append(totals[PRJ][0].T)
         if paired:
-            halves = split(store.totals[layer, SH])
+            halves = split(totals[SH])
             shared = [
                 jnp.concatenate([half[:, n * shared_units : (n + 1) * shared_units] for half in halves], axis=1)
                 for n in range(3)
             ]
-            by_expert = [split(store.totals[layer, EX + e]) for e in range(experts)]
+            by_expert = [split(totals[EX + e]) for e in range(experts)]
             wholes = [by_expert[e][a] for a in range(2) for e in range(experts)]
         else:
-            (whole,) = store.totals[layer, SH]
+            (whole,) = totals[SH]
             shared = [whole[:, n * units : (n + 1) * units] for n in range(3)]
-            wholes = [store.totals[layer, EX + e][0] for e in range(experts)]
+            wholes = [totals[EX + e][0] for e in range(experts)]
         widening_grad.append(jnp.stack(shared[:2]))
         narrowing_grad.append(shared[2].T)
         expansion_grad.append(

time: 638 us -> 612 us (0.959)
  Pallas kernels: 575 us -> 551 us
    pallas_call x9 -> x4, Pallas kernels: 575 us -> 551 us  [call(): pl.pallas_call(kernel, out_shape=[jax.ShapeDtypeStruct(out.shape, out.kin...]
  transfers between devices with their start and end apart: 1 -> 1, of which waited for: 0 -> 0; matrix products, arithmetic and copies ran while one was open for 3% -> 3% of each run, Pallas kernels for 11% -> 0%
where the time goes in v3:
time: 612 us; the launch traced here: 602 us
  Pallas kernels  551 us (90%)
  local copies, waits for them, and re-layouts  24.9 us (4%)
  other arithmetic  21.4 us (3%)
    pallas_call x4, Pallas kernels, call(): pl.pallas_call(kernel, out_shape=[jax.ShapeDtypeStruct(out.shape, out.kin...  551 us
  transfers between devices with their start and end apart: 1, of which 0 were waited for; matrix products, arithmetic and copies ran while one was open for 3% of the time, Pallas kernels for 0%

profile of v3, /device:TPU:0, one launch (start us, length us, event | category | flops | bytes accessed | tf_op | source)
XLA Modules:
  0.0 602.3 jit_solution(2280861724161270392)
XLA Ops:
  0.7 0.8 add_bitcast_fusion
  1.5 3.1 collective-permute-start
  4.6 1.3 slice_bitcast_fusion.70
  5.9 0.8 fusion.31
  6.7 1.0 copy.52
  7.7 0.6 slice_bitcast_fusion.60
  8.3 1.0 slice_bitcast_fusion.30
  9.3 1.0 slice_bitcast_fusion.65
  10.6 2.0 fusion.4
  12.6 1.3 pad_maximum_fusion.8.refs_2_.refs_1_
  13.9 0.1 slice_bitcast_fusion.45
  14.0 0.7 pad_maximum_fusion.11.refs_15_
  14.8 0.8 pad_maximum_fusion.12.refs_26_
  15.6 1.3 pad_maximum_fusion.9.refs_8_.refs_14_.refs_19_
  16.9 0.9 pad_maximum_fusion.5.refs_16_.refs_17_.refs_18_
  17.8 0.9 pad_maximum_fusion.4.refs_14_.refs_15_.refs_16_
  18.7 0.9 pad_maximum_fusion.3.refs_11_.refs_12_.refs_13_
  19.7 0.9 pad_maximum_fusion.6.refs_19_.refs_20_.refs_21_
  20.6 0.7 pad_maximum_fusion.14.refs_22_.refs_23_.refs_24_
  21.3 0.7 pad_maximum_fusion.13.refs_11_.refs_12_.refs_13_
  22.0 0.6 fusion.14
  22.6 0.8 copy.54.refs_4_
  23.4 0.8 copy.58.refs_4_
  24.3 1.0 copy.59.refs_6_.refs_12_.refs_17_
  25.6 0.6 squeeze.175.refs_10_.refs_21_
  26.2 0.6 squeeze.156.refs_10_.refs_16_
  27.0 0.2 fusion.1
  27.2 0.6 fusion.9
  27.9 1.0 copy.60.refs_9_.refs_15_
  28.9 1.0 copy.56.refs_9_.refs_20_
  29.9 1.3 copy.53.refs_0_
  31.2 1.3 copy.57.refs_0_
  32.5 146.7 %shard_map.204 = (f32[256,768]{1,0:T(8,128)}, f32[2,8,1024]{2,1,0:T(8,128)}, bf16[1024,768]{1,0:T(8,128)(2,1)}, bf16[1024,768]{1,0:T(8,128)(2,1)}, bf16[2,1024,7...) custom-call(f32[2,1024,128]{2,1,0:T(8,128)} %copy.53.refs_0_, ...), custom_call_target="tpu_custom_call" | custom-call | tf_op jit(solution)/shard_map/pallas_call | solution.py:968
  179.2 115.5 %shard_map.205 = (f32[256,768]{1,0:T(8,128)}, f32[2,8,1024]{2,1,0:T(8,128)}, bf16[1024,768]{1,0:T(8,128)(2,1)}, bf16[1024,768]{1,0:T(8,128)(2,1)}, bf16[2,1024,7...) custom-call(f32[2,1024,128]{2,1,0:T(8,128)} %copy.57.refs_0_, ...), custom_call_target="tpu_custom_call" | custom-call | tf_op jit(solution)/shard_map/pallas_call | solution.py:968
  294.7 123.7 %shard_map.206 = (f32[1,768]{1,0:T(1,128)}, f32[1,768]{1,0:T(1,128)}, f32[256,768]{1,0:T(8,128)}, bf16[4,2,96,576]{3,2,1,0:T(8,128)(2,1)}, bf16[4,2,96,192]{3,2,...) custom-call(f32[2,8,1024]{2,1,0:T(8,128)} %get-tuple-element.319.ref, ...), custom_call_target="tpu_custom_call" | custom-call | tf_op jit(solution)/shard_map/pallas_call | solution.py:968
  418.5 165.4 %shard_map.207 = (f32[1,768]{1,0:T(1,128)}, f32[1,768]{1,0:T(1,128)}, f32[256,768]{1,0:T(8,128)}, f32[8,768]{1,0:T(8,128)}, f32[24,768]{1,0:T(8,128)}, /*index=5...) custom-call(f32[2,8,1024]{2,1,0:T(8,128)} %get-tuple-element.318.ref, ...), custom_call_target="tpu_custom_call" | custom-call | tf_op jit(solution)/shard_map/pallas_call | solution.py:968
  583.9 0.8 slice.437
  584.7 0.8 slice_bitcast_fusion.62
  585.5 0.6 slice_bitcast_fusion.69
  586.2 0.6 reshape.56
  586.8 0.8 maximum_convert_fusion
  587.6 0.8 copy.65
  588.4 0.9 convert_element_type.56
  589.6 0.1 convert_select_fusion.9
  589.9 0.8 copy-done.5
  590.7 0.1 copy-done.6
  590.8 0.1 copy-done.11
  590.9 0.1 copy-done.12
  591.0 0.3 convert_select_fusion.1
  591.5 0.8 copy-done.7
  592.3 0.1 copy-done.8
  592.4 0.1 copy-done.9
  592.5 0.1 copy-done.10
  592.5 0.3 convert_select_fusion.5
  593.1 0.9 pad_maximum_fusion.7
  594.1 0.8 pad_maximum_fusion.10
  594.9 0.9 pad_maximum_fusion.2
  596.2 1.3 pad_maximum_fusion.1
  597.6 0.1 maximum_bitcast_fusion.1
  597.7 0.1 maximum_bitcast_fusion
  597.8 2.0 pad_maximum_fusion
  599.8 0.9 copy.74
  600.7 0.5 copy-done.3
  601.2 0.9 copy.75
  (102 shorter events, 2.0 us)
Async XLA Ops:
  0.6 9.7 %copy-start.4 = (bf16[2,2,96,512]{3,2,1,0:T(8,128)(2,1)S(1)}, bf16[2,2,96,512]{3,2,1,0:T(8,128)(2,1)}, u32[]{:S(2)}) copy-start(bf16[2,2,96,512]{3,2,1,0:T(8,128)(2,1)} %param.22) | copy-start | bytes 1179652
  1.5 23.8 %collective-permute-start = (s32[2,1,1024,4]{2,3,0,1:T(4,128)S(1)}, s32[2,1,1024,4]{2,3,0,1:T(4,128)S(1)}, u32[]{:S(2)}, u32[]{:S(2)}) collective-permute-start(s32[2,1,1024,4]{2,3,0,1:T(4,128)S(1)} %add_bitcast_fusion), channel_id=1, source_target_pairs={{0,8},{4,12},{8,0},{12,4},{16,24},{20,28},{24,16},{28,20},{1,9},{5... | collective-permute-start | bytes 98312 | tf_op jit(solution)/shard_map/ppermute | solution.py:1048
  7.7 2.8 copy-start.19
  9.3 1.3 copy-start.1
  10.6 3.3 copy-start
  19.6 4.6 copy-start.18
  583.9 5.6 copy-start.17
  583.9 5.7 copy-start.13
  583.9 5.7 copy-start.14
  583.9 5.7 copy-start.15
  583.9 5.7 copy-start.16
  589.7 1.0 copy-start.5
  589.7 1.0 copy-start.6
  589.7 1.1 copy-start.11
  589.8 1.2 copy-start.12
  591.3 1.0 copy-start.7
  591.3 1.0 copy-start.8
  591.3 1.1 copy-start.9
  591.3 1.2 copy-start.10
  597.8 2.0 copy-start.2
  599.8 1.4 copy-start.3

commit v4 on v3

--- a/solution.py
+++ b/solution.py
@@ -4,6 +4,7 @@
 
 import jax
 import jax.numpy as jnp
+import numpy as np
 from jax import lax
 from jax.experimental import pallas as pl
 from jax.experimental.pallas import tpu as pltpu
@@ -236,32 +237,51 @@
 
 
 class AsideSum:
-    def __init__(self, place, source, own, landing, out, sems):
-        self.place, self.source, self.own, self.landing, self.out = place, source, own, landing, out
+    def __init__(self, place, source, own, landing, out, onward, sems):
+        self.place, self.source, self.own, self.landing = place, source, own, landing
+        self.out, self.onward = out, onward
         self.send_sem, self.recv_sem, self.local_sem = sems
+        self.left = [2, 1, 3, 0]
 
     def start(self):
         place = self.place
-        self.copy = send(
-            self.source.at[:, 1 - place.x], self.landing, self.send_sem.at[0], self.recv_sem.at[0], place.beside()
-        )
+        self.copies = {}
+        for away in self.left:
+            at = lax.rem(place.z + away, 4)
+            self.copies[away] = send(
+                self.source.at[at, 1 - place.x],
+                self.landing.at[at],
+                self.send_sem.at[away],
+                self.recv_sem.at[away],
+                place.beside(),
+            )
+        self.load = None
         if self.own is not None:
             self.load = pltpu.make_async_copy(self.source.at[:, place.x], self.own, self.local_sem.at[0])
             self.load.start()
 
-    def arrived(self):
-        self.copy.wait_recv()
-        if self.own is not None:
-            self.load.wait()
-        for at in range(4):
+    def take(self, count):
+        for away in self.left[:count]:
+            at = lax.rem(self.place.z + away, 4)
+            self.copies[away].wait_recv()
+            if self.load is not None:
+                self.load.wait()
+                self.load = None
             own = self.source[at, self.place.x] if self.own is None else self.own[at]
             self.landing[at] = (own.astype(F32) + self.landing[at].astype(F32)).astype(BF16)
+            if self.onward is not None:
+                self.onward.push(away)
+        self.left = self.left[count:]
+
+    def arrived(self):
+        self.take(len(self.left))
         if self.out is not None:
             self.store = pltpu.make_async_copy(self.landing, self.out, self.local_sem.at[1])
             self.store.start()
 
     def close(self):
-        self.copy.wait_send()
+        for copy in self.copies.values():
+            copy.wait_send()
         if self.out is not None:
             self.store.wait()
 
@@ -270,21 +290,20 @@
     def __init__(self, place, source, landing, totals, sems):
         self.place, self.source, self.landing, self.totals = place, source, landing, totals
         self.send_sem, self.recv_sem, self.local_sem = sems
+        self.copies = []
+
+    def push(self, away):
+        block = self.source.at[lax.rem(self.place.z + away, 4)]
+        if away == 0:
+            self.own = pltpu.make_async_copy(block, self.landing.at[0], self.local_sem.at[0])
+            self.own.start()
+            return
+        sems = self.send_sem.at[away], self.recv_sem.at[away]
+        self.copies.append(send(block, self.landing.at[away], *sems, self.place.beyond(away)))
 
     def start(self):
-        place = self.place
-        self.copies = [
-            send(
-                self.source.at[lax.rem(place.z + away, 4)],
-                self.landing.at[away],
-                self.send_sem.at[away],
-                self.recv_sem.at[away],
-                place.beyond(away),
-            )
-            for away in (2, 1, 3)
-        ]
-        self.own = pltpu.make_async_copy(self.source.at[place.z], self.landing.at[0], self.local_sem.at[0])
-        self.own.start()
+        for away in (2, 1, 3, 0):
+            self.push(away)
 
     def arrived(self):
         for copy in self.copies:
@@ -333,12 +352,11 @@
     ) * jnp.concatenate([sine] * times, axis=1)
 
 
-def allowed_keys(seg_row, seg_col, offset, rows, extent):
-    row_index = offset + lax.broadcasted_iota(jnp.int32, (rows, extent), 0)
-    column_index = lax.broadcasted_iota(jnp.int32, (rows, extent), 1)
-    return (column_index <= row_index) & (
-        seg_row[:, :extent] == seg_col[offset : offset + rows, :]
-    )
+def allowed_keys(seg_row, seg_col, offset):
+    shape = (seg_col.shape[0], seg_row.shape[1])
+    row_index = offset + lax.broadcasted_iota(jnp.int32, shape, 0)
+    column_index = lax.broadcasted_iota(jnp.int32, shape, 1)
+    return (column_index <= row_index) & (seg_row == seg_col)
 
 
 def softmax_rows(query, keys, allowed):
@@ -349,6 +367,49 @@
 
 def sigmoid(values):
     return 1.0 / (1.0 + jnp.exp(-values))
+
+
+def make_tables(k, forward):
+    sequences = len(k.picks)
+    experts, length = k.slot_rows.shape[0] // sequences, k.slot_rows.shape[1]
+    count = sequences * experts
+    total = k.router.shape[0]
+    if k.exchange:
+        k.picks_sent.wait()
+        k.picks_out[...] = k.picks[1][...]
+    first = experts * k.place.half if sequences > 1 else 0
+    for s, picks in enumerate(k.picks):
+        pick_a, pick_b, slot_a, slot_b = (picks[4 * k.layer + n : 4 * k.layer + n + 1, :] for n in range(4))
+        rows = []
+        for e in range(total):
+            expert = lax.rem(e + first, total)
+            by_a, by_b = pick_a == expert, pick_b == expert
+            rows.append(jnp.where(by_a | by_b, 1.0, 0.0))
+            if e < experts:
+                k.slot_rows[s * experts + e : s * experts + e + 1, :] = jnp.where(
+                    by_a, slot_a, jnp.where(by_b, slot_b, -1)
+                )
+        chosen = jnp.concatenate(rows + [jnp.zeros((8 - total, length), F32)], axis=0)
+        k.chosen_rows[s] = chosen
+        if forward:
+            k.chosen_cols[s] = jnp.transpose(
+                jnp.concatenate([chosen, jnp.zeros((LANES - 8, length), F32)], axis=0)
+            )
+    rows = [
+        k.slot_rows[...].astype(F32),
+        jnp.zeros((8 - count, length), F32),
+        k.seg_row[...].astype(F32),
+        jnp.zeros((LANES - 9, length), F32),
+    ]
+    k.columns[...] = jnp.transpose(jnp.concatenate(rows, axis=0)).astype(jnp.int32)
+    router = k.router[...].astype(F32)
+    if sequences > 1:
+        turned = jnp.concatenate([router[experts:], router[:experts]], axis=0)
+        router = jnp.where(k.place.half == 1, turned, router)
+    k.router_rows[...] = jnp.zeros_like(k.router_rows)
+    k.router_rows[0:8, :] = jnp.concatenate(
+        [router, jnp.zeros((8 - total, router.shape[1]), F32)], axis=0
+    ).astype(BF16)
 
 
 def attention_forward(k):
@@ -361,6 +422,7 @@
     gather = TokenGather(place, normed, k.gather)
     normed[gather.rows(place.me), :] = normalise(k.x[...], k.gains[0:1, :]).astype(BF16)
     gather.start()
+    make_tables(k, True)
     k.at(1)
     k.weight(QKV)
     for owner in gather.arrivals():
@@ -373,7 +435,7 @@
     block = 128
     for offset in range(0, length, block):
         extent = offset + block
-        allowed = allowed_keys(k.seg_row, k.seg_col, offset, block, extent)
+        allowed = allowed_keys(k.seg_row[:, :extent], k.columns[offset:extent, 8:9], offset)
         for head in range(heads):
             first = head * HEAD
             query = turned[offset:extent, first : first + HEAD] * BF16(HEAD**-0.5)
@@ -418,7 +480,7 @@
         if offset % 256 == 0:
             k.at(11 + offset // 256)
         extent = offset + block
-        allowed = allowed_keys(k.seg_row, k.seg_col, offset, block, extent)
+        allowed = allowed_keys(k.seg_row[:, :extent], k.columns[offset:extent, 8:9], offset)
         for head in range(heads):
             own, key, value, out = (slice(n * wide + head * HEAD, n * wide + (head + 1) * HEAD) for n in range(4))
             query = turned[offset:extent, own] * BF16(HEAD**-0.5)
@@ -536,12 +598,16 @@
     units = k.w[SH].shape[-1] // 3
     wide = k.w[EX].shape[-1] // 3
 
-    def on_rows(s, rows):
+    def shared(s, rows):
         k.weight(SH)
         inner = nn(moe[s, rows, :], k.matrix(SH, 0, 2 * units))
         k.kept[SHARED][s, rows, :] = inner.astype(BF16)
-        branch[s, rows, :] = nt(hidden_of(inner), k.matrix(SH, 2 * units, 3 * units))
-        logits = nn(moe[s, rows, :], k.router[...])
+        return nt(hidden_of(inner), k.matrix(SH, 2 * units, 3 * units))
+
+    def on_rows(s, rows):
+        if not k.shared_last:
+            branch[s, rows, :] = shared(s, rows)
+        logits = nt(moe[s, rows, :], k.router_rows[...])
         k.gates[s, rows, :] = pick_softmax(logits, k.chosen_cols[s, rows, :], 1)
 
     scatters = [TokenScatter(place, refs) for refs in k.scatters]
@@ -560,42 +626,51 @@
             inner = nn(k.kept[ROUTED][e, slots, :], k.matrix(EX + e, 0, 2 * wide))
             k.kept[ACT][e, slots, :] = inner.astype(BF16)
             k.outs[first:last, :] = nt(hidden_of(inner), k.matrix(EX + e, 2 * wide, 3 * wide)).astype(BF16)
-        if e < experts - 1:
+        if e < experts - 1 or k.shared_last:
             for first in range(0, length, length // 2):
                 rows = slice(first, first + length // 2)
-                combine = tokens_by_slot(k.slot_cols[rows, index : index + 1])
-                branch[s, rows, :] += k.gates[s, rows, e : e + 1] * nn(combine, k.outs[...])
+                combine = tokens_by_slot(k.columns[rows, index : index + 1])
+                value = k.gates[s, rows, e : e + 1] * nn(combine, k.outs[...])
+                branch[s, rows, :] = value if k.shared_last and e == 0 else branch[s, rows, :] + value
             return
 
         def block_of(owner):
             rows = quarter_rows(length, owner)
-            combine = tokens_by_slot(k.slot_cols[rows, index : index + 1])
+            combine = tokens_by_slot(k.columns[rows, index : index + 1])
             return branch[s, rows, :] + k.gates[s, rows, e : e + 1] * nn(combine, k.outs[...])
 
         scatters[s].begin(block_of)
+
+    def shared_block(s, owner):
+        rows = quarter_rows(length, owner)
+        return branch[s, rows, :] + shared(s, rows)
 
     order = expert_order(sequences, experts)
 
     def between():
         for e in range(experts):
             dispatch(0, e)
-        k.gate_rows[0] = pick_softmax(nt(k.router_t[...], moe[0]), k.chosen_rows[0], 0)
+        k.gate_rows[0] = pick_softmax(nt(k.router_rows[0:8, :], moe[0]), k.chosen_rows[0], 0)
         expert(*order[0])
 
     both_arrivals(k, moe, on_rows, between, 8)
     k.local.start(moe, k.kept_out[MOE], True)
-    k.local.start(k.kept[SHARED], k.kept_out[SHARED], True)
     for step, (s, e) in enumerate(order[1:]):
         if s > 0:
             dispatch(s, e)
         expert(s, e)
         k.at(13 + step)
+    if k.shared_last:
+        for s in reversed(range(sequences)):
+            scatters[s].begin(functools.partial(shared_block, s))
+    k.local.start(k.kept[SHARED], k.kept_out[SHARED], True)
     for s in range(1, sequences):
-        k.gate_rows[s] = pick_softmax(nt(k.router_t[...], moe[s]), k.chosen_rows[s], 0)
+        k.gate_rows[s] = pick_softmax(nt(k.router_rows[0:8, :], moe[s]), k.chosen_rows[s], 0)
     k.local.start(k.kept[ROUTED], k.kept_out[ROUTED], True)
     k.local.start(k.kept[ACT], k.kept_out[ACT], True)
     if sequences > 1:
         returned = give_back(k, scatters[1].total())
+        k.at(16)
     following = k.mid[...] + scatters[0].total()
     if sequences > 1:
         returned.wait_recv()
@@ -621,6 +696,7 @@
     loads = {0: load_expert(0)}
     load_moe = k.local.start(k.kept_in[MOE], moe)
     k.early(QKV, PRJ)
+    make_tables(k, False)
     load_upstream.wait()
     up[0, quarter_rows(length, place.me), :] = k.grad[...].astype(BF16)
     units = k.w[SH].shape[-1] // 3
@@ -671,7 +747,7 @@
         if e < experts - 1:
             for first in range(0, length, length // 2):
                 rows = slice(first, first + length // 2)
-                combine = tokens_by_slot(k.slot_cols[rows, index : index + 1])
+                combine = tokens_by_slot(k.columns[rows, index : index + 1])
                 moe_grad[s, rows, :] += nn(combine, k.outs[...])
         else:
             gates = k.gate_rows[s]
@@ -683,8 +759,8 @@
 
             def block_of(owner):
                 rows = quarter_rows(length, owner)
-                combine = tokens_by_slot(k.slot_cols[rows, index : index + 1])
-                turned = tn(k.logit_grad[s, :, rows], k.router_t[...])
+                combine = tokens_by_slot(k.columns[rows, index : index + 1])
+                turned = tn(k.logit_grad[s, :, rows], k.router_rows[0:8, :])
                 return moe_grad[s, rows, :] + nn(combine, k.outs[...]) + turned
 
             scatters[s].begin(block_of)
@@ -710,6 +786,7 @@
     k.router_grad[...] = sum(nn(k.logit_grad[s], moe[s]) for s in range(sequences))
     if sequences > 1:
         returned = give_back(k, scatters[1].total())
+    k.at(18)
     total = scatters[0].total()
     if sequences > 1:
         returned.wait_recv()
@@ -785,6 +862,7 @@
         self.source, self.full = {}, {}
         self.z, self.x = {}, {}
         self.made, self.sums, self.totals = {}, {}, {}
+        self.own_sums, self.straight_on = set(), []
 
     def keys(self, layer, matrix):
         return [(layer, matrix, part) for part in range(len(self.parts[matrix]))]
@@ -803,8 +881,9 @@
     ins, outs, scratch = dict(ins), dict(outs), dict(scratch)
     dma, vmem = pltpu.SemaphoreType.DMA, pltpu.VMEM
     width = store.width
-    starts = [(kind, key) for _, kind, key, *end in plan if not end]
+    starts = [(kind, key) for _, kind, key, *taken in plan if not taken]
     starts += [(SUM_X, (layer, matrix)) for matrix in made if (layer, matrix) in store.own_sums]
+    starts += [(SUM_Z, key) for key in store.straight_on]
     keys = [[key for own, key in starts if own == kind] for kind in range(4)]
     keys_in = [key for matrix in weights for key in store.keys(layer, matrix)]
     ins["src"] = {key: Far(store.source[key[:2]]) for key in keys[GET_Z]}
@@ -834,7 +913,7 @@
     scratch["sems"] = {
         GET_Z: {key: [dma((4,)), dma((4,)), dma((1,))] for key in keys[GET_Z]},
         GET_X: {key: [dma((1,)), dma((1,))] for key in keys[GET_X]},
-        SUM_X: {key: [dma((1,)), dma((1,)), dma((2,))] for key in keys[SUM_X]},
+        SUM_X: {key: [dma((4,)), dma((4,)), dma((2,))] for key in keys[SUM_X]},
         SUM_Z: {key: [dma((4,)), dma((4,)), dma((1,))] for key in keys[SUM_Z]},
     }
     scratch["blocks"] = {key: vmem(block_shape(key), BF16) for key in keys[SUM_X]}
@@ -854,12 +933,18 @@
             at += len(flat)
         place = k.place = Place()
         k.local = Local(k.lsem)
+        k.layer = layer
+        k.shared_last = store.paired and layer == 0
         peers = place.greet_sequence() if tokens else []
         if around:
             peers += place.greet_all()
         elif store.paired:
             peers += [place.partner()]
         place.greet(peers)
+        k.exchange = hasattr(k, "news")
+        if k.exchange:
+            k.picks_sent = send(k.picks[0], k.news, k.news_send.at[0], k.news_recv.at[0], place.partner())
+            k.picks = [k.picks[0], k.news]
 
         def job(kind, key):
             sems = k.sems[kind][key]
@@ -870,15 +955,18 @@
                 return Aside(place, source, k.x_out[key], sems)
             if kind == SUM_X:
                 source = k.made_in[key] if key in k.made_in else k.w[key[1]]
-                return AsideSum(place, source, k.own.get(key), k.blocks[key], k.sums_out.get(key), sems)
+                onward = None
+                if key in k.lands:
+                    onward = running[SUM_Z, key] = job(SUM_Z, key)
+                return AsideSum(place, source, k.own.get(key), k.blocks[key], k.sums_out.get(key), onward, sems)
             source = k.blocks[key] if key in k.blocks else k.sums_in[key]
             return StraightSum(place, source, k.lands[key], k.totals[key], sems)
 
         running, ended = {}, set()
 
         def start(kind, key):
-            running[kind, key] = job(kind, key)
-            running[kind, key].start()
+            transfer = running[kind, key] = job(kind, key)
+            transfer.start()
 
         def end(kind, key):
             if (kind, key) not in ended:
@@ -886,9 +974,13 @@
                 running[kind, key].arrived()
 
         def at_point(point):
-            for own, kind, key, *is_end in plan:
-                if own == point:
-                    (end if is_end else start)(kind, key)
+            for own, kind, key, *taken in plan:
+                if own != point:
+                    continue
+                if kind == SUM_X and taken:
+                    running[kind, key].take(*taken)
+                else:
+                    (end if taken else start)(kind, key)
 
         loads, loaded = {}, set()
 
@@ -958,7 +1050,7 @@
         k.put_product = put_product
         at_point(0)
         body(k)
-        for kind, key in running:
+        for kind, key in sorted(running):
             end(kind, key)
         for transfer in running.values():
             transfer.close()
@@ -984,29 +1076,147 @@
     return result
 
 
+def plain(body, outs, *arrays):
+    near = pl.BlockSpec(memory_space=pltpu.VMEM)
+    return pl.pallas_call(
+        body,
+        out_shape=[jax.ShapeDtypeStruct(out.shape, out.kind) for out in outs],
+        in_specs=[near] * len(arrays),
+        out_specs=[near] * len(outs),
+        compiler_params=pltpu.CompilerParams(vmem_limit_bytes=VMEM_LIMIT),
+    )(*arrays)
+
+
+def turned_over(value):
+    return jnp.transpose(value.astype(F32))
+
+
+def pack_all(attention, projection, widening, narrowing, expansion, contraction, experts, shared_units):
+    layers, _, height, wide = attention.shape
+    units = widening.shape[3]
+    keys, outs = [], []
+    for layer in range(layers):
+        shapes = {QKV: (height, 3 * wide), PRJ: (height, wide), SH: (2, height, 3 * shared_units)}
+        shapes |= {EX + e: (2, height, 3 * units) for e in range(experts)}
+        keys += [(layer, matrix) for matrix in shapes]
+        outs += [Out(shape, BF16) for shape in shapes.values()]
+
+    def body(att, prj, wid, nar, exp, con, *results):
+        results = dict(zip(keys, results, strict=True))
+        for layer in range(layers):
+            for n in range(3):
+                results[layer, QKV][:, n * wide : (n + 1) * wide] = att[layer, n]
+            results[layer, PRJ][...] = turned_over(prj[layer]).astype(BF16)
+            for half in range(2):
+                cut = slice(half * shared_units, (half + 1) * shared_units)
+                shared = results[layer, SH]
+                shared[half, :, : 2 * shared_units] = jnp.concatenate([wid[layer, n, :, cut] for n in range(2)], axis=1)
+                shared[half, :, 2 * shared_units :] = nar[layer, :, cut]
+                for e in range(experts):
+                    whole, given = results[layer, EX + e], half * experts + e
+                    for n in range(2):
+                        whole[half, :, n * units : (n + 1) * units] = exp[layer, given, n]
+                    whole[half, :, 2 * units :] = con[layer, given]
+
+    narrowing, contraction = jnp.swapaxes(narrowing, 1, 2), jnp.swapaxes(contraction, 2, 3)
+    results = plain(body, outs, attention, projection, widening, narrowing, expansion, contraction)
+    return dict(zip(keys, results, strict=True))
+
+
+def unpack_all(current, upstream, small, totals, layers, all_experts, experts, shared_units, units, wide):
+    width = current.shape[1]
+    height = totals[0, QKV][0].shape[0]
+    keys = sorted(totals)
+    counts = [len(totals[key]) for key in keys]
+    outs = [
+        Out(current.shape),
+        Out(upstream.shape),
+        Out((layers, 2, width)),
+        Out((layers, 3, height, wide)),
+        Out((layers, wide, height)),
+        Out((layers, all_experts, width)),
+        Out((layers, 2, height, units)),
+        Out((layers, height, units)),
+        Out((layers, all_experts, 2, height, units)),
+        Out((layers, all_experts, height, units)),
+    ]
+
+    def body(*refs):
+        now, up, sums = refs[:3]
+        parts, at = {}, 3
+        for key, count in zip(keys, counts, strict=True):
+            parts[key] = refs[at : at + count]
+            at += count
+        now_out, up_out, gains, att, prj, router, wid, nar, exp, con = refs[at:]
+        upper = Place().half == 1
+        now_out[...] = now[...]
+        up_out[...] = up[...]
+
+        def halves(key):
+            mine, theirs = (part[...].astype(F32) for part in parts[key])
+            return jnp.where(upper, theirs, mine), jnp.where(upper, mine, theirs)
+
+        for layer in range(layers):
+            gains[layer] = sums[2 * layer : 2 * layer + 2, :]
+            router[layer] = sums[8 * layer + 8 : 8 * layer + 8 + all_experts, :]
+            whole = parts[layer, QKV][0]
+            for n in range(3):
+                att[layer, n] = whole[:, n * wide : (n + 1) * wide].astype(F32)
+            prj[layer] = turned_over(parts[layer, PRJ][0][...])
+            for half, value in enumerate(halves((layer, SH))):
+                cut = slice(half * shared_units, (half + 1) * shared_units)
+                for n in range(2):
+                    wid[layer, n, :, cut] = value[:, n * shared_units : (n + 1) * shared_units]
+                nar[layer, :, cut] = value[:, 2 * shared_units :]
+            for e in range(experts):
+                for half, value in enumerate(halves((layer, EX + e))):
+                    for n in range(2):
+                        exp[layer, half * experts + e, n] = value[:, n * units : (n + 1) * units]
+                    con[layer, half * experts + e] = value[:, 2 * units :]
+
+    arrays = [current, upstream, small, *(part for key in keys for part in totals[key])]
+    now, up, gains, att, prj, router, wid, nar, exp, con = plain(body, outs, *arrays)
+    return now, up, gains, att, prj, jnp.swapaxes(router, 1, 2), wid, jnp.swapaxes(nar, 1, 2), exp, jnp.swapaxes(con, 2, 3)
+
+
 def forward_plan(store, layer, last):
-    qkv, (prj,), (sh,) = (store.keys(layer, matrix) for matrix in (QKV, PRJ, SH))
+    qkv, (prj,), sh = (store.keys(layer, matrix) for matrix in (QKV, PRJ, SH))
     low, high = store.keys(layer, EX), store.keys(layer, EX + 1)
 
     def pass_on(point, *keys):
         return [step for key in keys for step in ((point, GET_Z, key, True), (point, GET_X, key))]
 
     if layer == 0:
-        plan = [(0, GET_Z, key) for key in (*qkv, prj, sh, *low)]
-        plan += pass_on(1, *qkv) + pass_on(2, prj) + pass_on(6, sh) + pass_on(7, low[0]) + pass_on(8, low[1])
-        plan += [(8, GET_Z, key) for key in high] + pass_on(9, low[2])
+        plan = [(0, GET_Z, key) for key in (*qkv, prj, *low)]
+        plan += pass_on(1, *qkv) + pass_on(2, prj) + [(2, GET_Z, high[0])]
+        plan += pass_on(5, low[0]) + pass_on(7, low[1]) + pass_on(8, low[2])
+        plan += [(8, GET_Z, key) for key in (*high[1:], *sh)]
+        plan += pass_on(9, high[0]) + pass_on(11, high[1]) + pass_on(12, high[2]) + pass_on(13, sh[0]) + pass_on(14, sh[1])
     else:
-        plan = [(0, GET_X, sh)] + [(0, GET_Z, key) for key in (*low, high[0])]
-        plan += pass_on(3, low[0]) + pass_on(4, low[1]) + pass_on(7, low[2]) + pass_on(8, high[0])
-        plan += [(8, GET_Z, key) for key in high[1:]]
+        plan = [(0, GET_X, low[0])] + [(0, GET_Z, key) for key in (*low[1:], *high)]
+        plan += pass_on(2, low[1]) + pass_on(4, low[2]) + pass_on(7, high[0]) + pass_on(8, high[1]) + pass_on(9, high[2])
     if layer < last:
-        qkv, (prj,), (sh,) = (store.keys(layer + 1, matrix) for matrix in (QKV, PRJ, SH))
-        plan += [(8, GET_Z, key) for key in (*qkv, prj, sh)] + pass_on(15, *qkv, prj)
+        qkv, (prj,), sh = (store.keys(layer + 1, matrix) for matrix in (QKV, PRJ, SH))
+        early = store.keys(layer + 1, EX)[0]
+        plan += [(8, GET_Z, key) for key in (*qkv, prj, *sh)] + [(12, GET_Z, early)]
+        plan += pass_on(15, *qkv, prj) + pass_on(16, *sh)
+    return plan
+
+
+def backward_plan(layer, last):
+    sh, low, high, prj, qkv = ((layer, matrix) for matrix in (SH, EX, EX + 1, PRJ, QKV))
+    plan = [(7, SUM_X, sh, 2), (8, SUM_X, sh, 2), (18, SUM_X, low, 2), (10, SUM_X, low, 1), (11, SUM_X, low, 1)]
+    own, onward = [sh, low, high], [sh, low]
+    if layer < last:
+        above = [(layer + 1, PRJ), (layer + 1, QKV)]
+        plan += [(0, SUM_X, key) for key in above] + [(1, SUM_Z, (layer + 1, EX + 1))]
+        plan += [(6, SUM_X, key, 4) for key in above]
+        onward += above
     if layer == 0:
-        plan += pass_on(11, high[0]) + pass_on(12, high[1]) + pass_on(13, high[2])
-    else:
-        plan += pass_on(11, high[1]) + pass_on(12, high[2])
-    return plan
+        plan += [(12, SUM_X, high, 1), (14, SUM_X, high, 1), (15, SUM_X, high, 2), (16, SUM_X, prj, 4)]
+        plan += [(17, SUM_X, qkv, 4)]
+        own, onward = [*own, prj, qkv], [*onward, high, prj, qkv]
+    return plan, own, onward
 
 
 def on_device(
@@ -1026,70 +1236,38 @@
     sequences = 2 if paired else 1
     experts = all_experts // sequences
     shared_units = units // sequences
-    dp = lax.axis_index("dp")
-    upper = (dp // 2) % 2 == 1
-
-    halfway = HEAD // 2
-    inverse = jnp.exp(jnp.arange(halfway, dtype=F32) * (-2.0 * math.log(10000.0) / HEAD))
-    phases = jnp.arange(length, dtype=F32)[:, None] * inverse[None, :]
-    cosine, sine = jnp.cos(phases), jnp.sin(phases)
-    cosine = jnp.concatenate([cosine] * 4, axis=1)
-    sine = jnp.concatenate([-sine, sine] * 2, axis=1)
-    places = dict(cosine=cosine, sine=sine, seg_row=segment[None, :], seg_col=segment[:, None])
-
-    def local_first(values, axis):
-        if not paired:
-            return values
-        return jnp.where(upper, jnp.roll(values, -experts, axis), values)
-
-    picks = jnp.concatenate([expert_pick, slot_index], axis=2)[:, None]
-    if paired:
-        swap = [(at, (at // 4) * 4 + (at % 4 + 2) % 4) for at in range(ring)]
-        picks = jnp.concatenate([picks, lax.ppermute(picks, "dp", swap)], axis=1)
-    expert_of, slot_of = picks[..., :2], picks[..., 2:]
-    held = expert_of[..., None] == jnp.arange(all_experts, dtype=jnp.int32)
-    slots = local_first(jnp.sum(jnp.where(held, slot_of[..., None] + 1, 0), axis=3) - 1, 3)
-    chosen = local_first(jnp.any(held, axis=3).astype(F32), 3)
-    slots = slots[..., :experts]
-    slot_rows = jnp.swapaxes(slots, 2, 3).reshape(layers, sequences * experts, length)
-    slot_cols = jnp.swapaxes(slots, 1, 2).reshape(layers, length, sequences * experts)
-    chosen_cols = jnp.pad(chosen, ((0, 0), (0, 0), (0, 0), (0, LANES - all_experts)))
-    chosen_rows = jnp.pad(jnp.swapaxes(chosen, 2, 3), ((0, 0), (0, 0), (0, 8 - all_experts), (0, 0)))
-    router_own = local_first(router, 2)
-    router_wide = jnp.pad(router_own, ((0, 0), (0, 0), (0, LANES - all_experts)))
-    router_t = jnp.pad(jnp.swapaxes(router_own, 1, 2), ((0, 0), (0, 8 - all_experts), (0, 0)))
-
-    projection_t = jnp.swapaxes(projection, 1, 2)
-    narrowing_t = jnp.swapaxes(narrowing, 1, 2)
-    contraction_t = jnp.swapaxes(contraction, 2, 3)
+    inverse = np.exp(np.arange(HEAD // 2, dtype=np.float32) * np.float32(-2.0 * math.log(10000.0) / HEAD))
+    phases = np.arange(length, dtype=np.float32)[:, None] * inverse[None, :]
+    cosine, sine = np.cos(phases), np.sin(phases)
+    places = dict(
+        cosine=jnp.asarray(np.concatenate([cosine] * 4, axis=1)),
+        sine=jnp.asarray(np.concatenate([-sine, sine] * 2, axis=1)),
+        seg_row=segment[None, :],
+    )
+    picks = [jnp.swapaxes(jnp.concatenate([expert_pick, slot_index], axis=2), 1, 2).reshape(4 * layers, length)]
+    router_rows = jnp.swapaxes(router, 1, 2)
+
     columns = {QKV: 3 * wide, PRJ: wide, SH: 3 * shared_units} | {EX + e: 3 * units for e in range(experts)}
     parts = {matrix: [(0, height)] for matrix in columns}
     if paired:
         third = height // 3
         parts[QKV] = parts[EX] = [(at, third) for at in (0, third, 2 * third)]
+        parts[SH] = [(0, height // 2), (height // 2, height - height // 2)]
         parts[EX + 1] = [(0, height // 2), (height // 2, third), (height // 2 + third, height - height // 2 - third)]
     store = Store(height, width, columns, parts, paired)
-    for layer in range(layers):
-        store.source[layer, QKV] = jnp.concatenate([*attention[layer]], axis=-1)
-        store.source[layer, PRJ] = projection_t[layer]
-        thirds = (widening[layer, 0], widening[layer, 1], narrowing_t[layer])
-        whole = [
-            jnp.concatenate([expansion[layer, e, 0], expansion[layer, e, 1], contraction_t[layer, e]], axis=-1)
-            for e in range(all_experts)
-        ]
-        if paired:
-            store.source[layer, SH] = jnp.stack(
-                [
-                    jnp.concatenate([third[:, a * shared_units : (a + 1) * shared_units] for third in thirds], axis=-1)
-                    for a in range(2)
-                ]
-            )
+    if paired:
+        store.source = pack_all(
+            attention, projection, widening, narrowing, expansion, contraction, experts, shared_units
+        )
+    else:
+        whole = jnp.concatenate([expansion[:, :, 0], expansion[:, :, 1], jnp.swapaxes(contraction, 2, 3)], axis=-1)
+        shared = jnp.concatenate([widening[:, 0], widening[:, 1], jnp.swapaxes(narrowing, 1, 2)], axis=-1)
+        for layer in range(layers):
+            store.source[layer, QKV] = jnp.concatenate([*attention[layer]], axis=-1)
+            store.source[layer, PRJ] = projection[layer].T
+            store.source[layer, SH] = shared[layer]
             for e in range(experts):
-                store.source[layer, EX + e] = jnp.stack([whole[e], whole[experts + e]])
-        else:
-            store.source[layer, SH] = jnp.concatenate(thirds, axis=-1)
-            for e in range(experts):
-                store.source[layer, EX + e] = whole[e]
+                store.source[layer, EX + e] = whole[layer, e]
     if not paired:
         store.full = {
             key: lax.all_gather(source, "dp", axis=0, tiled=True)[None, None] for key, source in store.source.items()
@@ -1124,7 +1302,17 @@
     def kept_outs(shapes):
         return {name: Out(shape, BF16, True) for name, shape in shapes.items()}
 
-    store.own_sums = set()
+    tables = dict(
+        slot_rows=vmem((sequences * experts, length), jnp.int32),
+        chosen_rows=vmem((sequences, 8, length), F32),
+        columns=vmem((length, LANES), jnp.int32),
+        router_rows=vmem((LANES, width), BF16),
+    )
+    news = dict(
+        news=vmem((4 * layers, length), jnp.int32),
+        news_send=pltpu.SemaphoreType.DMA((1,)),
+        news_recv=pltpu.SemaphoreType.DMA((1,)),
+    )
     saved = []
     current = stream
     next_id = 0
@@ -1136,12 +1324,8 @@
             dict(
                 x=current,
                 gains=norm_gains[layer],
-                router=router_wide[layer],
-                router_t=router_t[layer],
-                slot_rows=slot_rows[layer],
-                slot_cols=slot_cols[layer],
-                chosen_rows=chosen_rows[layer],
-                chosen_cols=chosen_cols[layer],
+                router=router_rows[layer],
+                picks=picks,
                 **places,
             ),
             dict(
@@ -1149,8 +1333,12 @@
                 following=rows_out,
                 gate_rows=Out((sequences, 8, length)),
                 kept_out=kept_outs(attention_shapes | ffn_shapes),
+                **(dict(picks_out=Out((4 * layers, length), jnp.int32)) if len(picks) < sequences else {}),
             ),
             dict(
+                chosen_cols=vmem((sequences, length, LANES), F32),
+                **tables,
+                **(news if len(picks) < sequences else {}),
                 kept=kept_scratch(attention_shapes | ffn_shapes),
                 branch=vmem((sequences, length, width), F32),
                 outs=vmem((CAP, width), BF16),
@@ -1163,6 +1351,8 @@
             [QKV, PRJ, *ffn_matrices],
             plan=forward_plan(store, layer, last) if paired else (),
         )
+        if len(picks) < sequences:
+            picks = [*picks, result.picks_out]
         saved.append((current, result.mid, result.kept_out, result.gate_rows))
         current = result.following
         next_id += 1
@@ -1171,35 +1361,22 @@
     parts_small = [None] * layers
     for layer in reversed(range(layers)):
         x_in, mid, kept, gate_rows = saved[layer]
-        plan = [
-            (8, SUM_X, (layer, SH), True), (8, SUM_Z, (layer, SH)), (11, SUM_X, (layer, EX), True), (11, SUM_Z, (layer, EX))
-        ]
-        made = [SH, EX, EX + 1]
-        if layer < last:
-            above = [(layer + 1, PRJ), (layer + 1, QKV)]
-            plan += [(0, SUM_X, key) for key in above] + [(1, SUM_Z, (layer + 1, EX + 1))]
-            plan += [step for key in above for step in ((6, SUM_X, key, True), (6, SUM_Z, key))]
         finish = paired and layer == 0
-        if finish:
-            made += [PRJ, QKV]
-            plan += [(15, SUM_X, (0, EX + 1), True), (15, SUM_Z, (0, EX + 1))]
-            plan += [step for m in (PRJ, QKV) for step in ((17, SUM_X, (0, m), True), (17, SUM_Z, (0, m)))]
-        store.own_sums = {(layer, matrix) for matrix in made} if paired else set()
+        plan, store.own_sums, store.straight_on = backward_plan(layer, last) if paired else ((), (), ())
         ins = dict(
             upstream=Far(upstream),
             x=Far(x_in),
             mid=Far(mid),
             gains=norm_gains[layer],
-            router_t=router_t[layer],
-            slot_rows=slot_rows[layer],
-            slot_cols=slot_cols[layer],
-            chosen_rows=chosen_rows[layer],
+            router=router_rows[layer],
+            picks=picks,
             gate_rows=gate_rows,
             kept_in={name: Far(array) for name, array in kept.items()},
             **places,
         )
         outs = dict(grad=rows_out, gain_att=gain_out, gain_ffn=gain_out, router_grad=Out((8, width)))
         work = dict(
+            **tables,
             kept={
                 MOE: vmem((sequences, length, width), BF16),
                 SHARED: vmem((sequences, length, 2 * shared_units), BF16),
@@ -1247,62 +1424,35 @@
         next_id += 1
 
     if paired:
-        gains_grad = result.small_sum[: 2 * layers].reshape(layers, 2, width)
-        router_grad = result.small_sum[8:].reshape(layers, 8, width)[:, :all_experts]
-    else:
-        gains_grad, router_grad = lax.psum(
-            (
-                jnp.stack([jnp.concatenate(part[:2], axis=0) for part in parts_small]),
-                jnp.stack([part[2][:all_experts] for part in parts_small]),
-            ),
-            ("dp", "tensor"),
+        return unpack_all(
+            current, upstream, result.small_sum, store.totals, layers, all_experts, experts, shared_units, units, wide
         )
-        store.totals = {
-            key: [lax.psum_scatter(part[0, 0], "dp", scatter_dimension=0, tiled=True).astype(F32)]
-            for key, part in store.made.items()
-        }
-
-    def split(pieces):
-        mine, theirs = pieces
-        return jnp.where(upper, theirs, mine), jnp.where(upper, mine, theirs)
-
-    attention_grad, projection_grad, widening_grad, narrowing_grad, expansion_grad, contraction_grad = (
-        [] for _ in range(6)
+    gains_grad, router_grad = lax.psum(
+        (
+            jnp.stack([jnp.concatenate(part[:2], axis=0) for part in parts_small]),
+            jnp.stack([part[2][:all_experts] for part in parts_small]),
+        ),
+        ("dp", "tensor"),
     )
-    for layer in range(layers):
-        totals = {matrix: [part.astype(F32) for part in store.totals[layer, matrix]] for matrix in columns}
-        (whole,) = totals[QKV]
-        attention_grad.append(jnp.stack([whole[:, n * wide : (n + 1) * wide] for n in range(3)]))
-        projection_grad.append(totals[PRJ][0].T)
-        if paired:
-            halves = split(totals[SH])
-            shared = [
-                jnp.concatenate([half[:, n * shared_units : (n + 1) * shared_units] for half in halves], axis=1)
-                for n in range(3)
-            ]
-            by_expert = [split(totals[EX + e]) for e in range(experts)]
-            wholes = [by_expert[e][a] for a in range(2) for e in range(experts)]
-        else:
-            (whole,) = totals[SH]
-            shared = [whole[:, n * units : (n + 1) * units] for n in range(3)]
-            wholes = [totals[EX + e][0] for e in range(experts)]
-        widening_grad.append(jnp.stack(shared[:2]))
-        narrowing_grad.append(shared[2].T)
-        expansion_grad.append(
-            jnp.stack([jnp.stack([one[:, :units], one[:, units : 2 * units]]) for one in wholes])
-        )
-        contraction_grad.append(jnp.stack([one[:, 2 * units :].T for one in wholes]))
+    totals = {
+        key: lax.psum_scatter(part[0, 0], "dp", scatter_dimension=0, tiled=True).astype(F32)
+        for key, part in store.made.items()
+    }
+    att = jnp.stack([totals[layer, QKV] for layer in range(layers)])
+    prj = jnp.stack([totals[layer, PRJ] for layer in range(layers)])
+    shared = jnp.stack([totals[layer, SH] for layer in range(layers)])
+    whole = jnp.stack([jnp.stack([totals[layer, EX + e] for e in range(experts)]) for layer in range(layers)])
     return (
         current,
         upstream,
         gains_grad,
-        jnp.stack(attention_grad),
-        jnp.stack(projection_grad),
+        jnp.stack([att[..., n * wide : (n + 1) * wide] for n in range(3)], axis=1),
+        jnp.swapaxes(prj, 1, 2),
         jnp.swapaxes(router_grad, 1, 2),
-        jnp.stack(widening_grad),
-        jnp.stack(narrowing_grad),
-        jnp.stack(expansion_grad),
-        jnp.stack(contraction_grad),
+        jnp.stack([shared[..., n * units : (n + 1) * units] for n in range(2)], axis=1),
+        jnp.swapaxes(shared[..., 2 * units :], 1, 2),
+        jnp.stack([whole[..., n * units : (n + 1) * units] for n in range(2)], axis=2),
+        jnp.swapaxes(whole[..., 2 * units :], 2, 3),
     )
 
 

time: 612 us -> 559 us (0.913)
  local copies, waits for them, and re-layouts: 24.9 us -> 3.24 us
  other arithmetic: 21.4 us -> 0.75 us
    pallas_call x4, Pallas kernels: 551 us -> 535 us  [call(): pl.pallas_call(kernel, out_shape=[jax.ShapeDtypeStruct(out.shape, out.kin...]
    another operation x45 -> x0, other arithmetic: 12.7 us -> none  [the longest x12 3.64 us: on_device(): store.source[layer, EX + e] = jnp.stack([whole[e], whole[experts + e]])]
    pallas_call x0 -> x2, Pallas kernels: none -> 9.64 us  [plain(): pl.pallas_call(body, out_shape=[jax.ShapeDtypeStruct(out.shape, out.kind)...]
    squeeze x19 -> x1, local copies, waits for them, and re-layouts: 10.9 us -> 1.31 us  [on_device(): router_rows[layer]]
    unnamed x44 -> x0, local copies, waits for them, and re-layouts: 6.32 us -> none
  transfers between devices with their start and end apart: 1 -> 0, of which waited for: 0 -> 0; matrix products, arithmetic and copies ran while one was open for 3% -> 0% of each run, Pallas kernels for 0% -> 0%
where the time goes in v4:
time: 559 us; the launch traced here: 550 us
  Pallas kernels  545 us (97%)
    pallas_call x4, Pallas kernels, call(): pl.pallas_call(kernel, out_shape=[jax.ShapeDtypeStruct(out.shape, out.kin...  535 us

profile of v4, /device:TPU:0, one launch (start us, length us, event | category | flops | bytes accessed | tf_op | source)
XLA Modules:
  0.0 550.1 jit_solution(1928289826104360720)
XLA Ops:
  0.6 1.3 slice_bitcast_fusion.2
  1.9 1.3 slice_bitcast_fusion
  3.3 0.8 add_bitcast_fusion
  4.0 0.6 reshape.23.refs_2_.refs_10_.refs_15_
  4.6 3.8 shard_map.222
  8.4 147.3 %shard_map.223 = (f32[256,768]{1,0:T(8,128)}, f32[2,8,1024]{2,1,0:T(8,128)}, bf16[1024,768]{1,0:T(8,128)(2,1)}, bf16[1024,768]{1,0:T(8,128)(2,1)}, bf16[2,1024,7...) custom-call(f32[1024,128]{1,0:T(8,128)} %constant.4.clone.refs_0_, ...), custom_call_target="tpu_custom_call" | custom-call | tf_op jit(solution)/shard_map/pallas_call | solution.py:1060
  155.7 108.9 %shard_map.224 = (f32[256,768]{1,0:T(8,128)}, f32[2,8,1024]{2,1,0:T(8,128)}, bf16[1024,768]{1,0:T(8,128)(2,1)}, bf16[1024,768]{1,0:T(8,128)(2,1)}, bf16[2,1024,7...) custom-call(f32[1024,128]{1,0:T(8,128)} %constant.4.clone.refs_0_, ...), custom_call_target="tpu_custom_call" | custom-call | tf_op jit(solution)/shard_map/pallas_call | solution.py:1060
  264.6 126.5 %shard_map.225 = (f32[1,768]{1,0:T(1,128)}, f32[1,768]{1,0:T(1,128)}, f32[256,768]{1,0:T(8,128)}, bf16[4,2,96,576]{3,2,1,0:T(8,128)(2,1)}, bf16[4,2,96,192]{3,2,...) custom-call(f32[1024,128]{1,0:T(8,128)} %constant.4.clone.refs_0_, ...), custom_call_target="tpu_custom_call" | custom-call | tf_op jit(solution)/shard_map/pallas_call | solution.py:1060
  391.2 152.6 %shard_map.226 = (f32[1,768]{1,0:T(1,128)}, f32[1,768]{1,0:T(1,128)}, f32[256,768]{1,0:T(8,128)}, f32[8,768]{1,0:T(8,128)}, f32[24,768]{1,0:T(8,128)}, /*index=5...) custom-call(f32[1024,128]{1,0:T(8,128)} %constant.4.clone.refs_0_, ...), custom_call_target="tpu_custom_call" | custom-call | tf_op jit(solution)/shard_map/pallas_call | solution.py:1060
  543.8 5.9 %shard_map.227 = (f32[256,768]{1,0:T(8,128)}, f32[256,768]{1,0:T(8,128)}, f32[2,2,768]{2,1,0:T(2,128)}, f32[2,3,96,192]{3,2,1,0:T(8,128)}, f32[2,192,96]{2,1,0:T...) custom-call(f32[256,768]{1,0:T(8,128)} %get-tuple-element.147.refs_0, ...), custom_call_target="tpu_custom_call" | custom-call | tf_op jit(solution)/shard_map/pallas_call | solution.py:1081

commit v5 on v4

--- a/solution.py
+++ b/solution.py
@@ -374,7 +374,7 @@
     experts, length = k.slot_rows.shape[0] // sequences, k.slot_rows.shape[1]
     count = sequences * experts
     total = k.router.shape[0]
-    if k.exchange:
+    if k.exchange and k.layer == 0:
         k.picks_sent.wait()
         k.picks_out[...] = k.picks[1][...]
     first = experts * k.place.half if sequences > 1 else 0
@@ -420,7 +420,7 @@
     normed, turned = k.kept[NRM], k.kept[TURNED]
     k.early(QKV, PRJ)
     gather = TokenGather(place, normed, k.gather)
-    normed[gather.rows(place.me), :] = normalise(k.x[...], k.gains[0:1, :]).astype(BF16)
+    normed[gather.rows(place.me), :] = normalise(k.x_in[...], k.gains_now[0:1, :]).astype(BF16)
     gather.start()
     make_tables(k, True)
     k.at(1)
@@ -430,7 +430,7 @@
         projected = nn(normed[rows, :], k.matrix(QKV, 0, 3 * wide))
         turned[rows, : 2 * wide] = turn(projected[:, : 2 * wide], k.cosine[rows, :], k.sine[rows, :]).astype(BF16)
         turned[rows, 2 * wide : 3 * wide] = projected[:, 2 * wide :].astype(BF16)
-    k.local.start(normed, k.kept_out[NRM], True)
+    k.keep(NRM)
     k.at(2)
     block = 128
     for offset in range(0, length, block):
@@ -445,12 +445,12 @@
             turned[offset:extent, 3 * wide + first : 3 * wide + first + HEAD] = nn(probability, values).astype(BF16)
         if extent % 256 == 0:
             k.at(2 + extent // 256)
-    k.local.start(turned, k.kept_out[TURNED], True)
+    k.keep(TURNED)
     scatter = TokenScatter(place, k.scatter)
     k.weight(PRJ)
     scatter.begin(lambda owner: nt(turned[quarter_rows(length, owner), 3 * wide :], k.matrix(PRJ, 0, wide)))
     k.at(7)
-    k.mid[...] = k.x[...] + scatter.total()
+    k.mid_now[...] = k.x_in[...] + scatter.total()
 
 
 def attention_backward(k):
@@ -594,7 +594,7 @@
     place = k.place
     moe, branch = k.kept[MOE], k.branch
     k.early(SH, *(EX + e for e in range(experts)))
-    moe[0, quarter_rows(length, place.me), :] = normalise(k.mid[...], k.gains[1:2, :]).astype(BF16)
+    moe[0, quarter_rows(length, place.me), :] = normalise(k.mid_now[...], k.gains_now[1:2, :]).astype(BF16)
     units = k.w[SH].shape[-1] // 3
     wide = k.w[EX].shape[-1] // 3
 
@@ -639,6 +639,8 @@
             combine = tokens_by_slot(k.columns[rows, index : index + 1])
             return branch[s, rows, :] + k.gates[s, rows, e : e + 1] * nn(combine, k.outs[...])
 
+        if s == 0:
+            k.settle()
         scatters[s].begin(block_of)
 
     def shared_block(s, owner):
@@ -650,11 +652,11 @@
     def between():
         for e in range(experts):
             dispatch(0, e)
-        k.gate_rows[0] = pick_softmax(nt(k.router_rows[0:8, :], moe[0]), k.chosen_rows[0], 0)
+        k.gates_out[0] = pick_softmax(nt(k.router_rows[0:8, :], moe[0]), k.chosen_rows[0], 0)
         expert(*order[0])
 
     both_arrivals(k, moe, on_rows, between, 8)
-    k.local.start(moe, k.kept_out[MOE], True)
+    k.keep(MOE)
     for step, (s, e) in enumerate(order[1:]):
         if s > 0:
             dispatch(s, e)
@@ -662,21 +664,24 @@
         k.at(13 + step)
     if k.shared_last:
         for s in reversed(range(sequences)):
+            if s == 0:
+                k.settle()
             scatters[s].begin(functools.partial(shared_block, s))
-    k.local.start(k.kept[SHARED], k.kept_out[SHARED], True)
+    k.keep(SHARED)
     for s in range(1, sequences):
-        k.gate_rows[s] = pick_softmax(nt(k.router_rows[0:8, :], moe[s]), k.chosen_rows[s], 0)
-    k.local.start(k.kept[ROUTED], k.kept_out[ROUTED], True)
-    k.local.start(k.kept[ACT], k.kept_out[ACT], True)
+        k.gates_out[s] = pick_softmax(nt(k.router_rows[0:8, :], moe[s]), k.chosen_rows[s], 0)
+    k.keep(ROUTED)
+    k.keep(ACT)
     if sequences > 1:
         returned = give_back(k, scatters[1].total())
         k.at(16)
-    following = k.mid[...] + scatters[0].total()
+    following = k.mid_now[...] + scatters[0].total()
     if sequences > 1:
         returned.wait_recv()
         following = following + k.pair_land[...].astype(F32)
         returned.wait_send()
-    k.following[...] = following
+    k.following_now[...] = following
+    k.settle()
 
 
 def ffn_backward(k):
@@ -797,9 +802,15 @@
     k.grad[...] += inward
 
 
-def layer_forward(k):
-    attention_forward(k)
-    ffn_forward(k)
+def forward(k):
+    for layer in range(len(k.gains)):
+        k.layer, k.base = layer, 20 * layer
+        k.shared_last = k.sharing and layer == 0
+        k.gains_now, k.router = k.gains[layer], k.routers[layer]
+        k.x_in = k.following[layer - 1] if layer else k.x
+        k.mid_now, k.following_now, k.gates_out = k.mid[layer], k.following[layer], k.gate_rows[layer]
+        attention_forward(k)
+        ffn_forward(k)
 
 
 def layer_backward(k):
@@ -877,17 +888,18 @@
     return not isinstance(value, (dict, list))
 
 
-def call(store, body, collective_id, ins, outs, scratch, layer, weights=(), made=(), plan=(), tokens=True):
+def call(store, body, collective_id, ins, outs, scratch, layers, weights=(), made=(), plan=()):
     ins, outs, scratch = dict(ins), dict(outs), dict(scratch)
+    layer = layers[0]
     dma, vmem = pltpu.SemaphoreType.DMA, pltpu.VMEM
     width = store.width
     starts = [(kind, key) for _, kind, key, *taken in plan if not taken]
     starts += [(SUM_X, (layer, matrix)) for matrix in made if (layer, matrix) in store.own_sums]
     starts += [(SUM_Z, key) for key in store.straight_on]
     keys = [[key for own, key in starts if own == kind] for kind in range(4)]
-    keys_in = [key for matrix in weights for key in store.keys(layer, matrix)]
+    keys_in = [key for own in layers for matrix in weights for key in store.keys(own, matrix)]
     ins["src"] = {key: Far(store.source[key[:2]]) for key in keys[GET_Z]}
-    ins["full_in"] = {m: Far(store.full[layer, m]) for m in weights if not store.paired}
+    ins["full_in"] = {(own, m): Far(store.full[own, m]) for own in layers for m in weights if not store.paired}
     ins["z_in"], ins["x_in"] = {}, {}
     if store.paired:
         wanted = set(keys_in) | set(keys[GET_X])
@@ -933,9 +945,9 @@
             at += len(flat)
         place = k.place = Place()
         k.local = Local(k.lsem)
-        k.layer = layer
-        k.shared_last = store.paired and layer == 0
-        peers = place.greet_sequence() if tokens else []
+        k.layer, k.base, k.sharing = layer, 0, store.paired
+        k.stores = []
+        peers = place.greet_sequence()
         if around:
             peers += place.greet_all()
         elif store.paired:
@@ -975,7 +987,7 @@
 
         def at_point(point):
             for own, kind, key, *taken in plan:
-                if own != point:
+                if own != point + k.base:
                     continue
                 if kind == SUM_X and taken:
                     running[kind, key].take(*taken)
@@ -985,7 +997,7 @@
         loads, loaded = {}, set()
 
         def parts_of(matrix):
-            return [(key, *store.parts[matrix][key[2]]) for key in store.keys(layer, matrix)]
+            return [(key, *store.parts[matrix][key[2]]) for key in store.keys(k.layer, matrix)]
 
         def load_part(key, first, rows):
             w = k.w[key[1]]
@@ -1002,18 +1014,18 @@
         def early(*matrices):
             for matrix in matrices:
                 if not store.paired:
-                    loads[matrix] = [k.local.start(k.full_in[matrix], k.w[matrix])]
+                    loads[k.layer, matrix] = [k.local.start(k.full_in[k.layer, matrix], k.w[matrix])]
                     continue
                 for key, first, rows in parts_of(matrix):
                     if key in k.z_in and key in k.x_in:
                         load_part(key, first, rows)
 
         def weight(matrix):
-            if matrix in loaded:
+            if (k.layer, matrix) in loaded:
                 return
-            loaded.add(matrix)
+            loaded.add((k.layer, matrix))
             if not store.paired:
-                for copy in loads[matrix]:
+                for copy in loads[k.layer, matrix]:
                     copy.wait()
                 return
             for key, first, rows in parts_of(matrix):
@@ -1048,6 +1060,15 @@
 
         k.at, k.early, k.weight, k.matrix, k.made = at_point, early, weight, matrix_of, finished
         k.put_product = put_product
+
+        def keep(name):
+            k.stores.append(k.local.start(k.kept[name], k.kept_out[k.layer][name]))
+
+        def settle():
+            while k.stores:
+                k.stores.pop().wait()
+
+        k.keep, k.settle = keep, settle
         at_point(0)
         body(k)
         for kind, key in sorted(running):
@@ -1179,27 +1200,27 @@
     return now, up, gains, att, prj, jnp.swapaxes(router, 1, 2), wid, jnp.swapaxes(nar, 1, 2), exp, jnp.swapaxes(con, 2, 3)
 
 
-def forward_plan(store, layer, last):
-    qkv, (prj,), sh = (store.keys(layer, matrix) for matrix in (QKV, PRJ, SH))
-    low, high = store.keys(layer, EX), store.keys(layer, EX + 1)
-
+def forward_plan(store, layers):
     def pass_on(point, *keys):
         return [step for key in keys for step in ((point, GET_Z, key, True), (point, GET_X, key))]
 
-    if layer == 0:
-        plan = [(0, GET_Z, key) for key in (*qkv, prj, *low)]
-        plan += pass_on(1, *qkv) + pass_on(2, prj) + [(2, GET_Z, high[0])]
-        plan += pass_on(5, low[0]) + pass_on(7, low[1]) + pass_on(8, low[2])
-        plan += [(8, GET_Z, key) for key in (*high[1:], *sh)]
-        plan += pass_on(9, high[0]) + pass_on(11, high[1]) + pass_on(12, high[2]) + pass_on(13, sh[0]) + pass_on(14, sh[1])
-    else:
-        plan = [(0, GET_X, low[0])] + [(0, GET_Z, key) for key in (*low[1:], *high)]
-        plan += pass_on(2, low[1]) + pass_on(4, low[2]) + pass_on(7, high[0]) + pass_on(8, high[1]) + pass_on(9, high[2])
-    if layer < last:
-        qkv, (prj,), sh = (store.keys(layer + 1, matrix) for matrix in (QKV, PRJ, SH))
-        early = store.keys(layer + 1, EX)[0]
-        plan += [(8, GET_Z, key) for key in (*qkv, prj, *sh)] + [(12, GET_Z, early)]
-        plan += pass_on(15, *qkv, prj) + pass_on(16, *sh)
+    def go(point, *keys):
+        return [(point, GET_Z, key) for key in keys]
+
+    plan = []
+    for layer in range(layers):
+        qkv, (prj,), sh = (store.keys(layer, matrix) for matrix in (QKV, PRJ, SH))
+        low, high = store.keys(layer, EX), store.keys(layer, EX + 1)
+        at = 20 * layer
+        if layer == 0:
+            plan += go(0, *qkv, prj, *low) + pass_on(1, *qkv) + pass_on(2, prj) + go(2, high[0])
+            plan += pass_on(5, low[0]) + pass_on(7, low[1]) + pass_on(8, low[2]) + go(8, *high[1:], *sh)
+            plan += pass_on(9, high[0]) + pass_on(11, high[1]) + pass_on(12, high[2])
+            plan += pass_on(13, sh[0]) + pass_on(14, sh[1])
+        else:
+            plan += go(at - 12, *qkv, prj, *sh) + pass_on(at - 5, *qkv, prj) + pass_on(at - 4, *sh)
+            plan += go(at - 4, *low, *high[:2]) + pass_on(at + 2, *low[:2]) + pass_on(at + 5, low[2])
+            plan += go(at + 8, high[2]) + pass_on(at + 8, *high[:2]) + pass_on(at + 11, high[2])
     return plan
 
 
@@ -1313,49 +1334,42 @@
         news_send=pltpu.SemaphoreType.DMA((1,)),
         news_recv=pltpu.SemaphoreType.DMA((1,)),
     )
-    saved = []
-    current = stream
-    next_id = 0
-    for layer in range(layers):
-        result = call(
-            store,
-            layer_forward,
-            next_id,
-            dict(
-                x=current,
-                gains=norm_gains[layer],
-                router=router_rows[layer],
-                picks=picks,
-                **places,
-            ),
-            dict(
-                mid=rows_out,
-                following=rows_out,
-                gate_rows=Out((sequences, 8, length)),
-                kept_out=kept_outs(attention_shapes | ffn_shapes),
-                **(dict(picks_out=Out((4 * layers, length), jnp.int32)) if len(picks) < sequences else {}),
-            ),
-            dict(
-                chosen_cols=vmem((sequences, length, LANES), F32),
-                **tables,
-                **(news if len(picks) < sequences else {}),
-                kept=kept_scratch(attention_shapes | ffn_shapes),
-                branch=vmem((sequences, length, width), F32),
-                outs=vmem((CAP, width), BF16),
-                gates=vmem((sequences, length, LANES), F32),
-                gather=gather_scratch(),
-                scatter=token_scatter,
-                **pair_scratch,
-            ),
-            layer,
-            [QKV, PRJ, *ffn_matrices],
-            plan=forward_plan(store, layer, last) if paired else (),
-        )
-        if len(picks) < sequences:
-            picks = [*picks, result.picks_out]
-        saved.append((current, result.mid, result.kept_out, result.gate_rows))
-        current = result.following
-        next_id += 1
+    result = call(
+        store,
+        forward,
+        0,
+        dict(x=stream, gains=[*norm_gains], routers=[*router_rows], picks=picks, **places),
+        dict(
+            mid=[rows_out] * layers,
+            following=[rows_out] * layers,
+            gate_rows=[Out((sequences, 8, length))] * layers,
+            kept_out=[kept_outs(attention_shapes | ffn_shapes)] * layers,
+            **(dict(picks_out=Out((4 * layers, length), jnp.int32)) if paired else {}),
+        ),
+        dict(
+            chosen_cols=vmem((sequences, length, LANES), F32),
+            **tables,
+            **(news if paired else {}),
+            kept=kept_scratch(attention_shapes | ffn_shapes),
+            branch=vmem((sequences, length, width), F32),
+            outs=vmem((CAP, width), BF16),
+            gates=vmem((sequences, length, LANES), F32),
+            gather=gather_scratch(),
+            scatter=token_scatter,
+            **pair_scratch,
+        ),
+        range(layers),
+        [QKV, PRJ, *ffn_matrices],
+        plan=forward_plan(store, layers) if paired else (),
+    )
+    if paired:
+        picks = [*picks, result.picks_out]
+    current = result.following[last]
+    saved = [
+        ([stream, *result.following][layer], result.mid[layer], result.kept_out[layer], result.gate_rows[layer])
+        for layer in range(layers)
+    ]
+    next_id = 1
 
     upstream = cotangent
     parts_small = [None] * layers
@@ -1414,7 +1428,7 @@
             ins,
             outs,
             work,
-            layer,
+            [layer],
             [QKV, PRJ, *ffn_matrices],
             [QKV, PRJ, *ffn_matrices],
             plan=plan if paired else (),

time: 559 us -> 545 us (0.975)
  Pallas kernels: 545 us -> 530 us
    pallas_call x4 -> x3, Pallas kernels: 535 us -> 521 us  [call(): pl.pallas_call(kernel, out_shape=[jax.ShapeDtypeStruct(out.shape, out.kin...]
where the time goes in v5:
time: 545 us; the launch traced here: 536 us
  Pallas kernels  530 us (97%)
    pallas_call x3, Pallas kernels, call(): pl.pallas_call(kernel, out_shape=[jax.ShapeDtypeStruct(out.shape, out.kin...  521 us

profile of v5, /device:TPU:0, one launch (start us, length us, event | category | flops | bytes accessed | tf_op | source)
XLA Modules:
  0.0 535.6 jit_solution(5943576506485969672)
XLA Ops:
  0.6 1.3 slice_bitcast_fusion.2
  1.9 1.3 slice_bitcast_fusion
  3.3 0.8 add_bitcast_fusion
  4.0 0.6 reshape.23.refs_3_.refs_10_.refs_15_
  4.6 3.8 shard_map.222
  8.4 238.8 %shard_map.223 = (f32[256,768]{1,0:T(8,128)}, f32[256,768]{1,0:T(8,128)}, f32[2,8,1024]{2,1,0:T(8,128)}, f32[2,8,1024]{2,1,0:T(8,128)}, bf16[1024,768]{1,0:T(8,1...) custom-call(f32[1024,128]{1,0:T(8,128)} %constant.4.clone.refs_0_, ...), custom_call_target="tpu_custom_call" | custom-call | tf_op jit(solution)/shard_map/pallas_call | solution.py:1081
  247.2 128.7 %shard_map.224 = (f32[1,768]{1,0:T(1,128)}, f32[1,768]{1,0:T(1,128)}, f32[256,768]{1,0:T(8,128)}, bf16[4,2,96,576]{3,2,1,0:T(8,128)(2,1)}, bf16[4,2,96,192]{3,2,...) custom-call(f32[1024,128]{1,0:T(8,128)} %constant.4.clone.refs_0_, ...), custom_call_target="tpu_custom_call" | custom-call | tf_op jit(solution)/shard_map/pallas_call | solution.py:1081
  375.9 153.4 %shard_map.225 = (f32[1,768]{1,0:T(1,128)}, f32[1,768]{1,0:T(1,128)}, f32[256,768]{1,0:T(8,128)}, f32[8,768]{1,0:T(8,128)}, f32[24,768]{1,0:T(8,128)}, /*index=5...) custom-call(f32[1024,128]{1,0:T(8,128)} %constant.4.clone.refs_0_, ...), custom_call_target="tpu_custom_call" | custom-call | tf_op jit(solution)/shard_map/pallas_call | solution.py:1081
  529.3 5.9 %shard_map.226 = (f32[256,768]{1,0:T(8,128)}, f32[256,768]{1,0:T(8,128)}, f32[2,2,768]{2,1,0:T(2,128)}, f32[2,3,96,192]{3,2,1,0:T(8,128)}, f32[2,192,96]{2,1,0:T...) custom-call(f32[256,768]{1,0:T(8,128)} %get-tuple-element.132.refs_0, ...), custom_call_target="tpu_custom_call" | custom-call | tf_op jit(solution)/shard_map/pallas_call | solution.py:1102

commit v6 on v5

--- a/solution.py
+++ b/solution.py
@@ -756,8 +756,9 @@
                 moe_grad[s, rows, :] += nn(combine, k.outs[...])
         else:
             gates = k.gate_rows[s]
-            pair = jnp.sum(gates, axis=0, keepdims=True)
-            product = 0.5 * (pair * pair - jnp.sum(gates * gates, axis=0, keepdims=True))
+            product = jnp.where(k.chosen_rows[s] > 0, gates, 1.0)
+            for rows in (4, 2, 1):
+                product = product[:rows, :] * product[rows:, :]
             sums = k.slot_sums[s]
             logit_grad = k.chosen_rows[s] * product * (2.0 * sums - jnp.sum(sums, axis=0, keepdims=True))
             k.logit_grad[s] = logit_grad.astype(BF16)

time: 545 us -> 545 us (level)
  no operation moved by 1% of the time
where the time goes in v6:
time: 545 us; the launch traced here: 536 us
  Pallas kernels  530 us (97%)
    pallas_call x3, Pallas kernels, call(): pl.pallas_call(kernel, out_shape=[jax.ShapeDtypeStruct(out.shape, out.kin...  521 us

profile of v6, /device:TPU:0, one launch (start us, length us, event | category | flops | bytes accessed | tf_op | source)
XLA Modules:
  0.0 535.5 jit_solution(10530981330100719922)
XLA Ops:
  0.6 1.3 slice_bitcast_fusion.2
  1.9 1.3 slice_bitcast_fusion
  3.3 0.8 add_bitcast_fusion
  4.0 0.6 reshape.23.refs_3_.refs_10_.refs_15_
  4.6 3.8 shard_map.222
  8.4 238.8 %shard_map.223 = (f32[256,768]{1,0:T(8,128)}, f32[256,768]{1,0:T(8,128)}, f32[2,8,1024]{2,1,0:T(8,128)}, f32[2,8,1024]{2,1,0:T(8,128)}, bf16[1024,768]{1,0:T(8,1...) custom-call(f32[1024,128]{1,0:T(8,128)} %constant.4.clone.refs_0_, ...), custom_call_target="tpu_custom_call" | custom-call | tf_op jit(solution)/shard_map/pallas_call | solution.py:1082
  247.2 128.6 %shard_map.224 = (f32[1,768]{1,0:T(1,128)}, f32[1,768]{1,0:T(1,128)}, f32[256,768]{1,0:T(8,128)}, bf16[4,2,96,576]{3,2,1,0:T(8,128)(2,1)}, bf16[4,2,96,192]{3,2,...) custom-call(f32[1024,128]{1,0:T(8,128)} %constant.4.clone.refs_0_, ...), custom_call_target="tpu_custom_call" | custom-call | tf_op jit(solution)/shard_map/pallas_call | solution.py:1082
  375.8 153.4 %shard_map.225 = (f32[1,768]{1,0:T(1,128)}, f32[1,768]{1,0:T(1,128)}, f32[256,768]{1,0:T(8,128)}, f32[8,768]{1,0:T(8,128)}, f32[24,768]{1,0:T(8,128)}, /*index=5...) custom-call(f32[1024,128]{1,0:T(8,128)} %constant.4.clone.refs_0_, ...), custom_call_target="tpu_custom_call" | custom-call | tf_op jit(solution)/shard_map/pallas_call | solution.py:1082
  529.2 5.9 %shard_map.226 = (f32[256,768]{1,0:T(8,128)}, f32[256,768]{1,0:T(8,128)}, f32[2,2,768]{2,1,0:T(2,128)}, f32[2,3,96,192]{3,2,1,0:T(8,128)}, f32[2,192,96]{2,1,0:T...) custom-call(f32[256,768]{1,0:T(8,128)} %get-tuple-element.132.refs_0, ...), custom_call_target="tpu_custom_call" | custom-call | tf_op jit(solution)/shard_map/pallas_call | solution.py:1103
